TPU v7x, 512 devices: a whole 4x8x8 slice. The times are simulated.
512 devices in a mesh: ctx: 64 (over x, z, core), dp: 8 (over y).
Axes of the slice: x: 4, y: 8, z: 8, core: 2. Of those that a mesh axis runs over, the one named last changes fastest.
Arguments:
- hidden_in: bfloat16 [8192, 2048], P('ctx'), may hold values from -6 to 6
- query_vectors: bfloat16 [8192, 1024], P('ctx', 'dp'), may hold values from -6 to 6
- key_vectors: bfloat16 [8192, 1024], P('ctx', 'dp')
- value_vectors: bfloat16 [8192, 2048], P('ctx', 'dp'), may hold values from -6 to 6
- out_cotangent: bfloat16 [8192, 2048], P('ctx', 'dp'), may hold values from -6 to 6
- w_decay: bfloat16 [2048, 16], P(None, 'dp'), may hold values from -0.125 to 0.125
- w_beta: bfloat16 [2048, 16], P(None, 'dp'), may hold values from -0.125 to 0.125
- log_decay_rate: float32 [16], P('dp')
- step_bias: float32 [16], P('dp'), may hold values from -1 to 1
- doc_start: int32 [1], replicated, may hold values from 0 to 8191
Outputs:
- query_grad: bfloat16 [8192, 1024], P('ctx', 'dp')
- key_grad: bfloat16 [8192, 1024], P('ctx', 'dp')
- value_grad: bfloat16 [8192, 2048], P('ctx', 'dp')
- hidden_grad: bfloat16 [8192, 2048], P('ctx', 'dp')
- w_decay_grad: float32 [2048, 16], P(None, 'dp')
- w_beta_grad: float32 [2048, 16], P(None, 'dp')
- rate_grad: float32 [16], P('dp')
- bias_grad: float32 [16], P('dp')
Inputs may be any that keep to these rules, and one draw needn't show every extreme that they name: `doc_start`: the state is cleared at that position.
All inputs are finite; a program needn't handle non-finite values.
Results may differ from a plain program's by a relative error of at most 0.0024.
Values may be sent and summed in bfloat16 or wider, within the bound.
No kernel may reach another device: no remote copies, remote signals or barrier semaphores. Data moves between devices by JAX's collectives and lax.ppermute only.
A program may use at most 128 MiB of HBM per device.

v0:
```python
import jax
import jax.numpy as jnp
from jax import lax
from jax.sharding import PartitionSpec as P

DK = 128
DV = 128
BLOCK = 64


norm_epsilon = 1e-06


def entering(part, axis, combine, identity, reverse):
    count = lax.axis_size(axis)
    place = lax.axis_index(axis)
    ahead = count - 1 - place if reverse else place
    gathered = jax.tree.map(lambda a: lax.all_gather(a, axis), part)
    state = jax.tree.map(lambda a, e: jnp.zeros_like(a) + jnp.asarray(e, a.dtype), part, identity)

    def one(step, state):
        source = count - 1 - step if reverse else step
        return combine(
            state, jax.tree.map(lambda a: lax.dynamic_index_in_dim(a, source, 0, False), gathered)
        )

    return lax.fori_loop(0, ahead, one, state)


def unit_rows(source):
    return source * lax.rsqrt(jnp.sum(source * source, axis=-1, keepdims=True) + norm_epsilon)


def block_step(carried, pieces):
    query_block, key_block, value_block, decay_block, beta_block, reset_block = pieces
    length = query_block.shape[-2]
    highest = lax.Precision.HIGHEST
    cumulative = jnp.cumsum(decay_block, axis=-1)
    counted = jnp.cumsum(reset_block, axis=-1)
    places = jnp.arange(length, dtype=jnp.int32)
    lower_mask = places[:, None] >= places[None, :]
    strict_mask = places[:, None] > places[None, :]
    same_doc = (counted[:, :, None] == counted[:, None, :])[:, None]
    keep_mask = jnp.logical_and(lower_mask, same_doc)
    spread = cumulative[..., :, None] - cumulative[..., None, :]
    decay_matrix = jnp.where(keep_mask, jnp.exp(jnp.where(keep_mask, spread, 0.0)), 0.0)
    carry_in = jnp.where(counted[:, None, :] == 0, jnp.exp(cumulative), 0.0)
    key_gram = jnp.einsum("bhid,bhjd->bhij", key_block, key_block, precision=highest)
    coupling = jnp.where(strict_mask, beta_block[..., :, None] * decay_matrix * key_gram, 0.0)
    key_state = jnp.einsum("bhid,bhde->bhie", key_block, carried, precision=highest)
    target = beta_block[..., None] * (value_block - carry_in[..., None] * key_state)
    system = coupling + jnp.eye(length, dtype=jnp.float32)
    updates = lax.linalg.triangular_solve(
        system, target, left_side=True, lower=True, unit_diagonal=True
    )
    query_key = jnp.einsum("bhid,bhjd->bhij", query_block, key_block, precision=highest)
    from_state = jnp.einsum("bhid,bhde->bhie", query_block, carried, precision=highest)
    outputs = carry_in[..., None] * from_state + jnp.einsum(
        "bhij,bhje->bhie", query_key * decay_matrix, updates, precision=highest
    )
    weighted_keys = key_block * decay_matrix[..., -1, :, None]
    new_state = carry_in[..., -1, None, None] * carried + jnp.einsum(
        "bhjd,bhje->bhde", weighted_keys, updates, precision=highest
    )
    return (new_state, outputs)


def blocked(source, blocks):
    seq_count, tokens = (source.shape[0], source.shape[1])
    shaped = source.reshape((seq_count, blocks, tokens // blocks) + source.shape[2:])
    if source.ndim == 4:
        return shaped.transpose(1, 0, 3, 2, 4)
    if source.ndim == 3:
        return shaped.transpose(1, 0, 3, 2)
    return shaped.transpose(1, 0, 2)


def run_block(carried, queries_f, keys_f, values_f, logit_rows, rate_logs, biases, resets):
    seq_count, tokens = (logit_rows.shape[0], logit_rows.shape[1])
    head_count = rate_logs.shape[0]
    size_key = carried.shape[2]
    size_value = carried.shape[3]
    group_size = head_count // (queries_f.shape[2] // size_key)
    log_decay = -jnp.exp(rate_logs) * jax.nn.softplus(logit_rows[..., :head_count] + biases)
    beta_all = jax.nn.sigmoid(logit_rows[..., head_count:])
    query_heads = unit_rows(queries_f.reshape(seq_count, tokens, -1, size_key)) * size_key ** (-0.5)
    key_heads = unit_rows(keys_f.reshape(seq_count, tokens, -1, size_key))
    query_heads = jnp.repeat(query_heads, group_size, axis=2)
    key_heads = jnp.repeat(key_heads, group_size, axis=2)
    value_heads = values_f.reshape(seq_count, tokens, head_count, size_value)
    blocks = tokens // BLOCK
    pieces = (
        blocked(query_heads, blocks),
        blocked(key_heads, blocks),
        blocked(value_heads, blocks),
        blocked(log_decay, blocks),
        blocked(beta_all, blocks),
        blocked(resets, blocks),
    )
    final_state, outputs = lax.scan(jax.checkpoint(block_step), carried, pieces)
    outputs = outputs.transpose(1, 0, 3, 2, 4).reshape(seq_count, tokens, head_count * size_value)
    return (outputs, final_state)


def apply_map(matrices, incoming):
    return jnp.einsum("bhij,bhjk->bhik", matrices, incoming, precision=lax.Precision.HIGHEST)


def compose(earlier, following):
    return (apply_map(following[0], earlier[0]), apply_map(following[0], earlier[1]) + following[1])


def on_device(
    hidden_in,
    query_vectors,
    key_vectors,
    value_vectors,
    out_cotangent,
    w_decay,
    w_beta,
    log_decay_rate,
    step_bias,
    doc_start,
):
    tokens = hidden_in.shape[0]
    head_count = log_decay_rate.shape[0]
    highest = lax.Precision.HIGHEST
    both_weights = jnp.concatenate([w_decay, w_beta], axis=1)
    logits = jnp.dot(hidden_in, both_weights, preferred_element_type=jnp.float32)[None]
    offset = lax.axis_index("ctx") * tokens
    positions = offset + jnp.arange(tokens, dtype=jnp.int32)
    resets = (positions == doc_start[0]).astype(jnp.float32)[None]
    query_f = query_vectors.astype(jnp.float32)[None]
    key_f = key_vectors.astype(jnp.float32)[None]
    value_f = value_vectors.astype(jnp.float32)[None]
    cotangent = out_cotangent.astype(jnp.float32)[None]
    zero_state = jnp.zeros((1, head_count, DK, DV), jnp.float32)
    identity = jnp.broadcast_to(jnp.eye(DK, dtype=jnp.float32), zero_state.shape)

    def from_state(carried):
        return run_block(
            carried, query_f, key_f, value_f, logits, log_decay_rate, step_bias, resets
        )

    (local_out, local_end), pull_zero = jax.vjp(from_state, zero_state)
    own_adjoint = pull_zero((cotangent, jnp.zeros_like(local_end)))[0]
    transition = run_block(
        identity, query_f, key_f, jnp.zeros_like(value_f), logits, log_decay_rate, step_bias, resets
    )[1]
    flipped = jnp.swapaxes(transition, 2, 3)
    state_in = entering((transition, local_end), "ctx", compose, (identity, zero_state), False)[1]
    adjoint_out = entering((flipped, own_adjoint), "ctx", compose, (identity, zero_state), True)[1]

    def whole_block(carried, queries_in, keys_in, values_in, logit_rows, rate_logs, biases):
        return run_block(
            carried, queries_in, keys_in, values_in, logit_rows, rate_logs, biases, resets
        )

    primal, pull_all = jax.vjp(
        whole_block, state_in, query_f, key_f, value_f, logits, log_decay_rate, step_bias
    )
    gradients = pull_all((cotangent, adjoint_out))
    logit_grad = gradients[4][0]
    hidden_part = jnp.dot(logit_grad, both_weights.astype(jnp.float32).T, precision=highest)
    hidden_grad = lax.psum_scatter(hidden_part, "dp", scatter_dimension=1, tiled=True).astype(
        jnp.bfloat16
    )
    weight_grad = jnp.dot(hidden_in.astype(jnp.float32).T, logit_grad, precision=highest)
    totals = lax.psum((weight_grad, gradients[5], gradients[6]), "ctx")
    return (
        gradients[1][0].astype(jnp.bfloat16),
        gradients[2][0].astype(jnp.bfloat16),
        gradients[3][0].astype(jnp.bfloat16),
        hidden_grad,
        totals[0][:, :head_count],
        totals[0][:, head_count:],
        totals[1],
        totals[2],
    )


def solution(mesh):
    in_specs = (
        P("ctx", None),
        P("ctx", "dp"),
        P("ctx", "dp"),
        P("ctx", "dp"),
        P("ctx", "dp"),
        P(None, "dp"),
        P(None, "dp"),
        P("dp"),
        P("dp"),
        P(),
    )
    out_specs = (
        P("ctx", "dp"),
        P("ctx", "dp"),
        P("ctx", "dp"),
        P("ctx", "dp"),
        P(None, "dp"),
        P(None, "dp"),
        P("dp"),
        P("dp"),
    )
    return jax.shard_map(
        on_device, mesh=mesh, in_specs=in_specs, out_specs=out_specs, check_vma=False
    )
```

profile of v0, /device:TPU:1, one launch (start us, length us, event | category | flops | bytes accessed | tf_op | source)
XLA Modules:
  0.0 796.5 jit_solution(10013993354215391559)
XLA Ops:
  13.5 24.8 %while.109 = (s32[]{:T(128)}, f32[1,2,128,128]{3,2,1,0:T(8,128)S(1)}, f32[2,1,64]{2,1,0:T(1,128)S(1)}, f32[2,1,2,64]{3,2,1,0:T(2,128)S(1)}, f32[2,1,2,64,128]{4,...) while((s32[]{:T(128)}, ...), condition=%wide.region_15.18_spmd.clone, body=%wide.region_12.17_spmd.clone.sunk | while | flops 75813440 | bytes 1131608 | solution.py:100
  14.5 9.8 %custom-call.39 = f32[1,2,1,64,64]{3,4,2,1,0:T(8,128)S(1)} custom-call(f32[1,2,1,64,64]{4,3,2,1,0:T(8,128)S(1)} %fusion.545), custom_call_target="InvertDiagBlocksLowerTriangular" | custom-call | tf_op jit(solution)/shard_map/jvp()/while/body/eval_jaxpr/triangular_solve/custom-call.1 | solution.py:53
  26.9 9.8 %custom-call.39 = f32[1,2,1,64,64]{3,4,2,1,0:T(8,128)S(1)} custom-call(f32[1,2,1,64,64]{4,3,2,1,0:T(8,128)S(1)} %fusion.545), custom_call_target="InvertDiagBlocksLowerTriangular" | custom-call | tf_op jit(solution)/shard_map/jvp()/while/body/eval_jaxpr/triangular_solve/custom-call.1 | solution.py:53
  39.0 24.8 %while.103 = (s32[]{:T(128)}, f32[1,2,128,128]{3,2,1,0:T(8,128)S(1)}, f32[2,1,64]{2,1,0:T(1,128)S(1)}, f32[2,1,2,64]{3,2,1,0:T(2,128)S(1)}, f32[2,1,2,64,128]{4,...) while((s32[]{:T(128)}, f32[1,2,128,128]{3,2,1,0:T(8,128)S(1)}, ...), condition=%wide.region_4.6_spmd, body=%wide.region_1.5_spmd.sunk | while | flops 75752000 | bytes 1069113 | solution.py:100
  40.1 9.8 %custom-call.34 = f32[1,2,1,64,64]{3,4,2,1,0:T(8,128)S(1)} custom-call(f32[1,2,1,64,64]{4,3,2,1,0:T(8,128)S(1)} %fusion.434), custom_call_target="InvertDiagBlocksLowerTriangular" | custom-call | tf_op jit(solution)/shard_map/while/body/eval_jaxpr/checkpoint/triangular_solve/custom-call.1 | solution.py:53
  52.5 9.8 %custom-call.34 = f32[1,2,1,64,64]{3,4,2,1,0:T(8,128)S(1)} custom-call(f32[1,2,1,64,64]{4,3,2,1,0:T(8,128)S(1)} %fusion.434), custom_call_target="InvertDiagBlocksLowerTriangular" | custom-call | tf_op jit(solution)/shard_map/while/body/eval_jaxpr/checkpoint/triangular_solve/custom-call.1 | solution.py:53
  65.0 26.9 %while.108 = (s32[]{:T(128)}, f32[1,2,128,128]{2,3,1,0:T(8,128)S(1)}, f32[2,1,2,64,128]{4,3,2,1,0:T(8,128)S(1)}, f32[2,1,2,64,128]{4,3,2,1,0:T(8,128)S(1)}, f32[...) while((s32[]{:T(128)}, ...), condition=%wide.region_9.12_spmd.clone, body=%wide.region_6.11_spmd.clone.sunk | while | flops 126214720 | bytes 2466919 | solution.py:100
  66.1 9.8 %custom-call.38 = f32[1,2,1,64,64]{3,4,2,1,0:T(8,128)S(1)} custom-call(f32[1,2,1,64,64]{4,3,2,1,0:T(8,128)S(1)} %fusion.531), custom_call_target="InvertDiagBlocksLowerTriangular" | custom-call | tf_op jit(solution)/shard_map/transpose(jvp())/while/body/eval_jaxpr/checkpoint/triangular_solve/custom-call.0 | solution.py:53
  79.5 9.8 %custom-call.38 = f32[1,2,1,64,64]{3,4,2,1,0:T(8,128)S(1)} custom-call(f32[1,2,1,64,64]{4,3,2,1,0:T(8,128)S(1)} %fusion.531), custom_call_target="InvertDiagBlocksLowerTriangular" | custom-call | tf_op jit(solution)/shard_map/transpose(jvp())/while/body/eval_jaxpr/checkpoint/triangular_solve/custom-call.0 | solution.py:53
  93.5 41.8 %all-gather.15.cloned.1.call-done = f32[64,2,128,128]{3,2,1,0:T(8,128)} async-done(((f32[1,2,128,128]{3,2,1,0:T(8,128)}), f32[64,2,128,128]{3,2,1,0:T(8,128)}) %all-gather.15.cloned.1.call-update) | async-done | bytes 8388624 | tf_op jit(solution)/shard_map/all_gather | solution.py:18
  135.3 89.3 %all-gather.13.cloned.1.call-done = f32[64,2,128,128]{3,2,1,0:T(8,128)} async-done(((f32[1,2,128,128]{3,2,1,0:T(8,128)}), f32[64,2,128,128]{3,2,1,0:T(8,128)}) %all-gather.13.cloned.1.call-update) | async-done | bytes 8388624 | tf_op jit(solution)/shard_map/all_gather | solution.py:18
  224.7 1.3 while.105
  226.0 24.8 %while.107 = (s32[]{:T(128)}, f32[1,2,128,128]{3,2,1,0:T(8,128)S(1)}, f32[2,1,2,128,128]{4,3,2,1,0:T(8,128)S(1)}, f32[2,1,64]{2,1,0:T(1,128)S(1)}, f32[2,1,2,64]...) while((s32[]{:T(128)}, ...), condition=%wide.region_21.24_spmd.clone, body=%wide.region_18.23_spmd.clone.sunk | while | flops 75747904 | bytes 1393745 | solution.py:100
  227.0 9.8 %custom-call.37 = f32[1,2,1,64,64]{3,4,2,1,0:T(8,128)S(1)} custom-call(f32[1,2,1,64,64]{4,3,2,1,0:T(8,128)S(1)} %fusion.509), custom_call_target="InvertDiagBlocksLowerTriangular" | custom-call | tf_op jit(solution)/shard_map/jvp()/while/body/eval_jaxpr/triangular_solve/custom-call.1 | solution.py:53
  239.3 9.8 %custom-call.37 = f32[1,2,1,64,64]{3,4,2,1,0:T(8,128)S(1)} custom-call(f32[1,2,1,64,64]{4,3,2,1,0:T(8,128)S(1)} %fusion.509), custom_call_target="InvertDiagBlocksLowerTriangular" | custom-call | tf_op jit(solution)/shard_map/jvp()/while/body/eval_jaxpr/triangular_solve/custom-call.1 | solution.py:53
  250.7 63.4 %all-gather.11.cloned.1.call-done = f32[64,2,128,128]{3,2,1,0:T(8,128)} async-done(((f32[1,2,128,128]{3,2,1,0:T(8,128)}), f32[64,2,128,128]{3,2,1,0:T(8,128)}) %all-gather.11.cloned.1.call-update) | async-done | bytes 8388624 | tf_op jit(solution)/shard_map/all_gather | solution.py:18
  314.1 89.2 %all-gather.9.cloned.1.call-done = f32[64,2,128,128]{3,2,1,0:T(8,128)} async-done(((f32[1,2,128,128]{3,2,1,0:T(8,128)}), f32[64,2,128,128]{3,2,1,0:T(8,128)}) %all-gather.9.cloned.1.call-update) | async-done | bytes 8388624 | tf_op jit(solution)/shard_map/all_gather | solution.py:18
  403.3 80.2 %while.104 = (s32[]{:T(128)}, f32[1,2,128,128]{3,2,1,0:T(8,128)S(1)}, s32[]{:T(128)}, f32[64,1,2,128,128]{4,3,2,1,0:T(8,128)}, f32[64,1,2,128,128]{4,3,2,1,0:T(8...) while((s32[]{:T(128)}, f32[1,2,128,128]{3,2,1,0:T(8,128)S(1)}, s32[]{:T(128)}, ...), condition=%wide.region_11.14_spmd, body=%wide.region_10.13_spmd.sunk | while | flops 50364420 | bytes 787595 | solution.py:27
  417.5 1.2 fusion.439
  421.4 1.2 fusion.439
  436.9 1.2 fusion.439
  456.3 1.2 fusion.439
  471.8 1.2 fusion.439
  475.6 1.2 fusion.439
  483.8 57.8 %while.106 = (s32[]{:T(128)}, f32[1,2,128,128]{2,3,1,0:T(8,128)S(1)}, f32[2,1,2,64,128]{4,3,2,1,0:T(8,128)S(1)}, f32[2,1,2,64,128]{4,3,2,1,0:T(8,128)S(1)}, bf16...) while((s32[]{:T(128)}, ...), condition=%wide.region_34.37_spmd, body=%wide.region_22.36_spmd.sunk | while | flops 347291968 | bytes 6834849 | solution.py:100
  485.1 9.8 %custom-call.36 = f32[1,2,1,64,64]{3,4,2,1,0:T(8,128)S(1)} custom-call(f32[1,2,1,64,64]{4,3,2,1,0:T(8,128)S(1)} %add_bitcast_fusion.2), custom_call_target="InvertDiagBlocksLowerTriangular" | custom-call | tf_op jit(solution)/shard_map/transpose(jvp())/while/body/eval_jaxpr/checkpoint/triangular_solve | solution.py:53
  495.1 9.8 %custom-call.35 = f32[1,2,1,64,64]{3,4,2,1,0:T(8,128)S(1)} custom-call(f32[1,2,1,64,64]{4,3,2,1,0:T(8,128)S(1)} %get-tuple-element.1698), custom_call_target="InvertDiagBlocksLowerTriangular" | custom-call | tf_op jit(solution)/shard_map/transpose(jvp())/while/body/eval_jaxpr/checkpoint/triangular_solve/custom-call.0 | solution.py:53
  514.0 9.8 %custom-call.36 = f32[1,2,1,64,64]{3,4,2,1,0:T(8,128)S(1)} custom-call(f32[1,2,1,64,64]{4,3,2,1,0:T(8,128)S(1)} %add_bitcast_fusion.2), custom_call_target="InvertDiagBlocksLowerTriangular" | custom-call | tf_op jit(solution)/shard_map/transpose(jvp())/while/body/eval_jaxpr/checkpoint/triangular_solve | solution.py:53
  523.9 9.8 %custom-call.35 = f32[1,2,1,64,64]{3,4,2,1,0:T(8,128)S(1)} custom-call(f32[1,2,1,64,64]{4,3,2,1,0:T(8,128)S(1)} %get-tuple-element.1698), custom_call_target="InvertDiagBlocksLowerTriangular" | custom-call | tf_op jit(solution)/shard_map/transpose(jvp())/while/body/eval_jaxpr/checkpoint/triangular_solve/custom-call.0 | solution.py:53
  541.9 1.6 fusion.263
  544.7 242.0 %all-reduce.4 = (f32[2048,4]{0,1:T(4,128)S(1)}, f32[2]{0:T(128)}, f32[2]{0:T(128)}) all-reduce(f32[2048,4]{0,1:T(4,128)S(1)} %convolution_bitcast_fusion.15, f32[2]{0:T(128)S(1)} %negate_multiply_fusion, f32[2]{0:T(128)S(1)} %get-tuple-element.1247), channel_id=1, replica_groups=mesh['ctx'=64,'dp'=8] {'ctx'}, use_global_device_ids=true, to_apply=%region_40.43 | all-reduce | flops 8196 | bytes 65568 | tf_op jit(solution)/shard_map/psum | solution.py:169
  788.4 1.5 convert_element_type.97
  (498 shorter events, 123.0 us)
Async XLA Ops:
  7.2 1.1 copy-start
  7.2 128.1 %all-gather.15.cloned.1.call-start = ((), (), s32[]{:S(2)}) async-start(), calls=%async_computation.5 | async-start | bytes 8519680 | tf_op jit(solution)/shard_map/all_gather | solution.py:18
  8.2 56.4 %copy-start.6 = (bf16[128,256]{1,0:T(8,128)(2,1)S(1)}, bf16[128,256]{1,0:T(8,128)(2,1)}, u32[]{:S(2)}) copy-start(bf16[128,256]{1,0:T(8,128)(2,1)} %param.32) | copy-start | bytes 196612
  11.9 52.8 %copy-start.4 = (bf16[128,128]{1,0:T(8,128)(2,1)S(1)}, bf16[128,128]{1,0:T(8,128)(2,1)}, u32[]{:S(2)}) copy-start(bf16[128,128]{1,0:T(8,128)(2,1)} %param.29) | copy-start | bytes 98308
  38.3 0.6 copy-start.3
  39.0 185.7 %all-gather.13.cloned.1.call-start = ((), (), s32[]{:S(2)}) async-start(), calls=%async_computation.4 | async-start | bytes 8519680 | tf_op jit(solution)/shard_map/all_gather | solution.py:18
  63.9 0.6 copy-start.1
  64.5 28.1 %copy-start.2 = (f32[1,2,128,128]{3,2,1,0:T(8,128)S(1)}, f32[1,2,128,128]{3,2,1,0:T(8,128)}, u32[]{:S(2)}) copy-start(f32[1,2,128,128]{3,2,1,0:T(8,128)} %copy-done.1) | copy-start | bytes 393220
  64.5 249.5 %all-gather.11.cloned.1.call-start = ((), (), s32[]{:S(2)}) async-start(), calls=%async_computation.3 | async-start | bytes 8519680 | tf_op jit(solution)/shard_map/all_gather | solution.py:18
  92.6 310.6 %all-gather.9.cloned.1.call-start = ((), (), s32[]{:S(2)}) async-start(), calls=%async_computation.2 | async-start | bytes 8519680 | tf_op jit(solution)/shard_map/all_gather | solution.py:18
  93.5 694.9 %reduce-scatter.2.cloned.1.call-start = ((), (), s32[]{:S(2)}) async-start(), calls=%async_computation.1 | async-start | bytes 1179648 | tf_op jit(solution)/shard_map/reduce_scatter | solution.py:165
  483.7 58.0 %copy-start.9 = (f32[2]{0:T(128)S(1)}, f32[2]{0:T(128)}, u32[]{:S(2)}) copy-start(f32[2]{0:T(128)} %param.36) | copy-start | bytes 28
  483.7 58.2 %copy-start.7 = (bf16[2048,2]{0,1:T(2,128)(2,1)S(1)}, bf16[2048,2]{0,1:T(2,128)(2,1)}, u32[]{:S(2)}) copy-start(bf16[2048,2]{0,1:T(2,128)(2,1)} %param.34) | copy-start | bytes 24580
  483.7 58.2 %copy-start.8 = (bf16[2048,2]{0,1:T(2,128)(2,1)S(1)}, bf16[2048,2]{0,1:T(2,128)(2,1)}, u32[]{:S(2)}) copy-start(bf16[2048,2]{0,1:T(2,128)(2,1)} %param.33) | copy-start | bytes 24580
  483.7 60.6 %copy-start.10 = (f32[2]{0:T(128)S(1)}, f32[2]{0:T(128)}, u32[]{:S(2)}) copy-start(f32[2]{0:T(128)} %param.35) | copy-start | bytes 28
  483.8 303.1 %copy-start.5 = (bf16[128,128]{1,0:T(8,128)(2,1)S(1)}, bf16[128,128]{1,0:T(8,128)(2,1)}, u32[]{:S(2)}) copy-start(bf16[128,128]{1,0:T(8,128)(2,1)} %param.30) | copy-start | bytes 98308
Sparse Core Ops, SparseCore 0:
  39.1 96.1 all-gather.14
  138.7 85.9 all-gather.12
  228.0 86.0 all-gather.10
  317.3 85.9 all-gather.8
  543.7 31.0 reduce-scatter.1
where the time goes:
time: 802 us; the launch traced here: 796 us
  waiting for transfers between devices  284 us (35%)
  blocking collectives  242 us (30%)
  other arithmetic  133 us (17%)
  matrix products  107 us (13%)
  between operations  14.9 us (2%)
  local copies, waits for them, and re-layouts  11.6 us (1%)
    all_gather x4, waiting for transfers between devices, entering(): gathered = jax.tree.map(lambda a: lax.all_gather(a, axis), part)  284 us
    psum x1, blocking collectives, on_device(): totals = lax.psum((weight_grad, gradients[5], gradients[6]), 'ctx')  242 us
    another operation x42, other arithmetic, block_step(): lax.linalg.triangular_solve(system, target, left_side=True, lower=True, u...  119 us
    dot_general x63, matrix products, apply_map(): jnp.einsum('bhij,bhjk->bhik', matrices, incoming, precision=lax.Precision...  78.1 us
  transfers between devices with their start and end apart: 5, of which 4 were waited for; matrix products, arithmetic and copies ran while one was open for 10% of the time, Pallas kernels for 0%

commit v1 on v0

v1 whole, which is shorter than its diff:
```python
import functools

import jax
import jax.numpy as jnp
from jax import lax
from jax.experimental import pallas as pl
from jax.experimental.pallas import tpu as pltpu
from jax.sharding import Mesh
from jax.sharding import PartitionSpec as P

F32 = jnp.float32
BF16 = jnp.bfloat16
F16 = jnp.float16
C = 128
HEADS = 2
D = 2048
NX, NZ, NC, NY = 4, 8, 2, 8
CTX = ("x", "z", "core")
norm_epsilon = 1e-06
SCALE = C**-0.5
LOG_FLOOR = -200.0
MAP_ROWS = 3 * C + 8
PACKED_ROWS = 3 * C + 16


def split(a):
    high = a.astype(BF16)
    return (high, (a - high.astype(F32)).astype(BF16))


def split3(a):
    high = a.astype(BF16)
    rest = a - high.astype(F32)
    middle = rest.astype(BF16)
    return (high, middle, (rest - middle.astype(F32)).astype(BF16))


def dot(a, b, ca, cb):
    return lax.dot_general(a, b, (((ca,), (cb,)), ((), ())), preferred_element_type=F32)


def mm(a, b, ca=1, cb=0):
    total = dot(a[0], b[0], ca, cb)
    for i in range(len(a)):
        for j in range(len(b)):
            if 0 < i + j < max(len(a), len(b)):
                total = total + dot(a[i], b[j], ca, cb)
    return total


def iotas():
    return (
        lax.broadcasted_iota(jnp.int32, (C, C), 0),
        lax.broadcasted_iota(jnp.int32, (C, C), 1),
    )


def pair_column(first, second):
    row = lax.broadcasted_iota(jnp.int32, (HEADS, C), 0)
    return jnp.where(row == 0, first, second)


def unit_rows(source):
    root = lax.rsqrt(jnp.sum(source * source, axis=-1, keepdims=True) + norm_epsilon)
    return source * root, root


def local_kernel(
    place_ref, rate_ref, bias_ref, hid_ref, q_ref, k_ref, v_ref, do_ref, wd_ref, wb_ref,
    map_ref, uhat_ref, what_ref, z0_ref, y_ref, gram_ref, qk_ref, rows_ref,
):
    reset = place_ref[0]
    ii, jj = iotas()
    keep = jnp.logical_and(ii >= jj, jnp.logical_or(jj >= reset, ii < reset))
    zd = dot(wd_ref[...], hid_ref[...], 1, 1)
    zb = dot(wb_ref[...], hid_ref[...], 1, 1)
    x = zd + pair_column(bias_ref[0], bias_ref[1])
    soft = jnp.maximum(x, 0.0) + jnp.log1p(jnp.exp(-jnp.abs(x)))
    log_decay = -jnp.exp(pair_column(rate_ref[0], rate_ref[1])) * soft
    beta = jax.nn.sigmoid(zb)
    upper = (ii <= jj).astype(BF16)
    cumulative = sum(dot(t, upper, 1, 0) for t in split3(log_decay))
    rows_ref[0:2, :] = cumulative
    rows_ref[2:4, :] = beta
    rows_ref[4:6, :] = log_decay
    rows_ref[6:8, :] = x
    cols = rows_ref[...].T
    keys, _ = unit_rows(k_ref[...].astype(F32))
    queries, _ = unit_rows(q_ref[...].astype(F32))
    queries = queries * SCALE
    ks, qs = split(keys), split(queries)
    gram = mm(ks, ks, 1, 1)
    qk = mm(qs, ks, 1, 1)
    gram_ref[...] = gram
    qk_ref[...] = qk
    ii_col = ii[:, 0:1]
    eye = jnp.where(ii == jj, 1.0, 0.0).astype(F32)
    for h in range(HEADS):
        c_col, c_row = cols[:, h : h + 1], rows_ref[h : h + 1, :]
        b_col = cols[:, 2 + h : 3 + h]
        lanes = slice(h * C, (h + 1) * C)
        decay = jnp.where(keep, jnp.exp(jnp.where(keep, c_col - c_row, 0.0)), 0.0)
        carry = jnp.where(ii_col < reset, jnp.exp(c_col), 0.0)
        c_last = c_col[C - 1 : C, :]
        late = jnp.logical_or(ii_col >= reset, reset > C - 1)
        weight = jnp.where(late, jnp.exp(jnp.where(late, c_last - c_col, 0.0)), 0.0)
        inner = jnp.where(ii > jj, decay * gram, 0.0)
        coupling = b_col * inner
        inverse = eye - jnp.where((ii & 1) * (ii - jj) == 1, coupling, 0.0)
        for level in range(1, 7):
            bi, bj = ii >> level, jj >> level
            part = jnp.where((bi & 1) * (bi - bj) == 1, coupling, 0.0)
            xs = split(inverse)
            inverse = inverse - mm(xs, split(mm(split(part), xs)))
        xs = split(inverse)
        keys_in = carry * keys
        values = v_ref[:, lanes].astype(F32)
        cotangent = (do_ref[:, lanes],)
        both = jnp.concatenate([keys_in, values], axis=1)
        wu = mm(xs, split(b_col * both))
        wus = split(wu)
        hats = both - mm(split(inner), wus)
        what_ref[h] = hats[:, :C]
        uhat_ref[h] = hats[:, C:]
        ps = split(qk * decay)
        keys_out = weight * keys
        zy = mm(xs, split(jnp.concatenate([mm(ps, cotangent, 0, 0), keys_out], axis=1)), 0, 0)
        z0_ref[h] = zy[:, :C]
        y_ref[h] = zy[:, C:]
        ml = mm(split(keys_out), wus, 0, 0)
        map_ref[h, 0:C, :] = ml[:, :C]
        map_ref[h, C : 2 * C, :] = ml[:, C:]
        effective = carry * queries - mm(ps, tuple(t[:, :C] for t in wus))
        map_ref[h, 2 * C : 3 * C, :] = mm(split(effective), cotangent, 0, 0)
        total = jnp.where(reset > C - 1, jnp.maximum(c_last, LOG_FLOOR), LOG_FLOOR)
        map_ref[h, 3 * C :, :] = jnp.broadcast_to(total, (8, C))


def read_map(ref, *at):
    m = ref[(*at, slice(0, C), slice(None))]
    state = ref[(*at, slice(C, 2 * C), slice(None))]
    adjoint = ref[(*at, slice(2 * C, 3 * C), slice(None))]
    log = ref[(*at, slice(3 * C, 3 * C + 1), slice(0, 1))]
    return m, state, adjoint, log


def pair_kernel(maps_ref, out_ref):
    m0, l0, a0, c0 = read_map(maps_ref, 0)
    m1, l1, a1, c1 = read_map(maps_ref, 1)
    g0, g1 = jnp.exp(c0), jnp.exp(c1)
    m0s, m1s = split(m0), split(m1)
    forward = mm(m1s, tuple(jnp.concatenate([a, b], axis=1) for a, b in zip(m0s, split(l0))))
    m = g1 * m0 + g0 * m1 - forward[:, :C]
    state = g1 * l0 - forward[:, C:] + l1
    adjoint = g0 * a1 - mm(m0s, split(a1), 0, 0) + a0
    log = jnp.maximum(c0 + c1, LOG_FLOOR)
    row = lax.broadcasted_iota(jnp.int32, (16, C), 0)
    meta = jnp.zeros((16, C), F32)
    for at, part in enumerate((m, state, adjoint)):
        largest = jnp.max(jnp.max(jnp.abs(part), axis=0, keepdims=True), axis=1, keepdims=True)
        power = jnp.floor(jnp.log2(jnp.maximum(largest, 1e-30)))
        out_ref[at * C : (at + 1) * C, :] = part * jnp.exp2(13.0 - power)
        meta = jnp.where(row == at, power, meta)
    quarters = jnp.floor(log * 4.0)
    fine = log * 4.0 - quarters
    coarse = jnp.floor(fine * 1024.0) * (1.0 / 1024.0)
    meta = jnp.where(row == 3, quarters * 0.25, meta)
    meta = jnp.where(row == 4, coarse, meta)
    meta = jnp.where(row == 5, (fine - coarse) * 1024.0, meta)
    out_ref[3 * C :, :] = meta


def ring_kernel(at_ref, maps_ref, out_ref, near_ref):
    here = at_ref[0]

    def fetch(z):
        meta = maps_ref[z, 3 * C :, :]
        scales = [jnp.exp2(meta[i : i + 1, 0:1] - 13.0) for i in range(3)]
        parts = [maps_ref[z, i * C : (i + 1) * C, :] * scales[i] for i in range(3)]
        log = meta[3:4, 0:1] + 0.25 * (meta[4:5, 0:1] + meta[5:6, 0:1] * (1.0 / 1024.0))
        return parts[0], parts[1], parts[2], log

    zero = jnp.zeros((C, C), F32)

    @pl.when(here == 0)
    def _():
        near_ref[0:C, :] = zero
        near_ref[C : 2 * C, :] = zero
        near_ref[4 * C : 4 * C + 8, :] = jnp.zeros((8, C), F32)

    @pl.when(here == NZ - 1)
    def _():
        near_ref[2 * C : 3 * C, :] = zero
        near_ref[3 * C : 4 * C, :] = zero
        near_ref[4 * C + 8 :, :] = jnp.zeros((8, C), F32)

    m, state, _, log = fetch(0)
    m_back, _, adjoint, log_back = fetch(NZ - 1)
    m_back = m_back.T
    for step in range(1, NZ):
        back = NZ - 1 - step

        @pl.when(here == step)
        def _():
            near_ref[0:C, :] = m
            near_ref[C : 2 * C, :] = state
            near_ref[4 * C : 4 * C + 8, :] = jnp.broadcast_to(log, (8, C))

        @pl.when(here == back)
        def _():
            near_ref[2 * C : 3 * C, :] = m_back
            near_ref[3 * C : 4 * C, :] = adjoint
            near_ref[4 * C + 8 :, :] = jnp.broadcast_to(log_back, (8, C))

        mz, lz, _, cz = fetch(step)
        moved = mm(split(mz), split(jnp.concatenate([m, state], axis=1)))
        gz, g = jnp.exp(cz), jnp.exp(log)
        m, state = gz * m + g * mz - moved[:, :C], gz * state + lz - moved[:, C:]
        log = log + cz
        mz, _, az, cz = fetch(back)
        mz = mz.T
        moved = mm(split(mz), split(jnp.concatenate([m_back, adjoint], axis=1)))
        gz, g = jnp.exp(cz), jnp.exp(log_back)
        m_back, adjoint = gz * m_back + g * mz - moved[:, :C], gz * adjoint + az - moved[:, C:]
        log_back = log_back + cz
    total = jnp.broadcast_to(jnp.maximum(log, LOG_FLOOR), (8, C))
    for slot in range(NX):
        out_ref[slot, 0:C, :] = m
        out_ref[slot, C : 2 * C, :] = state
        out_ref[slot, 2 * C : 3 * C, :] = adjoint
        out_ref[slot, 3 * C :, :] = total


def entry_kernel(at_ref, groups_ref, near_ref, maps_ref, out_ref, s_ref, a_ref):
    here = at_ref[0]
    _, first, _, _ = read_map(groups_ref, 0)
    _, _, last, _ = read_map(groups_ref, NX - 1)
    s_ref[...] = jnp.where(here > 0, first, 0.0)
    a_ref[...] = jnp.where(here < NX - 1, last, 0.0)
    for step in range(1, NX - 1):
        back = NX - 1 - step

        @pl.when(here > step)
        def _():
            m, state, _, log = read_map(groups_ref, step)
            s = s_ref[...]
            s_ref[...] = jnp.exp(log) * s - mm(split(m), split(s)) + state

        @pl.when(here < back)
        def _():
            m, _, adjoint, log = read_map(groups_ref, back)
            a = a_ref[...]
            a_ref[...] = jnp.exp(log) * a - mm(split(m), split(a), 0, 0) + adjoint

    s, a = s_ref[...], a_ref[...]
    g_in, g_out = (jnp.exp(near_ref[4 * C + 8 * i : 4 * C + 8 * i + 1, 0:1]) for i in range(2))
    s = g_in * s - mm(split(near_ref[0:C, :]), split(s)) + near_ref[C : 2 * C, :]
    a = g_out * a - mm(split(near_ref[2 * C : 3 * C, :]), split(a)) + near_ref[3 * C : 4 * C, :]
    out_ref[0, 0:C, :] = s
    out_ref[1, C : 2 * C, :] = a
    m, state, _, log = read_map(maps_ref, 0)
    out_ref[1, 0:C, :] = jnp.exp(log) * s - mm(split(m), split(s)) + state
    m, _, adjoint, log = read_map(maps_ref, 1)
    out_ref[0, C : 2 * C, :] = jnp.exp(log) * a - mm(split(m), split(a), 0, 0) + adjoint


def grad_kernel(
    place_ref, rate_ref, bias_ref, ends_ref, hid_ref, q_ref, k_ref, v_ref, do_ref, wd_ref, wb_ref,
    uhat_ref, what_ref, z0_ref, y_ref, gram_ref, qk_ref, rows_ref,
    dq_ref, dk_ref, dv_ref, share_ref, weight_ref, sums_ref,
):
    reset = place_ref[0]
    ii, jj = iotas()
    keep = jnp.logical_and(ii >= jj, jnp.logical_or(jj >= reset, ii < reset))
    rows = rows_ref[...]
    cols = rows.T
    keys, key_root = unit_rows(k_ref[...].astype(F32))
    unit_queries, query_root = unit_rows(q_ref[...].astype(F32))
    queries = unit_queries * SCALE
    ks, qs = split(keys), split(queries)
    gram, qk = gram_ref[...], qk_ref[...]
    ii_col = ii[:, 0:1]
    ones = jnp.ones((8, C), BF16)
    lower = (ii >= jj).astype(BF16)
    dq = dk = e_sum = f_sum = None
    for h in range(HEADS):
        c_col, c_row = cols[:, h : h + 1], rows[h : h + 1, :]
        b_col = cols[:, 2 + h : 3 + h]
        lanes = slice(h * C, (h + 1) * C)
        decay = jnp.where(keep, jnp.exp(jnp.where(keep, c_col - c_row, 0.0)), 0.0)
        carry = jnp.where(ii_col < reset, jnp.exp(c_col), 0.0)
        c_last = c_col[C - 1 : C, :]
        late = jnp.logical_or(ii_col >= reset, reset > C - 1)
        weight = jnp.where(late, jnp.exp(jnp.where(late, c_last - c_col, 0.0)), 0.0)
        s, a = ends_ref[h, 0:C, :], ends_ref[h, C : 2 * C, :]
        ss, as_ = split(s), split(a)
        uhat = uhat_ref[h] - mm(split(what_ref[h]), ss)
        z = z0_ref[h] + mm(split(y_ref[h]), as_)
        bz = b_col * z
        dv_ref[:, lanes] = bz.astype(BF16)
        us = split(b_col * uhat)
        cotangent = (do_ref[:, lanes],)
        e = jnp.where(keep, mm(cotangent, us, 1, 1) * decay, 0.0)
        f = jnp.where(ii > jj, mm(split(z), us, 1, 1) * decay * -b_col, 0.0)
        from_out = carry * mm(cotangent, ss, 1, 1)
        from_keys = weight * mm(us, as_, 1, 1)
        key_side = from_keys - carry * mm(split(bz), ss, 1, 1)
        h_mat = e * qk + f * gram
        by_row = h_mat + queries * from_out + keys * (key_side - 2.0 * from_keys)
        dc = sum(dot(ones, t, 1, 1) for t in split3(by_row))
        dc = dc[0:1, :] - jnp.sum(h_mat, axis=0, keepdims=True)
        tail = jnp.sum(jnp.sum(keys * from_keys, axis=0, keepdims=True), axis=1, keepdims=True)
        tail = tail + carry[C - 1 : C, :] * jnp.sum(
            jnp.sum(s * a, axis=0, keepdims=True), axis=1, keepdims=True
        )
        db = sum(dot(ones, t, 1, 1) for t in split3(z * uhat))
        sums_ref[h : h + 1, :] = dc
        sums_ref[2 + h : 3 + h, :] = db[0:1, :]
        sums_ref[4 + h : 5 + h, :] = jnp.broadcast_to(tail, (1, C))
        if h == 0:
            dq, dk, e_sum, f_sum = from_out, key_side, e, f
        else:
            dq, dk, e_sum, f_sum = dq + from_out, dk + key_side, e_sum + e, f_sum + f
    es = split(e_sum)
    dq = dq + mm(es, ks)
    dk = dk + mm(es, qs, 0, 0) + mm(split(f_sum + f_sum.T), ks)
    dq = dq - unit_queries * jnp.sum(unit_queries * dq, axis=-1, keepdims=True)
    dk = dk - keys * jnp.sum(keys * dk, axis=-1, keepdims=True)
    dq_ref[...] = (dq * (query_root * SCALE)).astype(BF16)
    dk_ref[...] = (dk * key_root).astype(BF16)
    dc, db, tail = sums_ref[0:2, :], sums_ref[2:4, :], sums_ref[4:6, :]
    dg = sum(dot(t, lower, 1, 0) for t in split3(dc)) + tail
    beta, log_decay, x = rows_ref[2:4, :], rows_ref[4:6, :], rows_ref[6:8, :]
    dz = dg * -jnp.exp(pair_column(rate_ref[0], rate_ref[1])) * jax.nn.sigmoid(x)
    dzb = db * beta * (1.0 - beta)
    rate_part = jnp.sum(dg * log_decay, axis=1, keepdims=True)
    bias_part = jnp.sum(dz, axis=1, keepdims=True)
    sums_ref[0:2, :] = dz
    sums_ref[2:4, :] = dzb
    sums_ref[4:6, :] = jnp.broadcast_to(rate_part, (2, C))
    sums_ref[6:8, :] = jnp.broadcast_to(bias_part, (2, C))
    for slot in range(NY):
        share_ref[slot, 0:4, :] = sums_ref[0:4, :]
        for half in range(2):
            at = slice((2 * slot + half) * C, (2 * slot + half + 1) * C)
            share_ref[slot, 4 + 4 * half : 6 + 4 * half, :] = wd_ref[:, at].astype(F32)
            share_ref[slot, 6 + 4 * half : 8 + 4 * half, :] = wb_ref[:, at].astype(F32)
        share_ref[slot, 12:16, :] = jnp.zeros((4, C), F32)
    grad = sum(dot(t, hid_ref[...], 1, 0) for t in split3(sums_ref[...]))
    for slot in range(NZ * NC):
        weight_ref[slot, 0:4, :] = grad[0:4, slot * C : (slot + 1) * C]
        weight_ref[slot, 4:8, :] = sums_ref[4:8, :]


def add_kernel(parts_ref, out_ref):
    total = parts_ref[0]
    for i in range(1, NZ * NC):
        total = total + parts_ref[i]
    for slot in range(NX * NZ * NC):
        out_ref[slot] = total


def finish_kernel(share_ref, parts_ref, hidden_ref, wd_ref, wb_ref, stat_ref):
    logit_rows = jnp.concatenate(
        [jnp.concatenate([share_ref[2 * i, 0:4, :], share_ref[2 * i + 1, 0:4, :]], axis=0) for i in range(NY // 2)],
        axis=0,
    )
    terms = split3(logit_rows)
    for half in range(2):
        at = slice(4 + 4 * half, 8 + 4 * half)
        weights = jnp.concatenate(
            [jnp.concatenate([share_ref[2 * i, at, :], share_ref[2 * i + 1, at, :]], axis=0) for i in range(NY // 2)],
            axis=0,
        ).astype(BF16)
        hidden_ref[:, half * C : (half + 1) * C] = sum(dot(t, weights, 0, 0) for t in terms).astype(BF16)
    per = NZ * NC
    for slot in range(per):
        total = parts_ref[slot]
        for group in range(1, NX):
            total = total + parts_ref[group * per + slot]
        wd_ref[:, slot * C : (slot + 1) * C] = total[0:2, :]
        wb_ref[:, slot * C : (slot + 1) * C] = total[2:4, :]
        if slot == 0:
            stat_ref[...] = total


VMEM = pl.BlockSpec(memory_space=pltpu.VMEM)
SMEM = pl.BlockSpec(memory_space=pltpu.SMEM)


def call(kernel, scalars, arrays, outs, scratch=()):
    return pl.pallas_call(
        kernel,
        out_shape=tuple(jax.ShapeDtypeStruct(s, t) for s, t in outs),
        in_specs=[SMEM] * len(scalars) + [VMEM] * len(arrays),
        out_specs=tuple([VMEM] * len(outs)),
        scratch_shapes=list(scratch),
        compiler_params=pltpu.CompilerParams(vmem_limit_bytes=40 * 1024 * 1024),
    )(*scalars, *arrays)


def exchange(a, axes):
    return lax.all_to_all(a, axes, 0, 0, tiled=True)


def on_device(hidden, queries, keys, values, cotangent, w_decay, w_beta, rate, bias, doc_start):
    at_x = lax.axis_index("x").astype(jnp.int32)
    at_z = lax.axis_index("z").astype(jnp.int32)
    at_core = lax.axis_index("core").astype(jnp.int32)
    place = doc_start - ((at_x * NZ + at_z) * NC + at_core) * C
    place = jnp.where(place < 0, C, place)
    wd, wb = w_decay.T, w_beta.T
    square, heads = (C, C), (HEADS, C, C)
    maps, uhat, what, z0, y, gram, qk, rows = call(
        local_kernel,
        (place, rate, bias),
        (hidden, queries, keys, values, cotangent, wd, wb),
        [((HEADS, MAP_ROWS, C), F32)] + [(heads, F32)] * 4 + [(square, F32)] * 2 + [((8, C), F32)],
    )
    maps = exchange(maps, "core")
    (packed,) = call(pair_kernel, (), (maps,), [((PACKED_ROWS, C), F32)])
    packed = jnp.broadcast_to(packed.astype(F16), (NZ, PACKED_ROWS, C))
    ring = exchange(packed, "z").astype(F32)
    groups, near = call(
        ring_kernel,
        (at_z[None],),
        (ring,),
        [((NX, MAP_ROWS, C), F32), ((4 * C + 16, C), F32)],
    )
    groups = exchange(groups, "x")
    (ends,) = call(
        entry_kernel,
        (at_x[None],),
        (groups, near, maps),
        [((NC, 2 * C, C), F32)],
        [pltpu.VMEM(square, F32), pltpu.VMEM(square, F32)],
    )
    ends = exchange(ends, "core")
    dq, dk, dv, share, weights = call(
        grad_kernel,
        (place, rate, bias),
        (ends, hidden, queries, keys, values, cotangent, wd, wb, uhat, what, z0, y, gram, qk, rows),
        [
            (square, BF16),
            (square, BF16),
            ((C, HEADS * C), BF16),
            ((NY, 16, C), F32),
            ((NZ * NC, 8, C), F32),
        ],
        [pltpu.VMEM((8, C), F32)],
    )
    share = exchange(share, "dp")
    weights = exchange(weights, ("z", "core"))
    (weights,) = call(add_kernel, (), (weights,), [((NX * NZ * NC, 8, C), F32)])
    weights = exchange(weights, CTX)
    hidden_grad, wd_grad, wb_grad, stats = call(
        finish_kernel,
        (),
        (share, weights),
        [((C, 2 * C), BF16), ((2, D), F32), ((2, D), F32), ((8, C), F32)],
    )
    return (dq, dk, dv, hidden_grad, wd_grad.T, wb_grad.T, stats[4:6, 0], stats[6:8, 0])


def solution(mesh):
    fine = Mesh(mesh.devices.reshape(NX, NZ, NC, NY), ("x", "z", "core", "dp"))
    rows, both, cols = P(CTX, None), P(CTX, "dp"), P(None, "dp")
    return jax.shard_map(
        on_device,
        mesh=fine,
        in_specs=(rows, both, both, both, both, cols, cols, P("dp"), P("dp"), P()),
        out_specs=(both, both, both, both, cols, cols, P("dp"), P("dp")),
        check_vma=False,
    )
```

time: 802 us -> 126 us (0.16)
  waiting for transfers between devices: 284 us -> 7.11 us
  blocking collectives: 242 us -> 86.8 us
  other arithmetic: 133 us -> 0.12 us
  matrix products: 107 us -> 0 us
  Pallas kernels: 0 us -> 14.9 us
  between operations: 14.9 us -> 1.48 us
    all_gather x4 -> x0, waiting for transfers between devices: 284 us -> none  [entering(): gathered = jax.tree.map(lambda a: lax.all_gather(a, axis), part)]
    psum x1 -> x0, blocking collectives: 242 us -> none  [on_device(): totals = lax.psum((weight_grad, gradients[5], gradients[6]), 'ctx')]
    another operation x78 -> x0, other arithmetic: 125 us -> none  [the longest x42 119 us: block_step(): lax.linalg.triangular_solve(system, target, left_side=True, lower=True, u...]
    dot_general x130 -> x0, matrix products: 103 us -> none  [the longest x63 78.1 us: apply_map(): jnp.einsum('bhij,bhjk->bhik', matrices, incoming, precision=lax.Precision...]
    all_to_all x0 -> x6, blocking collectives: none -> 86.8 us  [exchange(): return lax.all_to_all(a, axes, 0, 0, tiled=True)]
    pallas_call x0 -> x7, Pallas kernels: none -> 14.9 us  [call(): pl.pallas_call(kernel, out_shape=tuple((jax.ShapeDtypeStruct(s, t) for s,...]
  transfers between devices with their start and end apart: 5 -> 1, of which waited for: 4 -> 1; matrix products, arithmetic and copies ran while one was open for 10% -> 0% of each run, Pallas kernels for 0% -> 0%
where the time goes in v1:
time: 126 us; the launch traced here: 125 us
  blocking collectives  86.8 us (69%)
  Pallas kernels  14.9 us (12%)
  local copies, waits for them, and re-layouts  7.76 us (6%)
  waiting for transfers between devices  7.11 us (6%)
  starting transfers between devices  6.83 us (5%)
  between operations  1.48 us (1%)
    all_to_all x6, blocking collectives, exchange(): return lax.all_to_all(a, axes, 0, 0, tiled=True)  86.8 us
    pallas_call x7, Pallas kernels, call(): pl.pallas_call(kernel, out_shape=tuple((jax.ShapeDtypeStruct(s, t) for s,...  14.9 us
    all_to_all x1, waiting for transfers between devices, exchange(): return lax.all_to_all(a, axes, 0, 0, tiled=True)  7.11 us
    unnamed x36, local copies, waits for them, and re-layouts  6.99 us
    all_to_all x1, starting transfers between devices, exchange(): return lax.all_to_all(a, axes, 0, 0, tiled=True)  6.83 us
  transfers between devices with their start and end apart: 1, of which 1 were waited for; matrix products, arithmetic and copies ran while one was open for 0% of the time, Pallas kernels for 0%

profile of v1, /device:TPU:1, one launch (start us, length us, event | category | flops | bytes accessed | tf_op | source)
XLA Modules:
  0.0 125.0 jit_solution(3653238014584714033)
XLA Ops:
  1.3 0.0 copy-start
  1.3 1.0 copy-done
  2.3 0.8 copy-done.2
  3.2 0.8 copy-done.4
  4.0 0.8 copy-done.6
  4.8 0.8 copy-done.8
  5.5 0.7 copy-done.10
  6.2 0.7 copy-done.12
  6.9 0.7 copy-done.14
  7.6 0.7 copy-done.16
  8.2 6.9 %shard_map.161 = (f32[2,392,128]{2,1,0:T(8,128)S(1)}, f32[2,128,128]{2,1,0:T(8,128)S(1)}, f32[2,128,128]{2,1,0:T(8,128)S(1)}, f32[2,128,128]{2,1,0:T(8,128)S(1)}...) custom-call(s32[1]{0:T(128)S(6)} %select_n.4.place_ref, ...), custom_call_target="tpu_custom_call" | custom-call | tf_op jit(solution)/shard_map/pallas_call | solution.py:392
  15.1 10.5 %all_to_all.35.maps_ref = f32[2,392,128]{2,1,0:T(8,128)S(1)} all-to-all(f32[2,392,128]{2,1,0:T(8,128)S(1)} %get-tuple-element.27), channel_id=1, replica_groups=mesh['x'=4,'z'=8,'core'=2,'dp'=8] {'core'}, dimensions={0} | all-to-all | bytes 802816 | tf_op jit(solution)/shard_map/all_to_all | solution.py:403
  25.7 0.3 shard_map.162
  26.0 0.1 broadcast_in_dim.13
  26.2 27.8 %all_to_all.36 = f16[8,400,128]{2,1,0:T(8,128)(2,1)S(1)} all-to-all(f16[8,400,128]{2,1,0:T(8,128)(2,1)S(1)} %broadcast_in_dim.13), channel_id=1, replica_groups=mesh['x'=4,'z'=8,'core'=2,'dp'=8] {'z'}, dimensions={0} | all-to-all | bytes 1638400 | tf_op jit(solution)/shard_map/all_to_all | solution.py:403
  53.9 0.1 convert_element_type.7.maps_ref
  54.1 2.6 %shard_map.163 = (f32[4,392,128]{2,1,0:T(8,128)S(1)}, f32[528,128]{1,0:T(8,128)S(1)}) custom-call(s32[1]{0:T(128)} %bitcast.2.at_ref, f32[8,400,128]{2,1,0:T(8,128)S(1)} %convert_element_type.7.maps_ref), custom_call_target="tpu_custom_call" | custom-call | tf_op jit(solution)/shard_map/pallas_call | solution.py:392
  56.7 0.0 copy-start.1
  56.7 0.0 copy-start.3
  56.8 0.0 copy-start.9
  56.8 0.0 copy-start.11
  56.8 0.0 copy-start.17
  56.8 14.7 %all_to_all.37.groups_ref = f32[4,392,128]{2,1,0:T(8,128)S(1)} all-to-all(f32[4,392,128]{2,1,0:T(8,128)S(1)} %get-tuple-element.28), channel_id=1, replica_groups=mesh['x'=4,'z'=8,'core'=2,'dp'=8] {'x'}, dimensions={0} | all-to-all | bytes 1605632 | tf_op jit(solution)/shard_map/all_to_all | solution.py:403
  71.6 0.8 shard_map.164
  72.4 6.2 %all_to_all.38.ends_ref = f32[2,256,128]{2,1,0:T(8,128)S(1)} all-to-all(f32[2,256,128]{2,1,0:T(8,128)S(1)} %shard_map.164), channel_id=1, replica_groups=mesh['x'=4,'z'=8,'core'=2,'dp'=8] {'core'}, dimensions={0} | all-to-all | bytes 524288 | tf_op jit(solution)/shard_map/all_to_all | solution.py:403
  78.7 3.3 %shard_map.165 = (bf16[128,128]{1,0:T(8,128)(2,1)}, bf16[128,128]{1,0:T(8,128)(2,1)}, bf16[128,256]{1,0:T(8,128)(2,1)}, f32[8,16,128]{2,1,0:T(8,128)}, f32[16,8,128]{2,1,0:T(8,128)S(1)}) custom-call(s32[1]{0:T(128)S(6)} %select_n.4.place_ref, f32[2]{0:T(128)S(1)} %copy-done.15, f32[2]{0:T(128)S(1)} %copy-done.17, f32[2,256,128]{2,1,0:T(8,128)S(1)} %all_to_all.38.ends_ref, ...), custom_call_target="tpu_custom_call" | custom-call | tf_op jit(solution)/shard_map/pallas_call | solution.py:392
  81.9 10.6 %all_to_all.39.parts_ref = f32[16,8,128]{2,1,0:T(8,128)S(1)} all-to-all(f32[16,8,128]{2,1,0:T(8,128)S(1)} %get-tuple-element.41), channel_id=1, replica_groups=mesh['x'=4,'z'=8,'core'=2,'dp'=8] {'z','core'}, dimensions={0} | all-to-all | bytes 131072 | tf_op jit(solution)/shard_map/all_to_all | solution.py:403
  92.5 6.8 %all-to-all-start.4 = ((f32[8,16,128]{2,1,0:T(8,128)}), f32[8,16,128]{2,1,0:T(8,128)S(1)}, u32[]{:S(2)}, u32[]{:S(2)}) async-start(f32[8,16,128]{2,1,0:T(8,128)} %get-tuple-element.40), calls=%async_computation.4 | async-start | bytes 131072 | tf_op jit(solution)/shard_map/all_to_all | solution.py:403
  99.4 7.1 %all-to-all-done.4.share_ref = f32[8,16,128]{2,1,0:T(8,128)S(1)} async-done(((f32[8,16,128]{2,1,0:T(8,128)}), f32[8,16,128]{2,1,0:T(8,128)S(1)}, u32[]{:S(2)}, u32[]{:S(2)}) %all-to-all-start.4) | async-done | bytes 65568 | tf_op jit(solution)/shard_map/all_to_all | solution.py:403
  106.5 17.0 %all_to_all.40.parts_ref = f32[64,8,128]{2,1,0:T(8,128)S(1)} all-to-all(f32[64,8,128]{2,1,0:T(8,128)S(1)} %shard_map.166), channel_id=1, replica_groups=mesh['x'=4,'z'=8,'core'=2,'dp'=8] {'x','z','core'}, dimensions={0} | all-to-all | bytes 524288 | tf_op jit(solution)/shard_map/all_to_all | solution.py:403
  123.5 0.9 shard_map.167
  124.3 0.7 slice_reduce_fusion
  (23 shorter events, 0.1 us)
Async XLA Ops:
  1.3 1.0 copy-start
  2.3 0.8 copy-start.2
  3.2 0.8 copy-start.4
  4.0 0.8 copy-start.6
  4.8 0.8 copy-start.8
  5.5 0.7 copy-start.10
  6.2 0.7 copy-start.12
  6.9 0.7 copy-start.14
  7.6 0.7 copy-start.16
  56.7 21.9 %copy-start.1 = (bf16[128,2048]{1,0:T(8,128)(2,1)S(1)}, bf16[128,2048]{1,0:T(8,128)(2,1)}, u32[]{:S(2)}) copy-start(bf16[128,2048]{1,0:T(8,128)(2,1)} %hid_ref.3) | copy-start | bytes 1572868
  56.7 21.9 %copy-start.3 = (bf16[128,256]{1,0:T(8,128)(2,1)S(1)}, bf16[128,256]{1,0:T(8,128)(2,1)}, u32[]{:S(2)}) copy-start(bf16[128,256]{1,0:T(8,128)(2,1)} %v_ref.3) | copy-start | bytes 196612
  56.7 21.9 %copy-start.5 = (bf16[128,256]{1,0:T(8,128)(2,1)S(1)}, bf16[128,256]{1,0:T(8,128)(2,1)}, u32[]{:S(2)}) copy-start(bf16[128,256]{1,0:T(8,128)(2,1)} %do_ref.3) | copy-start | bytes 196612
  56.7 21.9 %copy-start.7 = (bf16[128,128]{1,0:T(8,128)(2,1)S(1)}, bf16[128,128]{1,0:T(8,128)(2,1)}, u32[]{:S(2)}) copy-start(bf16[128,128]{1,0:T(8,128)(2,1)} %q_ref.3) | copy-start | bytes 98308
  56.8 21.9 %copy-start.9 = (bf16[128,128]{1,0:T(8,128)(2,1)S(1)}, bf16[128,128]{1,0:T(8,128)(2,1)}, u32[]{:S(2)}) copy-start(bf16[128,128]{1,0:T(8,128)(2,1)} %k_ref.3) | copy-start | bytes 98308
  56.8 21.9 %copy-start.11 = (bf16[2048,2]{0,1:T(2,128)(2,1)S(1)}, bf16[2048,2]{0,1:T(2,128)(2,1)}, u32[]{:S(2)}) copy-start(bf16[2048,2]{0,1:T(2,128)(2,1)} %param.15) | copy-start | bytes 24580
  56.8 21.9 %copy-start.13 = (bf16[2048,2]{0,1:T(2,128)(2,1)S(1)}, bf16[2048,2]{0,1:T(2,128)(2,1)}, u32[]{:S(2)}) copy-start(bf16[2048,2]{0,1:T(2,128)(2,1)} %param.16) | copy-start | bytes 24580
  56.8 21.9 %copy-start.15 = (f32[2]{0:T(128)S(1)}, f32[2]{0:T(128)}, u32[]{:S(2)}) copy-start(f32[2]{0:T(128)} %rate_ref.3) | copy-start | bytes 28
  56.8 21.9 %copy-start.17 = (f32[2]{0:T(128)S(1)}, f32[2]{0:T(128)}, u32[]{:S(2)}) copy-start(f32[2]{0:T(128)} %bias_ref.3) | copy-start | bytes 28
  92.5 14.0 %all-to-all-start.4 = ((f32[8,16,128]{2,1,0:T(8,128)}), f32[8,16,128]{2,1,0:T(8,128)S(1)}, u32[]{:S(2)}, u32[]{:S(2)}) async-start(f32[8,16,128]{2,1,0:T(8,128)} %get-tuple-element.40), calls=%async_computation.4 | async-start | bytes 131072 | tf_op jit(solution)/shard_map/all_to_all | solution.py:403

commit v2 on v1

v2 whole, which is shorter than its diff:
```python
import functools

import jax
import jax.numpy as jnp
from jax import lax
from jax.experimental import pallas as pl
from jax.experimental.pallas import tpu as pltpu
from jax.sharding import Mesh
from jax.sharding import PartitionSpec as P

F32 = jnp.float32
BF16 = jnp.bfloat16
F16 = jnp.float16
C = 128
HEADS = 2
D = 2048
NX, NZ, NC, NY = 4, 8, 2, 8
CTX = ("x", "z", "core")
norm_epsilon = 1e-06
SCALE = C**-0.5
FULL_VMEM = 64 << 20
LOG_FLOOR = -200.0
MAP_ROWS = 3 * C + 8
PACKED_ROWS = 3 * C + 16


def split(a):
    high = a.astype(BF16)
    return (high, (a - high.astype(F32)).astype(BF16))


def split3(a):
    high = a.astype(BF16)
    rest = a - high.astype(F32)
    middle = rest.astype(BF16)
    return (high, middle, (rest - middle.astype(F32)).astype(BF16))


def dot(a, b, ca, cb):
    return lax.dot_general(a, b, (((ca,), (cb,)), ((), ())), preferred_element_type=F32)


def mm(a, b, ca=1, cb=0):
    total = dot(a[0], b[0], ca, cb)
    for i in range(len(a)):
        for j in range(len(b)):
            if 0 < i + j < max(len(a), len(b)):
                total = total + dot(a[i], b[j], ca, cb)
    return total


def iotas():
    return (
        lax.broadcasted_iota(jnp.int32, (C, C), 0),
        lax.broadcasted_iota(jnp.int32, (C, C), 1),
    )


def pair_column(first, second):
    row = lax.broadcasted_iota(jnp.int32, (HEADS, C), 0)
    return jnp.where(row == 0, first, second)


def unit_rows(source):
    root = lax.rsqrt(jnp.sum(source * source, axis=-1, keepdims=True) + norm_epsilon)
    return source * root, root


def gate_matrices(rows_ref, cols, h, ii, jj, reset):
    keep = jnp.logical_and(ii >= jj, jnp.logical_or(jj >= reset, ii < reset))
    ii_col = ii[:, 0:1]
    c_col, c_row = cols[:, h : h + 1], rows_ref[h : h + 1, :]
    decay = jnp.where(keep, jnp.exp(jnp.where(keep, c_col - c_row, 0.0)), 0.0)
    carry = jnp.where(ii_col < reset, jnp.exp(c_col), 0.0)
    c_last = c_col[C - 1 : C, :]
    late = jnp.logical_or(ii_col >= reset, reset > C - 1)
    weight = jnp.where(late, jnp.exp(jnp.where(late, c_last - c_col, 0.0)), 0.0)
    return keep, decay, carry, weight, cols[:, 2 + h : 3 + h], c_last


def local_kernel(
    at_ref, doc_hbm, rate_hbm, bias_hbm, k_hbm, hid_hbm, wd_hbm, wb_hbm, q_hbm, v_hbm, do_hbm,
    map_ref, wu_ref, inverse_ref, pdo_ref, gram_ref, qk_ref, rows_ref,
    doc_ref, rate_ref, bias_ref, k_ref, hid_ref, wd_ref, wb_ref, q_ref, v_ref, do_ref, sems,
):
    pairs = (
        (hid_hbm, hid_ref), (wd_hbm, wd_ref), (wb_hbm, wb_ref), (rate_hbm, rate_ref), (bias_hbm, bias_ref),
        (doc_hbm, doc_ref), (k_hbm, k_ref), (q_hbm, q_ref), (v_hbm, v_ref), (do_hbm, do_ref),
    )
    copies = [pltpu.make_async_copy(a, b, sems.at[i]) for i, (a, b) in enumerate(pairs)]
    for copy in copies:
        copy.start()
    ii, jj = iotas()
    copies[6].wait()
    copies[7].wait()
    keys, _ = unit_rows(k_ref[...].astype(F32))
    queries, _ = unit_rows(q_ref[...].astype(F32))
    queries = queries * SCALE
    ks, qs = split(keys), split(queries)
    gram = mm(ks, ks, 1, 1)
    qk = mm(qs, ks, 1, 1)
    gram_ref[...] = gram
    qk_ref[...] = qk
    for copy in copies[:6]:
        copy.wait()
    reset = doc_ref[0] - at_ref[0]
    reset = jnp.where(reset < 0, C, jnp.minimum(reset, C))
    zd = dot(wd_ref[...], hid_ref[...], 1, 1)
    zb = dot(wb_ref[...], hid_ref[...], 1, 1)
    x = zd + pair_column(bias_ref[0], bias_ref[1])
    soft = jnp.maximum(x, 0.0) + jnp.log1p(jnp.exp(-jnp.abs(x)))
    slope = -jnp.exp(pair_column(rate_ref[0], rate_ref[1]))
    log_decay = slope * soft
    upper = (ii <= jj).astype(BF16)
    rows_ref[0:2, :] = sum(dot(t, upper, 1, 0) for t in split3(log_decay))
    rows_ref[2:4, :] = jax.nn.sigmoid(zb)
    rows_ref[4:6, :] = log_decay
    rows_ref[6:8, :] = x
    rows_ref[8:10, :] = slope
    rows_ref[10:16, :] = jnp.broadcast_to(reset.astype(F32), (6, C))
    cols = rows_ref[0:8, :].T
    copies[8].wait()
    copies[9].wait()
    eye = jnp.where(ii == jj, 1.0, 0.0).astype(F32)
    both_heads = range(HEADS)
    gates = [gate_matrices(rows_ref, cols, h, ii, jj, reset) for h in both_heads]
    coupling = [g[4] * jnp.where(ii > jj, g[1] * gram, 0.0) for g in gates]
    inverse = [eye - jnp.where((ii & 1) * (ii - jj) == 1, c, 0.0) for c in coupling]
    for level in range(1, 7):
        bi, bj = ii >> level, jj >> level
        here = (bi & 1) * (bi - bj) == 1
        part = [split(jnp.where(here, c, 0.0)) for c in coupling]
        xs = [split(x) for x in inverse]
        step = [split(mm(part[h], xs[h])) for h in both_heads]
        inverse = [inverse[h] - mm(xs[h], step[h]) for h in both_heads]
    xs = [split(x) for x in inverse]
    cotangent = [(do_ref[:, h * C : (h + 1) * C],) for h in both_heads]
    ps = [split(qk * g[1]) for g in gates]
    right = [
        split(g[4] * jnp.concatenate([g[2] * keys, v_ref[:, h * C : (h + 1) * C].astype(F32)], axis=1))
        for h, g in enumerate(gates)
    ]
    wu = [mm(xs[h], right[h]) for h in both_heads]
    wus = [split(w) for w in wu]
    ml = [mm(split(gates[h][3] * keys), wus[h], 0, 0) for h in both_heads]
    reach = [mm(ps[h], tuple(t[:, :C] for t in wus[h])) for h in both_heads]
    effective = [split(gates[h][2] * queries - reach[h]) for h in both_heads]
    adjoint = [mm(effective[h], cotangent[h], 0, 0) for h in both_heads]
    pdo = [mm(ps[h], cotangent[h], 0, 0) for h in both_heads]
    for h in both_heads:
        inverse_ref[h] = inverse[h]
        wu_ref[h] = wu[h]
        pdo_ref[h] = pdo[h]
        map_ref[h, 0:C, :] = ml[h][:, :C]
        map_ref[h, C : 2 * C, :] = ml[h][:, C:]
        map_ref[h, 2 * C : 3 * C, :] = adjoint[h]
        total = jnp.where(reset > C - 1, jnp.maximum(gates[h][5], LOG_FLOOR), LOG_FLOOR)
        map_ref[h, 3 * C :, :] = jnp.broadcast_to(total, (8, C))


def own_rest(h, ii, jj, k_ref, v_ref, wu_ref, inverse_ref, pdo_ref, gram_ref, rows_ref, uhat_ref, what_ref, z0_ref, y_ref):
    reset = rows_ref[10:11, 0:1].astype(jnp.int32)
    keys, _ = unit_rows(k_ref[...].astype(F32))
    _, decay, carry, weight, _, _ = gate_matrices(rows_ref, rows_ref[0:8, :].T, h, ii, jj, reset)
    inner = jnp.where(ii > jj, decay * gram_ref[...], 0.0)
    both = jnp.concatenate([carry * keys, v_ref[:, h * C : (h + 1) * C].astype(F32)], axis=1)
    hats = both - mm(split(inner), split(wu_ref[h]))
    what_ref[h] = hats[:, :C]
    uhat_ref[h] = hats[:, C:]
    sides = jnp.concatenate([pdo_ref[h], weight * keys], axis=1)
    zy = mm(split(inverse_ref[h]), split(sides), 0, 0)
    z0_ref[h] = zy[:, :C]
    y_ref[h] = zy[:, C:]


def read_map(ref, *at):
    m = ref[(*at, slice(0, C), slice(None))]
    state = ref[(*at, slice(C, 2 * C), slice(None))]
    adjoint = ref[(*at, slice(2 * C, 3 * C), slice(None))]
    log = ref[(*at, slice(3 * C, 3 * C + 1), slice(0, 1))]
    return m, state, adjoint, log


def power_of_two(a):
    largest = jnp.max(jnp.max(jnp.abs(a), axis=0, keepdims=True), axis=1, keepdims=True)
    return jnp.floor(jnp.log2(jnp.maximum(largest, 1e-30)))


def pack(out_ref, parts, log):
    row = lax.broadcasted_iota(jnp.int32, (16, C), 0)
    meta = jnp.zeros((16, C), F32)
    for at, part in enumerate(parts):
        power = power_of_two(part)
        out_ref[at * C : (at + 1) * C, :] = part * jnp.exp2(13.0 - power)
        meta = jnp.where(row == at, power, meta)
    log = jnp.maximum(log, LOG_FLOOR)
    quarters = jnp.floor(log * 4.0)
    fine = log * 4.0 - quarters
    coarse = jnp.floor(fine * 1024.0) * (1.0 / 1024.0)
    meta = jnp.where(row == 3, quarters * 0.25, meta)
    meta = jnp.where(row == 4, coarse, meta)
    meta = jnp.where(row == 5, (fine - coarse) * 1024.0, meta)
    out_ref[3 * C :, :] = meta


def unpack(ref, at):
    meta = ref[at, 3 * C :, :]
    scales = [jnp.exp2(meta[i : i + 1, 0:1] - 13.0) for i in range(3)]
    parts = [ref[at, i * C : (i + 1) * C, :] * scales[i] for i in range(3)]
    log = meta[3:4, 0:1] + 0.25 * (meta[4:5, 0:1] + meta[5:6, 0:1] * (1.0 / 1024.0))
    return parts[0], parts[1], parts[2], log


def pair_kernel(maps_ref, out_ref):
    m0, l0, a0, c0 = read_map(maps_ref, 0)
    m1, l1, a1, c1 = read_map(maps_ref, 1)
    g0, g1 = jnp.exp(c0), jnp.exp(c1)
    m0s, m1s = split(m0), split(m1)
    forward = mm(m1s, tuple(jnp.concatenate([a, b], axis=1) for a, b in zip(m0s, split(l0))))
    m = g1 * m0 + g0 * m1 - forward[:, :C]
    state = g1 * l0 - forward[:, C:] + l1
    adjoint = g0 * a1 - mm(m0s, split(a1), 0, 0) + a0
    pack(out_ref, (m, state, adjoint), c0 + c1)


def ring_kernel(
    at_ref, maps_ref, k_ref, v_ref, wu_ref, inverse_ref, pdo_ref, gram_ref, rows_ref,
    out_ref, near_ref, uhat_ref, what_ref, z0_ref, y_ref,
):
    here = at_ref[0]
    ii, jj = iotas()

    fetch = functools.partial(unpack, maps_ref)
    zero = jnp.zeros((C, C), F32)

    @pl.when(here == 0)
    def _():
        near_ref[0:C, :] = zero
        near_ref[C : 2 * C, :] = zero
        near_ref[4 * C : 4 * C + 8, :] = jnp.zeros((8, C), F32)

    @pl.when(here == NZ - 1)
    def _():
        near_ref[2 * C : 3 * C, :] = zero
        near_ref[3 * C : 4 * C, :] = zero
        near_ref[4 * C + 8 :, :] = jnp.zeros((8, C), F32)

    m, state, _, log = fetch(0)
    m_back, _, adjoint, log_back = fetch(NZ - 1)
    m_back = m_back.T
    for step in range(1, NZ):
        back = NZ - 1 - step
        if step in (2, 5):
            own_rest(
                step // 4, ii, jj, k_ref, v_ref, wu_ref, inverse_ref, pdo_ref, gram_ref, rows_ref,
                uhat_ref, what_ref, z0_ref, y_ref,
            )

        @pl.when(here == step)
        def _():
            near_ref[0:C, :] = m
            near_ref[C : 2 * C, :] = state
            near_ref[4 * C : 4 * C + 8, :] = jnp.broadcast_to(log, (8, C))

        @pl.when(here == back)
        def _():
            near_ref[2 * C : 3 * C, :] = m_back
            near_ref[3 * C : 4 * C, :] = adjoint
            near_ref[4 * C + 8 :, :] = jnp.broadcast_to(log_back, (8, C))

        mz, lz, _, cz = fetch(step)
        moved = mm(split(mz), split(jnp.concatenate([m, state], axis=1)))
        gz, g = jnp.exp(cz), jnp.exp(log)
        m, state = gz * m + g * mz - moved[:, :C], gz * state + lz - moved[:, C:]
        log = log + cz
        mz, _, az, cz = fetch(back)
        mz = mz.T
        moved = mm(split(mz), split(jnp.concatenate([m_back, adjoint], axis=1)))
        gz, g = jnp.exp(cz), jnp.exp(log_back)
        m_back, adjoint = gz * m_back + g * mz - moved[:, :C], gz * adjoint + az - moved[:, C:]
        log_back = log_back + cz
    pack(out_ref, (m, state, adjoint), log)


def entry_kernel(at_ref, groups_ref, near_ref, maps_ref, out_ref, s_ref, a_ref):
    here = at_ref[0]
    _, first, _, _ = unpack(groups_ref, 0)
    _, _, last, _ = unpack(groups_ref, NX - 1)
    s_ref[...] = jnp.where(here > 0, first, 0.0)
    a_ref[...] = jnp.where(here < NX - 1, last, 0.0)
    for step in range(1, NX - 1):
        back = NX - 1 - step

        @pl.when(here > step)
        def _():
            m, state, _, log = unpack(groups_ref, step)
            s = s_ref[...]
            s_ref[...] = jnp.exp(log) * s - mm(split(m), split(s)) + state

        @pl.when(here < back)
        def _():
            m, _, adjoint, log = unpack(groups_ref, back)
            a = a_ref[...]
            a_ref[...] = jnp.exp(log) * a - mm(split(m), split(a), 0, 0) + adjoint

    s, a = s_ref[...], a_ref[...]
    g_in, g_out = (jnp.exp(near_ref[4 * C + 8 * i : 4 * C + 8 * i + 1, 0:1]) for i in range(2))
    s = g_in * s - mm(split(near_ref[0:C, :]), split(s)) + near_ref[C : 2 * C, :]
    a = g_out * a - mm(split(near_ref[2 * C : 3 * C, :]), split(a)) + near_ref[3 * C : 4 * C, :]
    out_ref[0, 0:C, :] = s
    out_ref[1, C : 2 * C, :] = a
    m, state, _, log = read_map(maps_ref, 0)
    out_ref[1, 0:C, :] = jnp.exp(log) * s - mm(split(m), split(s)) + state
    m, _, adjoint, log = read_map(maps_ref, 1)
    out_ref[0, C : 2 * C, :] = jnp.exp(log) * a - mm(split(m), split(a), 0, 0) + adjoint


def grad_kernel(
    at_z_ref, at_y_ref,
    ends_ref, hid_ref, k_ref, q_ref, do_ref, wd_ref, wb_ref,
    uhat_ref, what_ref, z0_ref, y_ref, gram_ref, qk_ref, rows_ref,
    dv_ref, e_ref, f_ref, query_side_ref, key_side_ref, share_ref, own_ref,
    sums_ref,
):
    here, mine = at_z_ref[0], at_y_ref[0]
    ii, jj = iotas()
    reset = rows_ref[10:11, 0:1].astype(jnp.int32)
    cols = rows_ref[0:8, :].T
    keys, _ = unit_rows(k_ref[...].astype(F32))
    queries = unit_rows(q_ref[...].astype(F32))[0] * SCALE
    gram, qk = gram_ref[...], qk_ref[...]
    ones = jnp.ones((8, C), BF16)
    lower = (ii >= jj).astype(BF16)
    both_heads = range(HEADS)
    gates = [gate_matrices(rows_ref, cols, h, ii, jj, reset) for h in both_heads]
    states = [ends_ref[h, 0:C, :] for h in both_heads]
    adjoints = [ends_ref[h, C : 2 * C, :] for h in both_heads]
    ss, as_ = [split(s) for s in states], [split(a) for a in adjoints]
    cotangent = [(do_ref[:, h * C : (h + 1) * C],) for h in both_heads]
    uhat = [uhat_ref[h] - mm(split(what_ref[h]), ss[h]) for h in both_heads]
    z = [z0_ref[h] + mm(split(y_ref[h]), as_[h]) for h in both_heads]
    from_out = [gates[h][2] * mm(cotangent[h], ss[h], 1, 1) for h in both_heads]
    bz = [gates[h][4] * z[h] for h in both_heads]
    us = [split(gates[h][4] * uhat[h]) for h in both_heads]
    zs, bzs = [split(a) for a in z], [split(a) for a in bz]
    from_keys = [gates[h][3] * mm(us[h], as_[h], 1, 1) for h in both_heads]
    through = [mm(bzs[h], ss[h], 1, 1) for h in both_heads]
    e = [mm(cotangent[h], us[h], 1, 1) for h in both_heads]
    f = [mm(zs[h], us[h], 1, 1) for h in both_heads]
    e = [jnp.where(gates[h][0], e[h] * gates[h][1], 0.0) for h in both_heads]
    f = [jnp.where(ii > jj, f[h] * gates[h][1] * -gates[h][4], 0.0) for h in both_heads]
    key_side = [from_keys[h] - gates[h][2] * through[h] for h in both_heads]
    h_mat = [e[h] * qk + f[h] * gram for h in both_heads]
    by_row = [
        split3(h_mat[h] + queries * from_out[h] + keys * (key_side[h] - 2.0 * from_keys[h]))
        for h in both_heads
    ]
    zu = [split3(z[h] * uhat[h]) for h in both_heads]
    dc = [sum(dot(ones, t, 1, 1) for t in by_row[h]) for h in both_heads]
    db = [sum(dot(ones, t, 1, 1) for t in zu[h]) for h in both_heads]
    for h in both_heads:
        carry = gates[h][2]
        ends = keys * from_keys[h] + carry[C - 1 : C, :] * states[h] * adjoints[h]
        tail = jnp.sum(jnp.sum(ends, axis=0, keepdims=True), axis=1, keepdims=True)
        sums_ref[h : h + 1, :] = dc[h][0:1, :] - jnp.sum(h_mat[h], axis=0, keepdims=True)
        sums_ref[2 + h : 3 + h, :] = db[h][0:1, :]
        sums_ref[4 + h : 5 + h, :] = jnp.broadcast_to(tail, (1, C))
        dv_ref[:, h * C : (h + 1) * C] = bz[h].astype(BF16)
    e_ref[...] = e[0] + e[1]
    f_ref[...] = f[0] + f[1]
    query_side_ref[...] = from_out[0] + from_out[1]
    key_side_ref[...] = key_side[0] + key_side[1]
    dc, db, tail = sums_ref[0:2, :], sums_ref[2:4, :], sums_ref[4:6, :]
    dg = sum(dot(t, lower, 1, 0) for t in split3(dc)) + tail
    beta, log_decay = rows_ref[2:4, :], rows_ref[4:6, :]
    dz = dg * rows_ref[8:10, :] * jax.nn.sigmoid(rows_ref[6:8, :])
    own_ref[0:2, :] = dz
    own_ref[2:4, :] = db * beta * (1.0 - beta)
    own_ref[4:6, :] = jnp.broadcast_to(jnp.sum(dg * log_decay, axis=1, keepdims=True), (2, C))
    own_ref[6:8, :] = jnp.broadcast_to(jnp.sum(dz, axis=1, keepdims=True), (2, C))
    grad = sum(dot(t, hid_ref[...], 1, 0) for t in split3(own_ref[0:4, :]))
    share_ref[...] = jnp.zeros_like(share_ref)
    after = lax.rem(here + 1, NZ)
    for other in range(NY):
        share_ref[here * NY + other, 0:4, :] = own_ref[0:4, :]
        for half in range(2):
            at = slice((2 * other + half) * C, (2 * other + half + 1) * C)
            share_ref[after * NY + other, 4 * half : 4 * half + 2, :] = wd_ref[:, at].astype(F32)
            share_ref[after * NY + other, 4 * half + 2 : 4 * half + 4, :] = wb_ref[:, at].astype(F32)
    for z in range(NZ):
        for half in range(2):
            at = slice((2 * z + half) * C, (2 * z + half + 1) * C)
            share_ref[z * NY + mine, 4 * half : 4 * half + 4, :] = grad[:, at]


def vector_kernel(k_ref, q_ref, e_ref, f_ref, query_side_ref, key_side_ref, dq_ref, dk_ref):
    keys, key_root = unit_rows(k_ref[...].astype(F32))
    unit_queries, query_root = unit_rows(q_ref[...].astype(F32))
    ks, qs = split(keys), split(unit_queries * SCALE)
    es, f = split(e_ref[...]), f_ref[...]
    dq = query_side_ref[...] + mm(es, ks)
    dk = key_side_ref[...] + mm(es, qs, 0, 0) + mm(split(f + f.T), ks)
    dq = dq - unit_queries * jnp.sum(unit_queries * dq, axis=-1, keepdims=True)
    dk = dk - keys * jnp.sum(keys * dk, axis=-1, keepdims=True)
    dq_ref[...] = (dq * (query_root * SCALE)).astype(BF16)
    dk_ref[...] = (dk * key_root).astype(BF16)


def sum_kernel(at_y_ref, share_ref, own_ref, out_ref):
    mine = at_y_ref[0]
    total = share_ref[mine]
    for z in range(1, NZ):
        total = total + share_ref[z * NY + mine]
    power = power_of_two(total)
    out_ref[0:8, :] = total * jnp.exp2(13.0 - power)
    lane = lax.broadcasted_iota(jnp.int32, (1, C), 1) >> 5
    sums = own_ref[4:5, :]
    for i in range(1, 4):
        sums = jnp.where(lane == i, own_ref[4 + i : 5 + i, :], sums)
    powers = jnp.floor(jnp.log2(jnp.maximum(jnp.abs(sums), 1e-30)))
    scaled = sums * jnp.exp2(-powers)
    high = jnp.floor(scaled * 256.0) * (1.0 / 256.0)
    out_ref[8:9, :] = jnp.broadcast_to(power, (1, C))
    out_ref[9:10, :] = powers
    out_ref[10:11, :] = high
    out_ref[11:12, :] = (scaled - high) * 256.0
    out_ref[12:16, :] = jnp.zeros((4, C), F32)


def hidden_kernel(at_z_ref, at_y_ref, share_ref, own_ref, wd_ref, wb_ref, hidden_ref, lg_ref, w_ref):
    here, mine = at_z_ref[0], at_y_ref[0]
    before = lax.rem(here + NZ - 1, NZ)
    for y in range(NY):
        rows = slice(4 * y, 4 * y + 4)

        @pl.when(mine == y)
        def _():
            lg_ref[rows, :] = own_ref[0:4, :]
            w_ref[4 * y : 4 * y + 2, :] = wd_ref[:, 2 * y * C : 2 * (y + 1) * C].astype(F32)
            w_ref[4 * y + 2 : 4 * y + 4, :] = wb_ref[:, 2 * y * C : 2 * (y + 1) * C].astype(F32)

        @pl.when(mine != y)
        def _():
            lg_ref[rows, :] = share_ref[here * NY + y, 0:4, :]
            w_ref[rows, 0:C] = share_ref[before * NY + y, 0:4, :]
            w_ref[rows, C : 2 * C] = share_ref[before * NY + y, 4:8, :]

    weights = w_ref[...].astype(BF16)
    hidden = sum(dot(t, weights, 0, 0) for t in split3(lg_ref[...]))
    hidden_ref[...] = hidden.astype(BF16)


def finish_kernel(parts_ref, wd_ref, wb_ref, rate_ref, bias_ref):
    per = NZ * NC
    sums = jnp.zeros((1, C), F32)
    for z in range(NZ):
        total = jnp.zeros((8, C), F32)
        for x in range(NX):
            for core in range(NC):
                part = parts_ref[x * per + z * NC + core]
                total = total + part[0:8, :] * jnp.exp2(part[8:9, :] - 13.0)
                sums = sums + (part[10:11, :] + part[11:12, :] * (1.0 / 256.0)) * jnp.exp2(part[9:10, :])
        for half in range(2):
            at = slice((2 * z + half) * C, (2 * z + half + 1) * C)
            wd_ref[:, at] = total[4 * half : 4 * half + 2, :]
            wb_ref[:, at] = total[4 * half + 2 : 4 * half + 4, :]
    lane = lax.broadcasted_iota(jnp.int32, (1, C), 1)
    for i in range(2):
        rate_ref[i] = jnp.sum(jnp.where(lane == 32 * i, sums, 0.0))
        bias_ref[i] = jnp.sum(jnp.where(lane == 64 + 32 * i, sums, 0.0))


VMEM = pl.BlockSpec(memory_space=pltpu.VMEM)
SMEM = pl.BlockSpec(memory_space=pltpu.SMEM)
HBM = pl.BlockSpec(memory_space=pltpu.HBM)


def call(kernel, scalars, arrays, outs, scratch=(), space=VMEM, small=0, flops=0, vmem=40 << 20):
    return pl.pallas_call(
        kernel,
        out_shape=tuple(jax.ShapeDtypeStruct(s, t) for s, t in outs),
        in_specs=[SMEM] * len(scalars) + [space] * len(arrays),
        out_specs=tuple([VMEM] * (len(outs) - small) + [SMEM] * small),
        scratch_shapes=list(scratch),
        compiler_params=pltpu.CompilerParams(vmem_limit_bytes=vmem),
        cost_estimate=pl.CostEstimate(flops=flops, bytes_accessed=1 << 20, transcendentals=0) if flops else None,
    )(*scalars, *arrays)


def exchange(a, axes):
    return lax.all_to_all(a, axes, 0, 0, tiled=True)


def spread(a, count, axes):
    a = jnp.broadcast_to(a.astype(F16), (count, *a.shape))
    return exchange(a, axes).astype(F32)


def on_device(hidden, queries, keys, values, cotangent, w_decay, w_beta, rate, bias, doc_start):
    at_x = lax.axis_index("x").astype(jnp.int32)
    at_z = lax.axis_index("z").astype(jnp.int32)
    at_core = lax.axis_index("core").astype(jnp.int32)
    at_y = lax.axis_index("dp").astype(jnp.int32)
    first = ((at_x * NZ + at_z) * NC + at_core) * C
    at_x, at_y, at_z, first = (a[None] for a in (at_x, at_y, at_z, first))
    wd, wb = w_decay.T, w_beta.T
    square, heads, wide = (C, C), (HEADS, C, C), (C, HEADS * C)
    maps, wu, inverse, pdo, gram, qk, rows = call(
        local_kernel,
        (first,),
        (doc_start, rate, bias, keys, hidden, wd, wb, queries, values, cotangent),
        [
            ((HEADS, MAP_ROWS, C), F32),
            ((HEADS, C, 2 * C), F32),
            (heads, F32),
            (heads, F32),
            (square, F32),
            (square, F32),
            ((16, C), F32),
        ],
        [
            pltpu.SMEM((1,), jnp.int32),
            pltpu.SMEM((2,), F32),
            pltpu.SMEM((2,), F32),
            pltpu.VMEM(square, BF16),
            pltpu.VMEM((C, D), BF16),
            pltpu.VMEM((2, D), BF16),
            pltpu.VMEM((2, D), BF16),
            pltpu.VMEM(square, BF16),
            pltpu.VMEM(wide, BF16),
            pltpu.VMEM(wide, BF16),
            pltpu.SemaphoreType.DMA((10,)),
        ],
        HBM,
        vmem=FULL_VMEM,
    )
    maps = exchange(maps, "core")
    (packed,) = call(pair_kernel, (), (maps,), [((PACKED_ROWS, C), F32)])
    ring = spread(packed, NZ, "z")
    packed, near, uhat, what, z0, y = call(
        ring_kernel,
        (at_z,),
        (ring, keys, values, wu, inverse, pdo, gram, rows),
        [((PACKED_ROWS, C), F32), ((4 * C + 16, C), F32)] + [(heads, F32)] * 4,
    )
    groups = spread(packed, NX, "x")
    (ends,) = call(
        entry_kernel,
        (at_x,),
        (groups, near, maps),
        [((NC, 2 * C, C), F32)],
        [pltpu.VMEM(square, F32), pltpu.VMEM(square, F32)],
    )
    ends = exchange(ends, "core")
    dv, e, f, query_side, key_side, share, own = call(
        grad_kernel,
        (at_z, at_y),
        (ends, hidden, keys, queries, cotangent, wd, wb, uhat, what, z0, y, gram, qk, rows),
        [(wide, BF16)] + [(square, F32)] * 4 + [((NZ * NY, 8, C), F32), ((8, C), F32)],
        [pltpu.VMEM((8, C), F32)],
    )
    share = exchange(share, ("z", "dp"))
    dq, dk = call(
        vector_kernel,
        (),
        (keys, queries, e, f, query_side, key_side),
        [(square, BF16), (square, BF16)],
        flops=1 << 28,
    )
    (sums,) = call(sum_kernel, (at_y,), (share, own), [((16, C), F32)])
    parts = spread(sums, NX * NZ * NC, CTX)
    (hidden_grad,) = call(
        hidden_kernel,
        (at_z, at_y),
        (share, own, wd, wb),
        [(wide, BF16)],
        [pltpu.VMEM((4 * NY, C), F32), pltpu.VMEM((4 * NY, 2 * C), F32)],
        flops=1 << 28,
    )
    wd_grad, wb_grad, rate_grad, bias_grad = call(
        finish_kernel,
        (),
        (parts,),
        [((2, D), F32), ((2, D), F32), ((HEADS,), F32), ((HEADS,), F32)],
        small=2,
    )
    return (dq, dk, dv, hidden_grad, wd_grad.T, wb_grad.T, rate_grad, bias_grad)


def solution(mesh):
    fine = Mesh(mesh.devices.reshape(NX, NZ, NC, NY), ("x", "z", "core", "dp"))
    rows, both, cols = P(CTX, None), P(CTX, "dp"), P(None, "dp")
    return jax.shard_map(
        on_device,
        mesh=fine,
        in_specs=(rows, both, both, both, both, cols, cols, P("dp"), P("dp"), P()),
        out_specs=(both, both, both, both, cols, cols, P("dp"), P("dp")),
        check_vma=False,
    )
```

time: 126 us -> 114 us (0.905)
  blocking collectives: 86.8 us -> 66.9 us
  waiting for transfers between devices: 7.11 us -> 16.3 us
  local copies, waits for them, and re-layouts: 7.76 us -> 2.69 us
  starting transfers between devices: 6.83 us -> 10.9 us
    all_to_all x6 -> x4, blocking collectives: 86.8 us -> 66.9 us  [exchange(): return lax.all_to_all(a, axes, 0, 0, tiled=True)]
    all_to_all x1 -> x2, waiting for transfers between devices: 7.11 us -> 16.3 us  [exchange(): return lax.all_to_all(a, axes, 0, 0, tiled=True)]
    unnamed x36 -> x26, local copies, waits for them, and re-layouts: 6.99 us -> 1.01 us
    all_to_all x1 -> x2, starting transfers between devices: 6.83 us -> 10.9 us  [exchange(): return lax.all_to_all(a, axes, 0, 0, tiled=True)]
    broadcast_in_dim x1 -> x3, local copies, waits for them, and re-layouts: 0.11 us -> 1.67 us  [spread(): a = jnp.broadcast_to(a.astype(F16), (count, *a.shape))]
    pallas_call x7 -> x9, Pallas kernels: 14.9 us -> 15.2 us  [call(): pl.pallas_call(kernel, out_shape=tuple((jax.ShapeDtypeStruct(s, t) for s,...]
  transfers between devices with their start and end apart: 1 -> 2, of which waited for: 1 -> 2; matrix products, arithmetic and copies ran while one was open for 0% -> 0% of each run, Pallas kernels for 0% -> 2%
where the time goes in v2:
time: 114 us
  blocking collectives  66.9 us (59%)
  waiting for transfers between devices  16.3 us (14%)
  Pallas kernels  15.2 us (13%)
  starting transfers between devices  10.9 us (10%)
  local copies, waits for them, and re-layouts  2.69 us (2%)
  between operations  1.46 us (1%)
    all_to_all x4, blocking collectives, exchange(): return lax.all_to_all(a, axes, 0, 0, tiled=True)  66.9 us
    all_to_all x2, waiting for transfers between devices, exchange(): return lax.all_to_all(a, axes, 0, 0, tiled=True)  16.3 us
    pallas_call x9, Pallas kernels, call(): pl.pallas_call(kernel, out_shape=tuple((jax.ShapeDtypeStruct(s, t) for s,...  15.2 us
    all_to_all x2, starting transfers between devices, exchange(): return lax.all_to_all(a, axes, 0, 0, tiled=True)  10.9 us
  transfers between devices with their start and end apart: 2, of which 2 were waited for; matrix products, arithmetic and copies ran while one was open for 0% of the time, Pallas kernels for 2%

profile of v2, /device:TPU:1, one launch (start us, length us, event | category | flops | bytes accessed | tf_op | source)
XLA Modules:
  0.0 113.7 jit_solution(1317103925097746655)
XLA Ops:
  1.3 5.9 %shard_map.161 = (f32[2,392,128]{2,1,0:T(8,128)}, f32[2,128,256]{2,1,0:T(8,128)}, f32[2,128,128]{2,1,0:T(8,128)}, f32[2,128,128]{2,1,0:T(8,128)}, f32[128,128]{1...) custom-call(s32[1]{0:T(128)} %bitcast.3.at_ref, s32[1]{0:T(128)S(6)} %copy.18.doc_hbm, f32[2]{0:T(128)} %rate_hbm.1, ...), custom_call_target="tpu_custom_call" | custom-call | tf_op jit(solution)/shard_map/pallas_call | solution.py:479
  7.2 11.6 %all_to_all.30.maps_ref = f32[2,392,128]{2,1,0:T(8,128)S(1)} all-to-all(f32[2,392,128]{2,1,0:T(8,128)} %get-tuple-element.34), channel_id=1, replica_groups=mesh['x'=4,'z'=8,'core'=2,'dp'=8] {'core'}, dimensions={0} | all-to-all | bytes 802816 | tf_op jit(solution)/shard_map/all_to_all | solution.py:491
  18.8 0.3 shard_map.162
  19.2 0.1 broadcast_in_dim.25
  19.3 27.8 %all_to_all.31 = f16[8,400,128]{2,1,0:T(8,128)(2,1)S(1)} all-to-all(f16[8,400,128]{2,1,0:T(8,128)(2,1)S(1)} %broadcast_in_dim.25), channel_id=1, replica_groups=mesh['x'=4,'z'=8,'core'=2,'dp'=8] {'z'}, dimensions={0} | all-to-all | bytes 1638400 | tf_op jit(solution)/shard_map/all_to_all | solution.py:491
  47.1 0.0 copy-start.12
  47.2 0.1 convert_element_type.19.maps_ref
  47.3 0.6 copy-done.1
  47.9 0.2 copy-done.2
  48.1 0.0 copy-done.5
  48.1 0.1 copy-done.6
  48.2 0.1 copy-done.7
  48.2 0.0 copy-done.12
  48.2 3.1 %shard_map.163 = (f32[400,128]{1,0:T(8,128)S(1)}, f32[528,128]{1,0:T(8,128)S(1)}, f32[2,128,128]{2,1,0:T(8,128)S(1)}, f32[2,128,128]{2,1,0:T(8,128)S(1)}, f32[2,...) custom-call(s32[1]{0:T(128)} %bitcast.at_ref.at_z_ref, f32[8,400,128]{2,1,0:T(8,128)S(1)} %convert_element_type.19.maps_ref, ...), custom_call_target="tpu_custom_call" | custom-call | tf_op jit(solution)/shard_map/pallas_call | solution.py:479
  51.4 0.8 broadcast_in_dim.26
  52.2 4.0 %all-to-all-start.2 = ((f16[4,400,128]{2,1,0:T(8,128)(2,1)}), f16[4,400,128]{2,1,0:T(8,128)(2,1)S(1)}, u32[]{:S(2)}, u32[]{:S(2)}) async-start(f16[4,400,128]{2,1,0:T(8,128)(2,1)} %broadcast_in_dim.26), calls=%async_computation.2 | async-start | bytes 819200 | tf_op jit(solution)/shard_map/all_to_all | solution.py:491
  56.2 0.0 copy-start.9
  56.3 0.0 copy-start.10
  56.3 0.0 copy-start.11
  56.3 6.3 %all-to-all-done.2 = f16[4,400,128]{2,1,0:T(8,128)(2,1)S(1)} async-done(((f16[4,400,128]{2,1,0:T(8,128)(2,1)}), f16[4,400,128]{2,1,0:T(8,128)(2,1)S(1)}, u32[]{:S(2)}, u32[]{:S(2)}) %all-to-all-start.2) | async-done | bytes 409632 | tf_op jit(solution)/shard_map/all_to_all | solution.py:491
  62.6 0.1 convert_element_type.21.groups_ref
  62.7 1.0 shard_map.164
  63.6 6.4 %all_to_all.32.ends_ref = f32[2,256,128]{2,1,0:T(8,128)S(1)} all-to-all(f32[2,256,128]{2,1,0:T(8,128)S(1)} %shard_map.164), channel_id=1, replica_groups=mesh['x'=4,'z'=8,'core'=2,'dp'=8] {'core'}, dimensions={0} | all-to-all | bytes 524288 | tf_op jit(solution)/shard_map/all_to_all | solution.py:491
  70.1 2.0 %shard_map.165 = (bf16[128,256]{1,0:T(8,128)(2,1)}, f32[128,128]{1,0:T(8,128)S(1)}, f32[128,128]{1,0:T(8,128)S(1)}, f32[128,128]{1,0:T(8,128)S(1)}, f32[128,128]...) custom-call(s32[1]{0:T(128)} %bitcast.at_ref.at_z_ref, s32[1]{0:T(128)} %bitcast.1.at_y_ref, ...), custom_call_target="tpu_custom_call" | custom-call | tf_op jit(solution)/shard_map/pallas_call | solution.py:479
  72.1 21.1 %all_to_all.33.share_ref = f32[64,8,128]{2,1,0:T(8,128)S(1)} all-to-all(f32[64,8,128]{2,1,0:T(8,128)S(1)} %get-tuple-element.54), channel_id=1, replica_groups=mesh['x'=4,'z'=8,'core'=2,'dp'=8] {'z','dp'}, dimensions={0} | all-to-all | bytes 524288 | tf_op jit(solution)/shard_map/all_to_all | solution.py:491
  93.2 0.1 shard_map.168
  93.3 0.7 broadcast_in_dim.27
  94.0 6.9 %all-to-all-start.5 = ((f16[64,16,128]{2,1,0:T(8,128)(2,1)}), f16[64,16,128]{2,1,0:T(8,128)(2,1)S(1)}, u32[]{:S(2)}, u32[]{:S(2)}) async-start(f16[64,16,128]{2,1,0:T(8,128)(2,1)} %broadcast_in_dim.27), calls=%async_computation.5 | async-start | bytes 524288 | tf_op jit(solution)/shard_map/all_to_all | solution.py:491
  100.9 1.1 shard_map.166
  102.0 0.9 shard_map.167
  102.9 10.0 %all-to-all-done.5 = f16[64,16,128]{2,1,0:T(8,128)(2,1)S(1)} async-done(((f16[64,16,128]{2,1,0:T(8,128)(2,1)}), f16[64,16,128]{2,1,0:T(8,128)(2,1)S(1)}, u32[]{:S(2)}, u32[]{:S(2)}) %all-to-all-start.5) | async-done | bytes 262176 | tf_op jit(solution)/shard_map/all_to_all | solution.py:491
  113.0 0.7 shard_map.169
  (20 shorter events, 0.1 us)
Async XLA Ops:
  47.1 0.8 copy-start.1
  47.1 1.0 copy-start.2
  47.1 1.0 copy-start.3
  47.1 1.0 copy-start.5
  47.1 1.1 copy-start.6
  47.1 1.1 copy-start.7
  47.1 1.1 copy-start.12
  52.2 10.4 %all-to-all-start.2 = ((f16[4,400,128]{2,1,0:T(8,128)(2,1)}), f16[4,400,128]{2,1,0:T(8,128)(2,1)S(1)}, u32[]{:S(2)}, u32[]{:S(2)}) async-start(f16[4,400,128]{2,1,0:T(8,128)(2,1)} %broadcast_in_dim.26), calls=%async_computation.2 | async-start | bytes 819200 | tf_op jit(solution)/shard_map/all_to_all | solution.py:491
  56.2 13.8 %copy-start = (bf16[128,2048]{1,0:T(8,128)(2,1)S(1)}, bf16[128,2048]{1,0:T(8,128)(2,1)}, u32[]{:S(2)}) copy-start(bf16[128,2048]{1,0:T(8,128)(2,1)} %hid_ref.1) | copy-start | bytes 1572868
  56.2 13.8 %copy-start.4 = (bf16[128,256]{1,0:T(8,128)(2,1)S(1)}, bf16[128,256]{1,0:T(8,128)(2,1)}, u32[]{:S(2)}) copy-start(bf16[128,256]{1,0:T(8,128)(2,1)} %do_ref.1) | copy-start | bytes 196612
  56.2 13.8 %copy-start.8 = (bf16[128,128]{1,0:T(8,128)(2,1)S(1)}, bf16[128,128]{1,0:T(8,128)(2,1)}, u32[]{:S(2)}) copy-start(bf16[128,128]{1,0:T(8,128)(2,1)} %q_ref.3) | copy-start | bytes 98308
  56.2 13.8 %copy-start.9 = (f32[128,128]{1,0:T(8,128)S(1)}, f32[128,128]{1,0:T(8,128)}, u32[]{:S(2)}) copy-start(f32[128,128]{1,0:T(8,128)} %get-tuple-element.46.qk_ref) | copy-start | bytes 196612
  56.3 13.8 %copy-start.10 = (bf16[2048,2]{0,1:T(2,128)(2,1)S(1)}, bf16[2048,2]{0,1:T(2,128)(2,1)}, u32[]{:S(2)}) copy-start(bf16[2048,2]{0,1:T(2,128)(2,1)} %param.15) | copy-start | bytes 24580
  56.3 13.8 %copy-start.11 = (bf16[2048,2]{0,1:T(2,128)(2,1)S(1)}, bf16[2048,2]{0,1:T(2,128)(2,1)}, u32[]{:S(2)}) copy-start(bf16[2048,2]{0,1:T(2,128)(2,1)} %param.16) | copy-start | bytes 24580
  94.0 18.9 %all-to-all-start.5 = ((f16[64,16,128]{2,1,0:T(8,128)(2,1)}), f16[64,16,128]{2,1,0:T(8,128)(2,1)S(1)}, u32[]{:S(2)}, u32[]{:S(2)}) async-start(f16[64,16,128]{2,1,0:T(8,128)(2,1)} %broadcast_in_dim.27), calls=%async_computation.5 | async-start | bytes 524288 | tf_op jit(solution)/shard_map/all_to_all | solution.py:491

commit v3 on v2

--- a/solution.py
+++ b/solution.py
@@ -18,10 +18,7 @@
 CTX = ("x", "z", "core")
 norm_epsilon = 1e-06
 SCALE = C**-0.5
-FULL_VMEM = 64 << 20
-LOG_FLOOR = -200.0
-MAP_ROWS = 3 * C + 8
-PACKED_ROWS = 3 * C + 16
+MAP_ROWS = 3 * C
 
 
 def split(a):
@@ -41,6 +38,8 @@
 
 
 def mm(a, b, ca=1, cb=0):
+    if len(a) == len(b) == 2 and (ca, cb) != (0, 1):
+        return dot(jnp.concatenate([a[0], a[0], a[1]], axis=ca), jnp.concatenate([b[0], b[1], b[0]], axis=cb), ca, cb)
     total = dot(a[0], b[0], ca, cb)
     for i in range(len(a)):
         for j in range(len(b)):
@@ -79,20 +78,20 @@
 
 
 def local_kernel(
-    at_ref, doc_hbm, rate_hbm, bias_hbm, k_hbm, hid_hbm, wd_hbm, wb_hbm, q_hbm, v_hbm, do_hbm,
-    map_ref, wu_ref, inverse_ref, pdo_ref, gram_ref, qk_ref, rows_ref,
-    doc_ref, rate_ref, bias_ref, k_ref, hid_ref, wd_ref, wb_ref, q_ref, v_ref, do_ref, sems,
+    at_ref, _x_ref, _y_ref, _z_ref, doc_ref, rate_hbm, bias_hbm, k_hbm, hid_hbm, wd_hbm, wb_hbm, q_hbm, v_hbm, do_hbm,
+    map_ref, uhat_ref, what_ref, z0_ref, y_ref, gram_ref, qk_ref, rows_ref,
+    rate_ref, bias_ref, k_ref, hid_ref, wd_ref, wb_ref, q_ref, v_ref, do_ref, sems,
 ):
     pairs = (
         (hid_hbm, hid_ref), (wd_hbm, wd_ref), (wb_hbm, wb_ref), (rate_hbm, rate_ref), (bias_hbm, bias_ref),
-        (doc_hbm, doc_ref), (k_hbm, k_ref), (q_hbm, q_ref), (v_hbm, v_ref), (do_hbm, do_ref),
+        (k_hbm, k_ref), (q_hbm, q_ref), (v_hbm, v_ref), (do_hbm, do_ref),
     )
     copies = [pltpu.make_async_copy(a, b, sems.at[i]) for i, (a, b) in enumerate(pairs)]
     for copy in copies:
         copy.start()
     ii, jj = iotas()
+    copies[5].wait()
     copies[6].wait()
-    copies[7].wait()
     keys, _ = unit_rows(k_ref[...].astype(F32))
     queries, _ = unit_rows(q_ref[...].astype(F32))
     queries = queries * SCALE
@@ -101,7 +100,7 @@
     qk = mm(qs, ks, 1, 1)
     gram_ref[...] = gram
     qk_ref[...] = qk
-    for copy in copies[:6]:
+    for copy in copies[:5]:
         copy.wait()
     reset = doc_ref[0] - at_ref[0]
     reset = jnp.where(reset < 0, C, jnp.minimum(reset, C))
@@ -119,200 +118,163 @@
     rows_ref[8:10, :] = slope
     rows_ref[10:16, :] = jnp.broadcast_to(reset.astype(F32), (6, C))
     cols = rows_ref[0:8, :].T
+    copies[7].wait()
     copies[8].wait()
-    copies[9].wait()
     eye = jnp.where(ii == jj, 1.0, 0.0).astype(F32)
     both_heads = range(HEADS)
     gates = [gate_matrices(rows_ref, cols, h, ii, jj, reset) for h in both_heads]
-    coupling = [g[4] * jnp.where(ii > jj, g[1] * gram, 0.0) for g in gates]
+    inner = [jnp.where(ii > jj, g[1] * gram, 0.0) for g in gates]
+    coupling = [g[4] * i for g, i in zip(gates, inner)]
     inverse = [eye - jnp.where((ii & 1) * (ii - jj) == 1, c, 0.0) for c in coupling]
-    for level in range(1, 7):
-        bi, bj = ii >> level, jj >> level
-        here = (bi & 1) * (bi - bj) == 1
-        part = [split(jnp.where(here, c, 0.0)) for c in coupling]
+    for level in (1, 3, 5):
+        same = (ii >> (level + 2)) == (jj >> (level + 2))
+        between = jnp.logical_and(same, (ii >> level) > (jj >> level))
+        part = [split(jnp.where(between, c, 0.0)) for c in coupling]
         xs = [split(x) for x in inverse]
-        step = [split(mm(part[h], xs[h])) for h in both_heads]
-        inverse = [inverse[h] - mm(xs[h], step[h]) for h in both_heads]
+        links = [split(mm(xs[h], part[h])) for h in both_heads]
+        twice = [split(mm(p, p)) for p in links]
+        inverse = [inverse[h] - mm(links[h], xs[h]) for h in both_heads]
+        inverse = [inverse[h] + mm(twice[h], split(inverse[h])) for h in both_heads]
     xs = [split(x) for x in inverse]
     cotangent = [(do_ref[:, h * C : (h + 1) * C],) for h in both_heads]
     ps = [split(qk * g[1]) for g in gates]
-    right = [
-        split(g[4] * jnp.concatenate([g[2] * keys, v_ref[:, h * C : (h + 1) * C].astype(F32)], axis=1))
+    both = [
+        jnp.concatenate([g[2] * keys, v_ref[:, h * C : (h + 1) * C].astype(F32)], axis=1)
         for h, g in enumerate(gates)
     ]
-    wu = [mm(xs[h], right[h]) for h in both_heads]
-    wus = [split(w) for w in wu]
-    ml = [mm(split(gates[h][3] * keys), wus[h], 0, 0) for h in both_heads]
-    reach = [mm(ps[h], tuple(t[:, :C] for t in wus[h])) for h in both_heads]
+    right = [split(g[4] * b) for g, b in zip(gates, both)]
+    wu = [split(mm(xs[h], right[h])) for h in both_heads]
+    pdo = [mm(ps[h], cotangent[h], 0, 0) for h in both_heads]
+    keys_out = [g[3] * keys for g in gates]
+    ml = [mm(split(keys_out[h]), wu[h], 0, 0) for h in both_heads]
+    reach = [mm(ps[h], tuple(t[:, :C] for t in wu[h])) for h in both_heads]
+    sides = [split(jnp.concatenate([pdo[h], keys_out[h]], axis=1)) for h in both_heads]
+    zy = [mm(xs[h], sides[h], 0, 0) for h in both_heads]
+    hats = [both[h] - mm(split(inner[h]), wu[h]) for h in both_heads]
     effective = [split(gates[h][2] * queries - reach[h]) for h in both_heads]
     adjoint = [mm(effective[h], cotangent[h], 0, 0) for h in both_heads]
-    pdo = [mm(ps[h], cotangent[h], 0, 0) for h in both_heads]
     for h in both_heads:
-        inverse_ref[h] = inverse[h]
-        wu_ref[h] = wu[h]
-        pdo_ref[h] = pdo[h]
-        map_ref[h, 0:C, :] = ml[h][:, :C]
+        left = jnp.where(reset > C - 1, 1.0 - jnp.exp(gates[h][5]), 1.0)
+        map_ref[h, 0:C, :] = ml[h][:, :C] + eye * left
         map_ref[h, C : 2 * C, :] = ml[h][:, C:]
         map_ref[h, 2 * C : 3 * C, :] = adjoint[h]
-        total = jnp.where(reset > C - 1, jnp.maximum(gates[h][5], LOG_FLOOR), LOG_FLOOR)
-        map_ref[h, 3 * C :, :] = jnp.broadcast_to(total, (8, C))
-
-
-def own_rest(h, ii, jj, k_ref, v_ref, wu_ref, inverse_ref, pdo_ref, gram_ref, rows_ref, uhat_ref, what_ref, z0_ref, y_ref):
-    reset = rows_ref[10:11, 0:1].astype(jnp.int32)
-    keys, _ = unit_rows(k_ref[...].astype(F32))
-    _, decay, carry, weight, _, _ = gate_matrices(rows_ref, rows_ref[0:8, :].T, h, ii, jj, reset)
-    inner = jnp.where(ii > jj, decay * gram_ref[...], 0.0)
-    both = jnp.concatenate([carry * keys, v_ref[:, h * C : (h + 1) * C].astype(F32)], axis=1)
-    hats = both - mm(split(inner), split(wu_ref[h]))
-    what_ref[h] = hats[:, :C]
-    uhat_ref[h] = hats[:, C:]
-    sides = jnp.concatenate([pdo_ref[h], weight * keys], axis=1)
-    zy = mm(split(inverse_ref[h]), split(sides), 0, 0)
-    z0_ref[h] = zy[:, :C]
-    y_ref[h] = zy[:, C:]
+        what_ref[h], uhat_ref[h] = hats[h][:, :C], hats[h][:, C:]
+        z0_ref[h], y_ref[h] = zy[h][:, :C], zy[h][:, C:]
 
 
 def read_map(ref, *at):
-    m = ref[(*at, slice(0, C), slice(None))]
-    state = ref[(*at, slice(C, 2 * C), slice(None))]
-    adjoint = ref[(*at, slice(2 * C, 3 * C), slice(None))]
-    log = ref[(*at, slice(3 * C, 3 * C + 1), slice(0, 1))]
-    return m, state, adjoint, log
-
-
-def power_of_two(a):
-    largest = jnp.max(jnp.max(jnp.abs(a), axis=0, keepdims=True), axis=1, keepdims=True)
-    return jnp.floor(jnp.log2(jnp.maximum(largest, 1e-30)))
-
-
-def pack(out_ref, parts, log):
-    row = lax.broadcasted_iota(jnp.int32, (16, C), 0)
-    meta = jnp.zeros((16, C), F32)
-    for at, part in enumerate(parts):
-        power = power_of_two(part)
-        out_ref[at * C : (at + 1) * C, :] = part * jnp.exp2(13.0 - power)
-        meta = jnp.where(row == at, power, meta)
-    log = jnp.maximum(log, LOG_FLOOR)
-    quarters = jnp.floor(log * 4.0)
-    fine = log * 4.0 - quarters
-    coarse = jnp.floor(fine * 1024.0) * (1.0 / 1024.0)
-    meta = jnp.where(row == 3, quarters * 0.25, meta)
-    meta = jnp.where(row == 4, coarse, meta)
-    meta = jnp.where(row == 5, (fine - coarse) * 1024.0, meta)
-    out_ref[3 * C :, :] = meta
+    return tuple(ref[(*at, slice(i * C, (i + 1) * C), slice(None))] for i in range(3))
+
+
+def pack(out_ref, parts):
+    ii, jj = iotas()
+    bits = jnp.zeros((C, C), jnp.int32)
+    for at, part in enumerate(parts[1:]):
+        largest = jnp.max(jnp.max(jnp.abs(part), axis=0, keepdims=True), axis=1, keepdims=True)
+        power = jnp.floor(jnp.log2(jnp.maximum(largest, 1e-30)))
+        out_ref[(at + 1) * C : (at + 2) * C, :] = part * jnp.exp2(13.0 - power)
+        code = power.astype(jnp.int32) + 256
+        place = jj - 16 * at
+        bits = jnp.where(jnp.logical_and(place >= 0, place < 16), (code >> (place & 15)) & 1, bits)
+    n = parts[0] * 8192.0
+    diagonal = jnp.maximum(n, 2.0**-13) * (1 - 2 * bits).astype(F32)
+    out_ref[0:C, :] = jnp.where(ii == jj, diagonal, n)
 
 
 def unpack(ref, at):
-    meta = ref[at, 3 * C :, :]
-    scales = [jnp.exp2(meta[i : i + 1, 0:1] - 13.0) for i in range(3)]
-    parts = [ref[at, i * C : (i + 1) * C, :] * scales[i] for i in range(3)]
-    log = meta[3:4, 0:1] + 0.25 * (meta[4:5, 0:1] + meta[5:6, 0:1] * (1.0 / 1024.0))
-    return parts[0], parts[1], parts[2], log
+    ii, jj = iotas()
+    n = ref[at, 0:C, :]
+    head = jnp.logical_and(ii == jj, n < 0.0)[0:32, :]
+    place = jj[0:32, :]
+    weight = jnp.where(head, 1 << (place & 15), 0)
+    parts = []
+    for i in range(2):
+        code = jnp.where((place >> 4) == i, weight, 0).astype(F32)
+        code = jnp.sum(jnp.sum(code, axis=0, keepdims=True), axis=1, keepdims=True)
+        parts.append(ref[at, (i + 1) * C : (i + 2) * C, :] * jnp.exp2(code - (256.0 + 13.0)))
+    return jnp.where(ii == jj, jnp.abs(n), n) * (1.0 / 8192.0), *parts
 
 
 def pair_kernel(maps_ref, out_ref):
-    m0, l0, a0, c0 = read_map(maps_ref, 0)
-    m1, l1, a1, c1 = read_map(maps_ref, 1)
-    g0, g1 = jnp.exp(c0), jnp.exp(c1)
-    m0s, m1s = split(m0), split(m1)
-    forward = mm(m1s, tuple(jnp.concatenate([a, b], axis=1) for a, b in zip(m0s, split(l0))))
-    m = g1 * m0 + g0 * m1 - forward[:, :C]
-    state = g1 * l0 - forward[:, C:] + l1
-    adjoint = g0 * a1 - mm(m0s, split(a1), 0, 0) + a0
-    pack(out_ref, (m, state, adjoint), c0 + c1)
-
-
-def ring_kernel(
-    at_ref, maps_ref, k_ref, v_ref, wu_ref, inverse_ref, pdo_ref, gram_ref, rows_ref,
-    out_ref, near_ref, uhat_ref, what_ref, z0_ref, y_ref,
-):
+    n0, l0, a0 = read_map(maps_ref, 0)
+    n1, l1, a1 = read_map(maps_ref, 1)
+    n0s = split(n0)
+    forward = mm(split(n1), tuple(jnp.concatenate([a, b], axis=1) for a, b in zip(n0s, split(l0))))
+    backward = mm(n0s, split(a1), 0, 0)
+    pack(out_ref, (n0 + n1 - forward[:, :C], l0 + l1 - forward[:, C:], a0 + a1 - backward))
+
+
+def ring_kernel(at_ref, maps_ref, out_ref, near_ref):
     here = at_ref[0]
-    ii, jj = iotas()
-
-    fetch = functools.partial(unpack, maps_ref)
     zero = jnp.zeros((C, C), F32)
 
     @pl.when(here == 0)
     def _():
         near_ref[0:C, :] = zero
         near_ref[C : 2 * C, :] = zero
-        near_ref[4 * C : 4 * C + 8, :] = jnp.zeros((8, C), F32)
 
     @pl.when(here == NZ - 1)
     def _():
         near_ref[2 * C : 3 * C, :] = zero
         near_ref[3 * C : 4 * C, :] = zero
-        near_ref[4 * C + 8 :, :] = jnp.zeros((8, C), F32)
-
-    m, state, _, log = fetch(0)
-    m_back, _, adjoint, log_back = fetch(NZ - 1)
-    m_back = m_back.T
+
+    maps = [unpack(maps_ref, z) for z in range(NZ)]
+    n, state, _ = maps[0]
+    n_back, _, adjoint = maps[NZ - 1]
+    n_back = n_back.T
     for step in range(1, NZ):
         back = NZ - 1 - step
-        if step in (2, 5):
-            own_rest(
-                step // 4, ii, jj, k_ref, v_ref, wu_ref, inverse_ref, pdo_ref, gram_ref, rows_ref,
-                uhat_ref, what_ref, z0_ref, y_ref,
-            )
 
         @pl.when(here == step)
         def _():
-            near_ref[0:C, :] = m
+            near_ref[0:C, :] = n
             near_ref[C : 2 * C, :] = state
-            near_ref[4 * C : 4 * C + 8, :] = jnp.broadcast_to(log, (8, C))
 
         @pl.when(here == back)
         def _():
-            near_ref[2 * C : 3 * C, :] = m_back
+            near_ref[2 * C : 3 * C, :] = n_back
             near_ref[3 * C : 4 * C, :] = adjoint
-            near_ref[4 * C + 8 :, :] = jnp.broadcast_to(log_back, (8, C))
-
-        mz, lz, _, cz = fetch(step)
-        moved = mm(split(mz), split(jnp.concatenate([m, state], axis=1)))
-        gz, g = jnp.exp(cz), jnp.exp(log)
-        m, state = gz * m + g * mz - moved[:, :C], gz * state + lz - moved[:, C:]
-        log = log + cz
-        mz, _, az, cz = fetch(back)
-        mz = mz.T
-        moved = mm(split(mz), split(jnp.concatenate([m_back, adjoint], axis=1)))
-        gz, g = jnp.exp(cz), jnp.exp(log_back)
-        m_back, adjoint = gz * m_back + g * mz - moved[:, :C], gz * adjoint + az - moved[:, C:]
-        log_back = log_back + cz
-    pack(out_ref, (m, state, adjoint), log)
+
+        nz, lz, _ = maps[step]
+        ahead = jnp.concatenate([n, state], axis=1)
+        nb, _, az = maps[back]
+        nb = nb.T
+        behind = jnp.concatenate([n_back, adjoint], axis=1)
+        ahead = ahead - mm(split(nz), split(ahead))
+        behind = behind - mm(split(nb), split(behind))
+        n, state = ahead[:, :C] + nz, ahead[:, C:] + lz
+        n_back, adjoint = behind[:, :C] + nb, behind[:, C:] + az
+    pack(out_ref, (n, state, adjoint))
 
 
 def entry_kernel(at_ref, groups_ref, near_ref, maps_ref, out_ref, s_ref, a_ref):
     here = at_ref[0]
-    _, first, _, _ = unpack(groups_ref, 0)
-    _, _, last, _ = unpack(groups_ref, NX - 1)
-    s_ref[...] = jnp.where(here > 0, first, 0.0)
-    a_ref[...] = jnp.where(here < NX - 1, last, 0.0)
+    s_ref[...] = jnp.where(here > 0, unpack(groups_ref, 0)[1], 0.0)
+    a_ref[...] = jnp.where(here < NX - 1, unpack(groups_ref, NX - 1)[2], 0.0)
     for step in range(1, NX - 1):
         back = NX - 1 - step
 
         @pl.when(here > step)
         def _():
-            m, state, _, log = unpack(groups_ref, step)
+            n, state, _ = unpack(groups_ref, step)
             s = s_ref[...]
-            s_ref[...] = jnp.exp(log) * s - mm(split(m), split(s)) + state
+            s_ref[...] = s - mm(split(n), split(s)) + state
 
         @pl.when(here < back)
         def _():
-            m, _, adjoint, log = unpack(groups_ref, back)
+            n, _, adjoint = unpack(groups_ref, back)
             a = a_ref[...]
-            a_ref[...] = jnp.exp(log) * a - mm(split(m), split(a), 0, 0) + adjoint
+            a_ref[...] = a - mm(split(n), split(a), 0, 0) + adjoint
 
     s, a = s_ref[...], a_ref[...]
-    g_in, g_out = (jnp.exp(near_ref[4 * C + 8 * i : 4 * C + 8 * i + 1, 0:1]) for i in range(2))
-    s = g_in * s - mm(split(near_ref[0:C, :]), split(s)) + near_ref[C : 2 * C, :]
-    a = g_out * a - mm(split(near_ref[2 * C : 3 * C, :]), split(a)) + near_ref[3 * C : 4 * C, :]
+    s = s - mm(split(near_ref[0:C, :]), split(s)) + near_ref[C : 2 * C, :]
+    a = a - mm(split(near_ref[2 * C : 3 * C, :]), split(a)) + near_ref[3 * C : 4 * C, :]
     out_ref[0, 0:C, :] = s
     out_ref[1, C : 2 * C, :] = a
-    m, state, _, log = read_map(maps_ref, 0)
-    out_ref[1, 0:C, :] = jnp.exp(log) * s - mm(split(m), split(s)) + state
-    m, _, adjoint, log = read_map(maps_ref, 1)
-    out_ref[0, C : 2 * C, :] = jnp.exp(log) * a - mm(split(m), split(a), 0, 0) + adjoint
+    n, state, _ = read_map(maps_ref, 0)
+    out_ref[1, 0:C, :] = s - mm(split(n), split(s)) + state
+    n, _, adjoint = read_map(maps_ref, 1)
+    out_ref[0, C : 2 * C, :] = a - mm(split(n), split(a), 0, 0) + adjoint
 
 
 def grad_kernel(
@@ -411,7 +373,8 @@
     total = share_ref[mine]
     for z in range(1, NZ):
         total = total + share_ref[z * NY + mine]
-    power = power_of_two(total)
+    largest = jnp.max(jnp.max(jnp.abs(total), axis=0, keepdims=True), axis=1, keepdims=True)
+    power = jnp.floor(jnp.log2(jnp.maximum(largest, 1e-30)))
     out_ref[0:8, :] = total * jnp.exp2(13.0 - power)
     lane = lax.broadcasted_iota(jnp.int32, (1, C), 1) >> 5
     sums = own_ref[4:5, :]
@@ -475,14 +438,16 @@
 HBM = pl.BlockSpec(memory_space=pltpu.HBM)
 
 
-def call(kernel, scalars, arrays, outs, scratch=(), space=VMEM, small=0, flops=0, vmem=40 << 20):
+def call(kernel, scalars, arrays, outs, scratch=(), space=VMEM, small=0, flops=0):
+    if space is HBM:
+        arrays = tuple(pltpu.with_memory_space_constraint(a, pltpu.HBM) for a in arrays)
     return pl.pallas_call(
         kernel,
         out_shape=tuple(jax.ShapeDtypeStruct(s, t) for s, t in outs),
         in_specs=[SMEM] * len(scalars) + [space] * len(arrays),
         out_specs=tuple([VMEM] * (len(outs) - small) + [SMEM] * small),
         scratch_shapes=list(scratch),
-        compiler_params=pltpu.CompilerParams(vmem_limit_bytes=vmem),
+        compiler_params=pltpu.CompilerParams(vmem_limit_bytes=40 << 20),
         cost_estimate=pl.CostEstimate(flops=flops, bytes_accessed=1 << 20, transcendentals=0) if flops else None,
     )(*scalars, *arrays)
 
@@ -505,21 +470,12 @@
     at_x, at_y, at_z, first = (a[None] for a in (at_x, at_y, at_z, first))
     wd, wb = w_decay.T, w_beta.T
     square, heads, wide = (C, C), (HEADS, C, C), (C, HEADS * C)
-    maps, wu, inverse, pdo, gram, qk, rows = call(
+    maps, uhat, what, z0, y, gram, qk, rows = call(
         local_kernel,
-        (first,),
-        (doc_start, rate, bias, keys, hidden, wd, wb, queries, values, cotangent),
+        (first, at_x, at_y, at_z, doc_start),
+        (rate, bias, keys, hidden, wd, wb, queries, values, cotangent),
+        [((HEADS, MAP_ROWS, C), F32)] + [(heads, F32)] * 4 + [(square, F32)] * 2 + [((16, C), F32)],
         [
-            ((HEADS, MAP_ROWS, C), F32),
-            ((HEADS, C, 2 * C), F32),
-            (heads, F32),
-            (heads, F32),
-            (square, F32),
-            (square, F32),
-            ((16, C), F32),
-        ],
-        [
-            pltpu.SMEM((1,), jnp.int32),
             pltpu.SMEM((2,), F32),
             pltpu.SMEM((2,), F32),
             pltpu.VMEM(square, BF16),
@@ -529,19 +485,15 @@
             pltpu.VMEM(square, BF16),
             pltpu.VMEM(wide, BF16),
             pltpu.VMEM(wide, BF16),
-            pltpu.SemaphoreType.DMA((10,)),
+            pltpu.SemaphoreType.DMA((9,)),
         ],
         HBM,
-        vmem=FULL_VMEM,
     )
     maps = exchange(maps, "core")
-    (packed,) = call(pair_kernel, (), (maps,), [((PACKED_ROWS, C), F32)])
+    (packed,) = call(pair_kernel, (), (maps,), [((MAP_ROWS, C), F32)])
     ring = spread(packed, NZ, "z")
-    packed, near, uhat, what, z0, y = call(
-        ring_kernel,
-        (at_z,),
-        (ring, keys, values, wu, inverse, pdo, gram, rows),
-        [((PACKED_ROWS, C), F32), ((4 * C + 16, C), F32)] + [(heads, F32)] * 4,
+    packed, near = call(
+        ring_kernel, (at_z,), (ring,), [((MAP_ROWS, C), F32), ((4 * C, C), F32)]
     )
     groups = spread(packed, NX, "x")
     (ends,) = call(

time: 114 us -> 107 us (0.939)
  blocking collectives: 66.9 us -> 74.8 us
  waiting for transfers between devices: 16.3 us -> 10.1 us
  starting transfers between devices: 10.9 us -> 6.88 us
  Pallas kernels: 15.2 us -> 12.5 us
  local copies, waits for them, and re-layouts: 2.69 us -> 0.95 us
    all_to_all x4 -> x5, blocking collectives: 66.9 us -> 74.8 us  [exchange(): return lax.all_to_all(a, axes, 0, 0, tiled=True)]
    all_to_all x2 -> x1, waiting for transfers between devices: 16.3 us -> 10.1 us  [exchange(): return lax.all_to_all(a, axes, 0, 0, tiled=True)]
    all_to_all x2 -> x1, starting transfers between devices: 10.9 us -> 6.88 us  [exchange(): return lax.all_to_all(a, axes, 0, 0, tiled=True)]
    pallas_call x9, Pallas kernels: 15.2 us -> 12.5 us  [call(): pl.pallas_call(kernel, out_shape=tuple((jax.ShapeDtypeStruct(s, t) for s,...]
  transfers between devices with their start and end apart: 2 -> 1, of which waited for: 2 -> 1; matrix products, arithmetic and copies ran while one was open for 0% -> 0% of each run, Pallas kernels for 2% -> 2%
where the time goes in v3:
time: 107 us
  blocking collectives  74.8 us (70%)
  Pallas kernels  12.5 us (12%)
  waiting for transfers between devices  10.1 us (9%)
  starting transfers between devices  6.88 us (6%)
  between operations  1.43 us (1%)
    all_to_all x5, blocking collectives, exchange(): return lax.all_to_all(a, axes, 0, 0, tiled=True)  74.8 us
    pallas_call x9, Pallas kernels, call(): pl.pallas_call(kernel, out_shape=tuple((jax.ShapeDtypeStruct(s, t) for s,...  12.5 us
    all_to_all x1, waiting for transfers between devices, exchange(): return lax.all_to_all(a, axes, 0, 0, tiled=True)  10.1 us
    all_to_all x1, starting transfers between devices, exchange(): return lax.all_to_all(a, axes, 0, 0, tiled=True)  6.88 us
  transfers between devices with their start and end apart: 1, of which 1 were waited for; matrix products, arithmetic and copies ran while one was open for 0% of the time, Pallas kernels for 2%

profile of v3, /device:TPU:1, one launch (start us, length us, event | category | flops | bytes accessed | tf_op | source)
XLA Modules:
  0.0 106.9 jit_solution(16544351134478502228)
XLA Ops:
  1.3 4.5 %shard_map.161 = (f32[2,384,128]{2,1,0:T(8,128)S(1)}, f32[2,128,128]{2,1,0:T(8,128)S(1)}, f32[2,128,128]{2,1,0:T(8,128)S(1)}, f32[2,128,128]{2,1,0:T(8,128)S(1)}...) custom-call(s32[1]{0:T(128)} %bitcast.3.at_ref, ...), custom_call_target="tpu_custom_call" | custom-call | tf_op jit(solution)/shard_map/pallas_call | solution.py:444
  5.8 10.6 %all_to_all.30.maps_ref = f32[2,384,128]{2,1,0:T(8,128)S(1)} all-to-all(f32[2,384,128]{2,1,0:T(8,128)S(1)} %get-tuple-element.31), channel_id=1, replica_groups=mesh['x'=4,'z'=8,'core'=2,'dp'=8] {'core'}, dimensions={0} | all-to-all | bytes 786432 | tf_op jit(solution)/shard_map/all_to_all | solution.py:456
  16.4 0.3 shard_map.162
  16.7 0.1 broadcast_in_dim.25
  16.9 26.8 %all_to_all.31 = f16[8,384,128]{2,1,0:T(8,128)(2,1)S(1)} all-to-all(f16[8,384,128]{2,1,0:T(8,128)(2,1)S(1)} %broadcast_in_dim.25), channel_id=1, replica_groups=mesh['x'=4,'z'=8,'core'=2,'dp'=8] {'z'}, dimensions={0} | all-to-all | bytes 1572864 | tf_op jit(solution)/shard_map/all_to_all | solution.py:456
  43.6 0.1 convert_element_type.19.maps_ref
  43.8 2.1 %shard_map.163 = (f32[384,128]{1,0:T(8,128)S(1)}, f32[512,128]{1,0:T(8,128)S(1)}) custom-call(s32[1]{0:T(128)} %bitcast._z_ref.at_ref.at_z_ref, f32[8,384,128]{2,1,0:T(8,128)S(1)} %convert_element_type.19.maps_ref), custom_call_target="tpu_custom_call" | custom-call | tf_op jit(solution)/shard_map/pallas_call | solution.py:444
  45.9 0.1 broadcast_in_dim.26
  46.0 10.0 %all_to_all.32 = f16[4,384,128]{2,1,0:T(8,128)(2,1)S(1)} all-to-all(f16[4,384,128]{2,1,0:T(8,128)(2,1)S(1)} %broadcast_in_dim.26), channel_id=1, replica_groups=mesh['x'=4,'z'=8,'core'=2,'dp'=8] {'x'}, dimensions={0} | all-to-all | bytes 786432 | tf_op jit(solution)/shard_map/all_to_all | solution.py:456
  56.0 0.0 copy-start
  56.0 0.0 copy-start.1
  56.0 0.0 copy-start.2
  56.0 0.0 copy-start.4
  56.1 0.0 copy-start.5
  56.1 0.1 convert_element_type.21.groups_ref
  56.1 0.9 shard_map.164
  57.1 6.7 %all_to_all.33.ends_ref = f32[2,256,128]{2,1,0:T(8,128)S(1)} all-to-all(f32[2,256,128]{2,1,0:T(8,128)S(1)} %shard_map.164), channel_id=1, replica_groups=mesh['x'=4,'z'=8,'core'=2,'dp'=8] {'core'}, dimensions={0} | all-to-all | bytes 524288 | tf_op jit(solution)/shard_map/all_to_all | solution.py:456
  63.8 0.0 copy-done
  63.8 0.0 copy-done.1
  63.8 0.0 copy-done.2
  63.8 0.0 copy-done.3
  63.8 0.0 copy-done.4
  63.8 0.0 copy-done.5
  63.9 1.8 %shard_map.165 = (bf16[128,256]{1,0:T(8,128)(2,1)}, f32[128,128]{1,0:T(8,128)S(1)}, f32[128,128]{1,0:T(8,128)S(1)}, f32[128,128]{1,0:T(8,128)S(1)}, f32[128,128]...) custom-call(s32[1]{0:T(128)} %bitcast._z_ref.at_ref.at_z_ref, s32[1]{0:T(128)} %bitcast.1._y_ref.at_y_ref, ...), custom_call_target="tpu_custom_call" | custom-call | tf_op jit(solution)/shard_map/pallas_call | solution.py:444
  65.7 20.7 %all_to_all.34.share_ref = f32[64,8,128]{2,1,0:T(8,128)S(1)} all-to-all(f32[64,8,128]{2,1,0:T(8,128)S(1)} %get-tuple-element.48), channel_id=1, replica_groups=mesh['x'=4,'z'=8,'core'=2,'dp'=8] {'z','dp'}, dimensions={0} | all-to-all | bytes 524288 | tf_op jit(solution)/shard_map/all_to_all | solution.py:456
  86.4 0.1 shard_map.168
  86.5 0.8 broadcast_in_dim.27
  87.2 6.9 %all-to-all-start.5 = ((f16[64,16,128]{2,1,0:T(8,128)(2,1)}), f16[64,16,128]{2,1,0:T(8,128)(2,1)S(1)}, u32[]{:S(2)}, u32[]{:S(2)}) async-start(f16[64,16,128]{2,1,0:T(8,128)(2,1)} %broadcast_in_dim.27), calls=%async_computation.5 | async-start | bytes 524288 | tf_op jit(solution)/shard_map/all_to_all | solution.py:456
  94.1 1.0 shard_map.166
  95.1 0.9 shard_map.167
  96.1 10.1 %all-to-all-done.5 = f16[64,16,128]{2,1,0:T(8,128)(2,1)S(1)} async-done(((f16[64,16,128]{2,1,0:T(8,128)(2,1)}), f16[64,16,128]{2,1,0:T(8,128)(2,1)S(1)}, u32[]{:S(2)}, u32[]{:S(2)}) %all-to-all-start.5) | async-done | bytes 262176 | tf_op jit(solution)/shard_map/all_to_all | solution.py:456
  106.2 0.7 shard_map.169
  (5 shorter events, 0.1 us)
Async XLA Ops:
  56.0 7.8 %copy-start = (bf16[128,2048]{1,0:T(8,128)(2,1)S(1)}, bf16[128,2048]{1,0:T(8,128)(2,1)}, u32[]{:S(2)}) copy-start(bf16[128,2048]{1,0:T(8,128)(2,1)} %hid_ref.1) | copy-start | bytes 1572868
  56.0 7.8 %copy-start.1 = (bf16[128,256]{1,0:T(8,128)(2,1)S(1)}, bf16[128,256]{1,0:T(8,128)(2,1)}, u32[]{:S(2)}) copy-start(bf16[128,256]{1,0:T(8,128)(2,1)} %do_ref.1) | copy-start | bytes 196612
  56.0 7.8 %copy-start.2 = (bf16[128,128]{1,0:T(8,128)(2,1)S(1)}, bf16[128,128]{1,0:T(8,128)(2,1)}, u32[]{:S(2)}) copy-start(bf16[128,128]{1,0:T(8,128)(2,1)} %k_ref.3) | copy-start | bytes 98308
  56.0 7.8 %copy-start.3 = (bf16[128,128]{1,0:T(8,128)(2,1)S(1)}, bf16[128,128]{1,0:T(8,128)(2,1)}, u32[]{:S(2)}) copy-start(bf16[128,128]{1,0:T(8,128)(2,1)} %q_ref.3) | copy-start | bytes 98308
  56.0 7.8 %copy-start.4 = (bf16[2048,2]{0,1:T(2,128)(2,1)S(1)}, bf16[2048,2]{0,1:T(2,128)(2,1)}, u32[]{:S(2)}) copy-start(bf16[2048,2]{0,1:T(2,128)(2,1)} %param.15) | copy-start | bytes 24580
  56.1 7.8 %copy-start.5 = (bf16[2048,2]{0,1:T(2,128)(2,1)S(1)}, bf16[2048,2]{0,1:T(2,128)(2,1)}, u32[]{:S(2)}) copy-start(bf16[2048,2]{0,1:T(2,128)(2,1)} %param.16) | copy-start | bytes 24580
  87.2 18.9 %all-to-all-start.5 = ((f16[64,16,128]{2,1,0:T(8,128)(2,1)}), f16[64,16,128]{2,1,0:T(8,128)(2,1)S(1)}, u32[]{:S(2)}, u32[]{:S(2)}) async-start(f16[64,16,128]{2,1,0:T(8,128)(2,1)} %broadcast_in_dim.27), calls=%async_computation.5 | async-start | bytes 524288 | tf_op jit(solution)/shard_map/all_to_all | solution.py:456

commit v4 on v3

--- a/solution.py
+++ b/solution.py
@@ -15,6 +15,7 @@
 HEADS = 2
 D = 2048
 NX, NZ, NC, NY = 4, 8, 2, 8
+PARTS = D // NX // C
 CTX = ("x", "z", "core")
 norm_epsilon = 1e-06
 SCALE = C**-0.5
@@ -166,29 +167,30 @@
     return tuple(ref[(*at, slice(i * C, (i + 1) * C), slice(None))] for i in range(3))
 
 
-def pack(out_ref, parts):
+def scaled(part):
+    largest = jnp.max(jnp.max(jnp.abs(part), axis=0, keepdims=True), axis=1, keepdims=True)
+    power = jnp.floor(jnp.log2(jnp.maximum(largest, 1e-30)))
+    return part * jnp.exp2(13.0 - power), power
+
+
+def coded(n, powers):
     ii, jj = iotas()
     bits = jnp.zeros((C, C), jnp.int32)
-    for at, part in enumerate(parts[1:]):
-        largest = jnp.max(jnp.max(jnp.abs(part), axis=0, keepdims=True), axis=1, keepdims=True)
-        power = jnp.floor(jnp.log2(jnp.maximum(largest, 1e-30)))
-        out_ref[(at + 1) * C : (at + 2) * C, :] = part * jnp.exp2(13.0 - power)
+    for at, power in enumerate(powers):
         code = power.astype(jnp.int32) + 256
-        place = jj - 16 * at
-        bits = jnp.where(jnp.logical_and(place >= 0, place < 16), (code >> (place & 15)) & 1, bits)
-    n = parts[0] * 8192.0
-    diagonal = jnp.maximum(n, 2.0**-13) * (1 - 2 * bits).astype(F32)
-    out_ref[0:C, :] = jnp.where(ii == jj, diagonal, n)
-
-
-def unpack(ref, at):
+        bits = jnp.where((jj >> 4) == at, (code >> (jj & 15)) & 1, bits)
+    n = n * 8192.0
+    return jnp.where(ii == jj, jnp.maximum(n, 2.0**-13) * (1 - 2 * bits).astype(F32), n)
+
+
+def unpack(ref, at, count):
     ii, jj = iotas()
     n = ref[at, 0:C, :]
     head = jnp.logical_and(ii == jj, n < 0.0)[0:32, :]
     place = jj[0:32, :]
     weight = jnp.where(head, 1 << (place & 15), 0)
     parts = []
-    for i in range(2):
+    for i in range(count):
         code = jnp.where((place >> 4) == i, weight, 0).astype(F32)
         code = jnp.sum(jnp.sum(code, axis=0, keepdims=True), axis=1, keepdims=True)
         parts.append(ref[at, (i + 1) * C : (i + 2) * C, :] * jnp.exp2(code - (256.0 + 13.0)))
@@ -201,10 +203,12 @@
     n0s = split(n0)
     forward = mm(split(n1), tuple(jnp.concatenate([a, b], axis=1) for a, b in zip(n0s, split(l0))))
     backward = mm(n0s, split(a1), 0, 0)
-    pack(out_ref, (n0 + n1 - forward[:, :C], l0 + l1 - forward[:, C:], a0 + a1 - backward))
-
-
-def ring_kernel(at_ref, maps_ref, out_ref, near_ref):
+    out_ref[C : 2 * C, :], state_power = scaled(l0 + l1 - forward[:, C:])
+    out_ref[2 * C : 3 * C, :], adjoint_power = scaled(a0 + a1 - backward)
+    out_ref[0:C, :] = coded(n0 + n1 - forward[:, :C], (state_power, adjoint_power))
+
+
+def ring_kernel(at_x_ref, at_ref, maps_ref, out_ref, near_ref):
     here = at_ref[0]
     zero = jnp.zeros((C, C), F32)
 
@@ -218,7 +222,7 @@
         near_ref[2 * C : 3 * C, :] = zero
         near_ref[3 * C : 4 * C, :] = zero
 
-    maps = [unpack(maps_ref, z) for z in range(NZ)]
+    maps = [unpack(maps_ref, z, 2) for z in range(NZ)]
     n, state, _ = maps[0]
     n_back, _, adjoint = maps[NZ - 1]
     n_back = n_back.T
@@ -244,25 +248,38 @@
         behind = behind - mm(split(nb), split(behind))
         n, state = ahead[:, :C] + nz, ahead[:, C:] + lz
         n_back, adjoint = behind[:, :C] + nb, behind[:, C:] + az
-    pack(out_ref, (n, state, adjoint))
+    state, state_power = scaled(state)
+    adjoint, adjoint_power = scaled(adjoint)
+    onward, backward = coded(n, (state_power,)), coded(n, (adjoint_power,))
+    for x in range(NX):
+
+        @pl.when(x > at_x_ref[0])
+        def _():
+            out_ref[x, 0:C, :] = onward
+            out_ref[x, C : 2 * C, :] = state
+
+        @pl.when(x <= at_x_ref[0])
+        def _():
+            out_ref[x, 0:C, :] = backward
+            out_ref[x, C : 2 * C, :] = adjoint
 
 
 def entry_kernel(at_ref, groups_ref, near_ref, maps_ref, out_ref, s_ref, a_ref):
     here = at_ref[0]
-    s_ref[...] = jnp.where(here > 0, unpack(groups_ref, 0)[1], 0.0)
-    a_ref[...] = jnp.where(here < NX - 1, unpack(groups_ref, NX - 1)[2], 0.0)
+    s_ref[...] = jnp.where(here > 0, unpack(groups_ref, 0, 1)[1], 0.0)
+    a_ref[...] = jnp.where(here < NX - 1, unpack(groups_ref, NX - 1, 1)[1], 0.0)
     for step in range(1, NX - 1):
         back = NX - 1 - step
 
         @pl.when(here > step)
         def _():
-            n, state, _ = unpack(groups_ref, step)
+            n, state = unpack(groups_ref, step, 1)
             s = s_ref[...]
             s_ref[...] = s - mm(split(n), split(s)) + state
 
         @pl.when(here < back)
         def _():
-            n, _, adjoint = unpack(groups_ref, back)
+            n, adjoint = unpack(groups_ref, back, 1)
             a = a_ref[...]
             a_ref[...] = a - mm(split(n), split(a), 0, 0) + adjoint
 
@@ -278,20 +295,19 @@
 
 
 def grad_kernel(
-    at_z_ref, at_y_ref,
+    at_x_ref, at_y_ref,
     ends_ref, hid_ref, k_ref, q_ref, do_ref, wd_ref, wb_ref,
     uhat_ref, what_ref, z0_ref, y_ref, gram_ref, qk_ref, rows_ref,
     dv_ref, e_ref, f_ref, query_side_ref, key_side_ref, share_ref, own_ref,
-    sums_ref,
+    sums_ref, terms_ref,
 ):
-    here, mine = at_z_ref[0], at_y_ref[0]
+    here, mine = at_x_ref[0], at_y_ref[0]
     ii, jj = iotas()
     reset = rows_ref[10:11, 0:1].astype(jnp.int32)
     cols = rows_ref[0:8, :].T
     keys, _ = unit_rows(k_ref[...].astype(F32))
     queries = unit_rows(q_ref[...].astype(F32))[0] * SCALE
     gram, qk = gram_ref[...], qk_ref[...]
-    ones = jnp.ones((8, C), BF16)
     lower = (ii >= jj).astype(BF16)
     both_heads = range(HEADS)
     gates = [gate_matrices(rows_ref, cols, h, ii, jj, reset) for h in both_heads]
@@ -314,18 +330,21 @@
     key_side = [from_keys[h] - gates[h][2] * through[h] for h in both_heads]
     h_mat = [e[h] * qk + f[h] * gram for h in both_heads]
     by_row = [
-        split3(h_mat[h] + queries * from_out[h] + keys * (key_side[h] - 2.0 * from_keys[h]))
+        h_mat[h] + queries * from_out[h] + keys * (key_side[h] - 2.0 * from_keys[h])
         for h in both_heads
     ]
-    zu = [split3(z[h] * uhat[h]) for h in both_heads]
-    dc = [sum(dot(ones, t, 1, 1) for t in by_row[h]) for h in both_heads]
-    db = [sum(dot(ones, t, 1, 1) for t in zu[h]) for h in both_heads]
+    zu = [z[h] * uhat[h] for h in both_heads]
+    by_lane = jnp.zeros((C, C), F32)
+    for i, t in enumerate((*by_row, *zu)):
+        by_lane = jnp.where(jj == i, jnp.sum(t, axis=1, keepdims=True), by_lane)
+    by_lane = by_lane.T
+    dc, db = by_lane[0:2, :], by_lane[2:4, :]
     for h in both_heads:
         carry = gates[h][2]
         ends = keys * from_keys[h] + carry[C - 1 : C, :] * states[h] * adjoints[h]
         tail = jnp.sum(jnp.sum(ends, axis=0, keepdims=True), axis=1, keepdims=True)
-        sums_ref[h : h + 1, :] = dc[h][0:1, :] - jnp.sum(h_mat[h], axis=0, keepdims=True)
-        sums_ref[2 + h : 3 + h, :] = db[h][0:1, :]
+        sums_ref[h : h + 1, :] = dc[h : h + 1, :] - jnp.sum(h_mat[h], axis=0, keepdims=True)
+        sums_ref[2 + h : 3 + h, :] = db[h : h + 1, :]
         sums_ref[4 + h : 5 + h, :] = jnp.broadcast_to(tail, (1, C))
         dv_ref[:, h * C : (h + 1) * C] = bz[h].astype(BF16)
     e_ref[...] = e[0] + e[1]
@@ -340,19 +359,22 @@
     own_ref[2:4, :] = db * beta * (1.0 - beta)
     own_ref[4:6, :] = jnp.broadcast_to(jnp.sum(dg * log_decay, axis=1, keepdims=True), (2, C))
     own_ref[6:8, :] = jnp.broadcast_to(jnp.sum(dz, axis=1, keepdims=True), (2, C))
-    grad = sum(dot(t, hid_ref[...], 1, 0) for t in split3(own_ref[0:4, :]))
+    for i, t in enumerate(split3(own_ref[0:4, :])):
+        terms_ref[4 * i : 4 * i + 4, :] = t.astype(F32)
+    terms_ref[12:16, :] = jnp.zeros((4, C), F32)
+    grad = dot(terms_ref[...].astype(BF16), hid_ref[...], 1, 0)
+    grad = grad[0:4, :] + grad[4:8, :] + grad[8:12, :]
     share_ref[...] = jnp.zeros_like(share_ref)
-    after = lax.rem(here + 1, NZ)
     for other in range(NY):
         share_ref[here * NY + other, 0:4, :] = own_ref[0:4, :]
         for half in range(2):
             at = slice((2 * other + half) * C, (2 * other + half + 1) * C)
-            share_ref[after * NY + other, 4 * half : 4 * half + 2, :] = wd_ref[:, at].astype(F32)
-            share_ref[after * NY + other, 4 * half + 2 : 4 * half + 4, :] = wb_ref[:, at].astype(F32)
-    for z in range(NZ):
-        for half in range(2):
-            at = slice((2 * z + half) * C, (2 * z + half + 1) * C)
-            share_ref[z * NY + mine, 4 * half : 4 * half + 4, :] = grad[:, at]
+            share_ref[here * NY + other, 4 * half + 4 : 4 * half + 6, :] = wd_ref[:, at].astype(F32)
+            share_ref[here * NY + other, 4 * half + 6 : 4 * half + 8, :] = wb_ref[:, at].astype(F32)
+    for x in range(NX):
+        for i in range(PARTS):
+            at = slice((PARTS * x + i) * C, (PARTS * x + i + 1) * C)
+            share_ref[x * NY + mine, 4 * i : 4 * i + 4, :] = grad[:, at]
 
 
 def vector_kernel(k_ref, q_ref, e_ref, f_ref, query_side_ref, key_side_ref, dq_ref, dk_ref):
@@ -371,28 +393,26 @@
 def sum_kernel(at_y_ref, share_ref, own_ref, out_ref):
     mine = at_y_ref[0]
     total = share_ref[mine]
-    for z in range(1, NZ):
-        total = total + share_ref[z * NY + mine]
-    largest = jnp.max(jnp.max(jnp.abs(total), axis=0, keepdims=True), axis=1, keepdims=True)
-    power = jnp.floor(jnp.log2(jnp.maximum(largest, 1e-30)))
-    out_ref[0:8, :] = total * jnp.exp2(13.0 - power)
+    for x in range(1, NX):
+        total = total + share_ref[x * NY + mine]
+    total, power = scaled(total)
     lane = lax.broadcasted_iota(jnp.int32, (1, C), 1) >> 5
     sums = own_ref[4:5, :]
     for i in range(1, 4):
         sums = jnp.where(lane == i, own_ref[4 + i : 5 + i, :], sums)
     powers = jnp.floor(jnp.log2(jnp.maximum(jnp.abs(sums), 1e-30)))
-    scaled = sums * jnp.exp2(-powers)
-    high = jnp.floor(scaled * 256.0) * (1.0 / 256.0)
-    out_ref[8:9, :] = jnp.broadcast_to(power, (1, C))
-    out_ref[9:10, :] = powers
-    out_ref[10:11, :] = high
-    out_ref[11:12, :] = (scaled - high) * 256.0
-    out_ref[12:16, :] = jnp.zeros((4, C), F32)
-
-
-def hidden_kernel(at_z_ref, at_y_ref, share_ref, own_ref, wd_ref, wb_ref, hidden_ref, lg_ref, w_ref):
-    here, mine = at_z_ref[0], at_y_ref[0]
-    before = lax.rem(here + NZ - 1, NZ)
+    fractions = sums * jnp.exp2(-powers)
+    high = jnp.floor(fractions * 256.0) * (1.0 / 256.0)
+    for i in range(PARTS):
+        out_ref[:, i * C : (i + 1) * C] = total[4 * i : 4 * i + 4, :]
+    out_ref[0:1, PARTS * C :] = jnp.broadcast_to(power, (1, C))
+    out_ref[1:2, PARTS * C :] = powers
+    out_ref[2:3, PARTS * C :] = high
+    out_ref[3:4, PARTS * C :] = (fractions - high) * 256.0
+
+
+def hidden_kernel(at_x_ref, at_y_ref, share_ref, own_ref, wd_ref, wb_ref, hidden_ref, lg_ref, w_ref):
+    here, mine = at_x_ref[0], at_y_ref[0]
     for y in range(NY):
         rows = slice(4 * y, 4 * y + 4)
 
@@ -405,8 +425,8 @@
         @pl.when(mine != y)
         def _():
             lg_ref[rows, :] = share_ref[here * NY + y, 0:4, :]
-            w_ref[rows, 0:C] = share_ref[before * NY + y, 0:4, :]
-            w_ref[rows, C : 2 * C] = share_ref[before * NY + y, 4:8, :]
+            w_ref[rows, 0:C] = share_ref[here * NY + y, 4:8, :]
+            w_ref[rows, C : 2 * C] = share_ref[here * NY + y, 8:12, :]
 
     weights = w_ref[...].astype(BF16)
     hidden = sum(dot(t, weights, 0, 0) for t in split3(lg_ref[...]))
@@ -416,17 +436,17 @@
 def finish_kernel(parts_ref, wd_ref, wb_ref, rate_ref, bias_ref):
     per = NZ * NC
     sums = jnp.zeros((1, C), F32)
-    for z in range(NZ):
-        total = jnp.zeros((8, C), F32)
-        for x in range(NX):
-            for core in range(NC):
-                part = parts_ref[x * per + z * NC + core]
-                total = total + part[0:8, :] * jnp.exp2(part[8:9, :] - 13.0)
-                sums = sums + (part[10:11, :] + part[11:12, :] * (1.0 / 256.0)) * jnp.exp2(part[9:10, :])
-        for half in range(2):
-            at = slice((2 * z + half) * C, (2 * z + half + 1) * C)
-            wd_ref[:, at] = total[4 * half : 4 * half + 2, :]
-            wb_ref[:, at] = total[4 * half + 2 : 4 * half + 4, :]
+    for x in range(NX):
+        totals = [jnp.zeros((4, C), F32)] * PARTS
+        for at in range(x * per, (x + 1) * per):
+            meta = parts_ref[at, :, PARTS * C :]
+            scale = jnp.exp2(meta[0:1, :] - 13.0)
+            totals = [t + parts_ref[at, :, i * C : (i + 1) * C] * scale for i, t in enumerate(totals)]
+            sums = sums + (meta[2:3, :] + meta[3:4, :] * (1.0 / 256.0)) * jnp.exp2(meta[1:2, :])
+        for i, total in enumerate(totals):
+            at = slice((PARTS * x + i) * C, (PARTS * x + i + 1) * C)
+            wd_ref[:, at] = total[0:2, :]
+            wb_ref[:, at] = total[2:4, :]
     lane = lax.broadcasted_iota(jnp.int32, (1, C), 1)
     for i in range(2):
         rate_ref[i] = jnp.sum(jnp.where(lane == 32 * i, sums, 0.0))
@@ -492,10 +512,10 @@
     maps = exchange(maps, "core")
     (packed,) = call(pair_kernel, (), (maps,), [((MAP_ROWS, C), F32)])
     ring = spread(packed, NZ, "z")
-    packed, near = call(
-        ring_kernel, (at_z,), (ring,), [((MAP_ROWS, C), F32), ((4 * C, C), F32)]
-    )
-    groups = spread(packed, NX, "x")
+    groups, near = call(
+        ring_kernel, (at_x, at_z), (ring,), [((NX, 2 * C, C), F32), ((4 * C, C), F32)]
+    )
+    groups = exchange(groups.astype(F16), "x").astype(F32)
     (ends,) = call(
         entry_kernel,
         (at_x,),
@@ -506,12 +526,12 @@
     ends = exchange(ends, "core")
     dv, e, f, query_side, key_side, share, own = call(
         grad_kernel,
-        (at_z, at_y),
+        (at_x, at_y),
         (ends, hidden, keys, queries, cotangent, wd, wb, uhat, what, z0, y, gram, qk, rows),
-        [(wide, BF16)] + [(square, F32)] * 4 + [((NZ * NY, 8, C), F32), ((8, C), F32)],
-        [pltpu.VMEM((8, C), F32)],
-    )
-    share = exchange(share, ("z", "dp"))
+        [(wide, BF16)] + [(square, F32)] * 4 + [((NX * NY, 4 * PARTS, C), F32), ((8, C), F32)],
+        [pltpu.VMEM((8, C), F32), pltpu.VMEM((16, C), F32)],
+    )
+    share = exchange(share, ("x", "dp"))
     dq, dk = call(
         vector_kernel,
         (),
@@ -519,11 +539,11 @@
         [(square, BF16), (square, BF16)],
         flops=1 << 28,
     )
-    (sums,) = call(sum_kernel, (at_y,), (share, own), [((16, C), F32)])
+    (sums,) = call(sum_kernel, (at_y,), (share, own), [((4, (PARTS + 1) * C), F32)])
     parts = spread(sums, NX * NZ * NC, CTX)
     (hidden_grad,) = call(
         hidden_kernel,
-        (at_z, at_y),
+        (at_x, at_y),
         (share, own, wd, wb),
         [(wide, BF16)],
         [pltpu.VMEM((4 * NY, C), F32), pltpu.VMEM((4 * NY, 2 * C), F32)],

time: 107 us -> 105 us (0.981)
  blocking collectives: 74.8 us -> 70.8 us
  waiting for transfers between devices: 10.1 us -> 11.4 us
    all_to_all x5, blocking collectives: 74.8 us -> 70.8 us  [exchange(): return lax.all_to_all(a, axes, 0, 0, tiled=True)]
    all_to_all x1, waiting for transfers between devices: 10.1 us -> 11.4 us  [exchange(): return lax.all_to_all(a, axes, 0, 0, tiled=True)]
where the time goes in v4:
time: 105 us
  blocking collectives  70.8 us (67%)
  Pallas kernels  12.4 us (12%)
  waiting for transfers between devices  11.4 us (11%)
  starting transfers between devices  7.75 us (7%)
  between operations  1.45 us (1%)
    all_to_all x5, blocking collectives, exchange(): return lax.all_to_all(a, axes, 0, 0, tiled=True)  70.8 us
    pallas_call x9, Pallas kernels, call(): pl.pallas_call(kernel, out_shape=tuple((jax.ShapeDtypeStruct(s, t) for s,...  12.4 us
    all_to_all x1, waiting for transfers between devices, exchange(): return lax.all_to_all(a, axes, 0, 0, tiled=True)  11.4 us
    all_to_all x1, starting transfers between devices, exchange(): return lax.all_to_all(a, axes, 0, 0, tiled=True)  7.75 us
  transfers between devices with their start and end apart: 1, of which 1 were waited for; matrix products, arithmetic and copies ran while one was open for 0% of the time, Pallas kernels for 2%

profile of v4, /device:TPU:1, one launch (start us, length us, event | category | flops | bytes accessed | tf_op | source)
XLA Modules:
  0.0 105.1 jit_solution(5387750534231360997)
XLA Ops:
  1.3 4.5 %shard_map.161 = (f32[2,384,128]{2,1,0:T(8,128)S(1)}, f32[2,128,128]{2,1,0:T(8,128)S(1)}, f32[2,128,128]{2,1,0:T(8,128)S(1)}, f32[2,128,128]{2,1,0:T(8,128)S(1)}...) custom-call(s32[1]{0:T(128)} %bitcast.3.at_ref, ...), custom_call_target="tpu_custom_call" | custom-call | tf_op jit(solution)/shard_map/pallas_call | solution.py:464
  5.8 10.6 %all_to_all.30.maps_ref = f32[2,384,128]{2,1,0:T(8,128)S(1)} all-to-all(f32[2,384,128]{2,1,0:T(8,128)S(1)} %get-tuple-element.31), channel_id=1, replica_groups=mesh['x'=4,'z'=8,'core'=2,'dp'=8] {'core'}, dimensions={0} | all-to-all | bytes 786432 | tf_op jit(solution)/shard_map/all_to_all | solution.py:476
  16.4 0.3 shard_map.162
  16.7 0.1 broadcast_in_dim.22
  16.9 26.8 %all_to_all.31 = f16[8,384,128]{2,1,0:T(8,128)(2,1)S(1)} all-to-all(f16[8,384,128]{2,1,0:T(8,128)(2,1)S(1)} %broadcast_in_dim.22), channel_id=1, replica_groups=mesh['x'=4,'z'=8,'core'=2,'dp'=8] {'z'}, dimensions={0} | all-to-all | bytes 1572864 | tf_op jit(solution)/shard_map/all_to_all | solution.py:476
  43.6 0.1 convert_element_type.19.maps_ref
  43.8 2.2 %shard_map.163 = (f32[4,256,128]{2,1,0:T(8,128)S(1)}, f32[512,128]{1,0:T(8,128)S(1)}) custom-call(s32[1]{0:T(128)} %bitcast._x_ref.at_x_ref.at_ref, s32[1]{0:T(128)} %bitcast.2._z_ref.at_ref, f32[8,384,128]{2,1,0:T(8,128)S(1)} %convert_element_type.19.maps_ref), custom_call_target="tpu_custom_call" | custom-call | tf_op jit(solution)/shard_map/pallas_call | solution.py:464
  46.0 0.0 copy-start
  46.0 0.0 copy-start.1
  46.0 0.0 copy-start.2
  46.1 0.0 copy-start.3
  46.1 0.0 copy-start.4
  46.1 0.0 copy-start.5
  46.1 9.5 %all_to_all.32 = f16[4,256,128]{2,1,0:T(8,128)(2,1)S(1)} all-to-all(f16[4,256,128]{2,1,0:T(8,128)(2,1)S(1)} %convert_element_type.20), channel_id=1, replica_groups=mesh['x'=4,'z'=8,'core'=2,'dp'=8] {'x'}, dimensions={0} | all-to-all | bytes 524288 | tf_op jit(solution)/shard_map/all_to_all | solution.py:476
  55.6 0.9 shard_map.164
  56.5 6.7 %all_to_all.33.ends_ref = f32[2,256,128]{2,1,0:T(8,128)S(1)} all-to-all(f32[2,256,128]{2,1,0:T(8,128)S(1)} %shard_map.164), channel_id=1, replica_groups=mesh['x'=4,'z'=8,'core'=2,'dp'=8] {'core'}, dimensions={0} | all-to-all | bytes 524288 | tf_op jit(solution)/shard_map/all_to_all | solution.py:476
  63.3 0.0 copy-done
  63.3 0.0 copy-done.1
  63.3 0.0 copy-done.2
  63.3 0.0 copy-done.3
  63.3 0.0 copy-done.4
  63.3 0.0 copy-done.5
  63.3 1.6 %shard_map.165 = (bf16[128,256]{1,0:T(8,128)(2,1)}, f32[128,128]{1,0:T(8,128)S(1)}, f32[128,128]{1,0:T(8,128)S(1)}, f32[128,128]{1,0:T(8,128)S(1)}, f32[128,128]...) custom-call(s32[1]{0:T(128)} %bitcast._x_ref.at_x_ref.at_ref, s32[1]{0:T(128)} %bitcast.1._y_ref.at_y_ref, ...), custom_call_target="tpu_custom_call" | custom-call | tf_op jit(solution)/shard_map/pallas_call | solution.py:464
  64.9 17.2 %all_to_all.34.share_ref = f32[32,16,128]{2,1,0:T(8,128)S(1)} all-to-all(f32[32,16,128]{2,1,0:T(8,128)S(1)} %get-tuple-element.48), channel_id=1, replica_groups=mesh['x'=4,'z'=8,'core'=2,'dp'=8] {'x','dp'}, dimensions={0} | all-to-all | bytes 524288 | tf_op jit(solution)/shard_map/all_to_all | solution.py:476
  82.1 0.1 shard_map.168
  82.2 0.8 broadcast_in_dim.23
  83.0 7.8 %all-to-all-start.5 = ((f16[64,4,640]{2,1,0:T(4,128)(2,1)}), f16[64,4,640]{2,1,0:T(4,128)(2,1)S(1)}, u32[]{:S(2)}, u32[]{:S(2)}) async-start(f16[64,4,640]{2,1,0:T(4,128)(2,1)} %broadcast_in_dim.23), calls=%async_computation.5 | async-start | bytes 655360 | tf_op jit(solution)/shard_map/all_to_all | solution.py:476
  90.8 1.0 shard_map.166
  91.8 0.9 shard_map.167
  92.7 11.4 %all-to-all-done.5 = f16[64,4,640]{2,1,0:T(4,128)(2,1)S(1)} async-done(((f16[64,4,640]{2,1,0:T(4,128)(2,1)}), f16[64,4,640]{2,1,0:T(4,128)(2,1)S(1)}, u32[]{:S(2)}, u32[]{:S(2)}) %all-to-all-start.5) | async-done | bytes 327712 | tf_op jit(solution)/shard_map/all_to_all | solution.py:476
  104.2 0.1 convert_element_type.23.parts_ref
  104.3 0.8 shard_map.169
  (4 shorter events, 0.1 us)
Async XLA Ops:
  46.0 17.3 %copy-start = (bf16[128,2048]{1,0:T(8,128)(2,1)S(1)}, bf16[128,2048]{1,0:T(8,128)(2,1)}, u32[]{:S(2)}) copy-start(bf16[128,2048]{1,0:T(8,128)(2,1)} %hid_ref.1) | copy-start | bytes 1572868
  46.0 17.3 %copy-start.1 = (bf16[128,256]{1,0:T(8,128)(2,1)S(1)}, bf16[128,256]{1,0:T(8,128)(2,1)}, u32[]{:S(2)}) copy-start(bf16[128,256]{1,0:T(8,128)(2,1)} %do_ref.1) | copy-start | bytes 196612
  46.0 17.3 %copy-start.2 = (bf16[128,128]{1,0:T(8,128)(2,1)S(1)}, bf16[128,128]{1,0:T(8,128)(2,1)}, u32[]{:S(2)}) copy-start(bf16[128,128]{1,0:T(8,128)(2,1)} %k_ref.3) | copy-start | bytes 98308
  46.1 17.2 %copy-start.3 = (bf16[128,128]{1,0:T(8,128)(2,1)S(1)}, bf16[128,128]{1,0:T(8,128)(2,1)}, u32[]{:S(2)}) copy-start(bf16[128,128]{1,0:T(8,128)(2,1)} %q_ref.3) | copy-start | bytes 98308
  46.1 17.2 %copy-start.4 = (bf16[2048,2]{0,1:T(2,128)(2,1)S(1)}, bf16[2048,2]{0,1:T(2,128)(2,1)}, u32[]{:S(2)}) copy-start(bf16[2048,2]{0,1:T(2,128)(2,1)} %param.15) | copy-start | bytes 24580
  46.1 17.2 %copy-start.5 = (bf16[2048,2]{0,1:T(2,128)(2,1)S(1)}, bf16[2048,2]{0,1:T(2,128)(2,1)}, u32[]{:S(2)}) copy-start(bf16[2048,2]{0,1:T(2,128)(2,1)} %param.16) | copy-start | bytes 24580
  83.0 21.1 %all-to-all-start.5 = ((f16[64,4,640]{2,1,0:T(4,128)(2,1)}), f16[64,4,640]{2,1,0:T(4,128)(2,1)S(1)}, u32[]{:S(2)}, u32[]{:S(2)}) async-start(f16[64,4,640]{2,1,0:T(4,128)(2,1)} %broadcast_in_dim.23), calls=%async_computation.5 | async-start | bytes 655360 | tf_op jit(solution)/shard_map/all_to_all | solution.py:476

commit v5 on v4

--- a/solution.py
+++ b/solution.py
@@ -295,13 +295,13 @@
 
 
 def grad_kernel(
-    at_x_ref, at_y_ref,
+    at_y_ref,
     ends_ref, hid_ref, k_ref, q_ref, do_ref, wd_ref, wb_ref,
     uhat_ref, what_ref, z0_ref, y_ref, gram_ref, qk_ref, rows_ref,
-    dv_ref, e_ref, f_ref, query_side_ref, key_side_ref, share_ref, own_ref,
+    dv_ref, e_ref, f_ref, query_side_ref, key_side_ref, share_ref, own_ref, send_ref, keep_ref,
     sums_ref, terms_ref,
 ):
-    here, mine = at_x_ref[0], at_y_ref[0]
+    mine = at_y_ref[0]
     ii, jj = iotas()
     reset = rows_ref[10:11, 0:1].astype(jnp.int32)
     cols = rows_ref[0:8, :].T
@@ -364,17 +364,87 @@
     terms_ref[12:16, :] = jnp.zeros((4, C), F32)
     grad = dot(terms_ref[...].astype(BF16), hid_ref[...], 1, 0)
     grad = grad[0:4, :] + grad[4:8, :] + grad[8:12, :]
-    share_ref[...] = jnp.zeros_like(share_ref)
-    for other in range(NY):
-        share_ref[here * NY + other, 0:4, :] = own_ref[0:4, :]
-        for half in range(2):
-            at = slice((2 * other + half) * C, (2 * other + half + 1) * C)
-            share_ref[here * NY + other, 4 * half + 4 : 4 * half + 6, :] = wd_ref[:, at].astype(F32)
-            share_ref[here * NY + other, 4 * half + 6 : 4 * half + 8, :] = wb_ref[:, at].astype(F32)
     for x in range(NX):
         for i in range(PARTS):
             at = slice((PARTS * x + i) * C, (PARTS * x + i + 1) * C)
-            share_ref[x * NY + mine, 4 * i : 4 * i + 4, :] = grad[:, at]
+            share_ref[x, 4 * i : 4 * i + 4, :] = grad[:, at]
+    send_ref[0:4, :] = own_ref[0:4, :]
+    send_ref[4:8, :] = own_ref[0:4, :]
+    for other in range(NY):
+
+        at = other % 4
+
+        @pl.when(mine // 4 == other // 4)
+        def _():
+            keep_ref[at] = weight_rows(wd_ref, wb_ref, other)
+
+        @pl.when(mine // 4 != other // 4)
+        def _():
+            send_ref[8 + 8 * at : 16 + 8 * at, :] = weight_rows(wd_ref, wb_ref, other)
+
+
+def weight_rows(wd_ref, wb_ref, place):
+    return jnp.concatenate(
+        [
+            jnp.concatenate([ref[:, (2 * place + half) * C : (2 * place + half + 1) * C] for ref in (wd_ref, wb_ref)], axis=0)
+            for half in range(2)
+        ],
+        axis=0,
+    ).astype(F32)
+
+
+def second_kernel(at_y_ref, got_ref, sent_ref, keep_ref, send_ref, kept_ref):
+    bit = (at_y_ref[0] >> 1) & 1
+    send_ref[0:4, :] = sent_ref[0:4, :]
+    send_ref[4:8, :] = got_ref[0:4, :]
+    for high in range(2):
+        for low in range(2):
+            place = 2 * high + low
+            pair = (keep_ref[place], got_ref[8 + 8 * place : 16 + 8 * place, :])
+            for source, rows in enumerate(pair):
+
+                at = 2 * source + low
+
+                @pl.when(bit == high)
+                def _():
+                    kept_ref[at] = rows
+
+                @pl.when(bit != high)
+                def _():
+                    send_ref[8 + 8 * at : 16 + 8 * at, :] = rows
+
+
+def third_kernel(at_y_ref, got_ref, sent_ref, keep_ref, send_ref, kept_ref):
+    bit = at_y_ref[0] & 1
+    send_ref[0:8, :] = sent_ref[0:8, :]
+    send_ref[8:16, :] = got_ref[0:8, :]
+    for source in range(4):
+        for low in range(2):
+            at = 2 * (source % 2) + low
+            rows = keep_ref[at] if source < 2 else got_ref[8 + 8 * at : 16 + 8 * at, :]
+
+            @pl.when(bit == low)
+            def _():
+                kept_ref[source] = rows
+
+            @pl.when(bit != low)
+            def _():
+                send_ref[16 + 8 * source : 24 + 8 * source, :] = rows
+
+
+def hidden_kernel(got_ref, sent_ref, keep_ref, hidden_ref, w_ref):
+    for source in range(NY):
+        for half in range(2):
+            lanes, at = slice(half * C, (half + 1) * C), slice(4 * half, 4 * half + 4)
+            if source < 4:
+                rows = keep_ref[source, at, :]
+            else:
+                rows = got_ref[16 + 8 * (source - 4) + 4 * half : 20 + 8 * (source - 4) + 4 * half, :]
+            w_ref[4 * source : 4 * source + 4, lanes] = rows
+    logit_rows = jnp.concatenate([sent_ref[0:16, :], got_ref[0:16, :]], axis=0)
+    weights = w_ref[...].astype(BF16)
+    hidden = sum(dot(t, weights, 0, 0) for t in split3(logit_rows))
+    hidden_ref[...] = hidden.astype(BF16)
 
 
 def vector_kernel(k_ref, q_ref, e_ref, f_ref, query_side_ref, key_side_ref, dq_ref, dk_ref):
@@ -390,11 +460,10 @@
     dk_ref[...] = (dk * key_root).astype(BF16)
 
 
-def sum_kernel(at_y_ref, share_ref, own_ref, out_ref):
-    mine = at_y_ref[0]
-    total = share_ref[mine]
+def sum_kernel(share_ref, own_ref, _send_ref, out_ref):
+    total = share_ref[0]
     for x in range(1, NX):
-        total = total + share_ref[x * NY + mine]
+        total = total + share_ref[x]
     total, power = scaled(total)
     lane = lax.broadcasted_iota(jnp.int32, (1, C), 1) >> 5
     sums = own_ref[4:5, :]
@@ -409,28 +478,6 @@
     out_ref[1:2, PARTS * C :] = powers
     out_ref[2:3, PARTS * C :] = high
     out_ref[3:4, PARTS * C :] = (fractions - high) * 256.0
-
-
-def hidden_kernel(at_x_ref, at_y_ref, share_ref, own_ref, wd_ref, wb_ref, hidden_ref, lg_ref, w_ref):
-    here, mine = at_x_ref[0], at_y_ref[0]
-    for y in range(NY):
-        rows = slice(4 * y, 4 * y + 4)
-
-        @pl.when(mine == y)
-        def _():
-            lg_ref[rows, :] = own_ref[0:4, :]
-            w_ref[4 * y : 4 * y + 2, :] = wd_ref[:, 2 * y * C : 2 * (y + 1) * C].astype(F32)
-            w_ref[4 * y + 2 : 4 * y + 4, :] = wb_ref[:, 2 * y * C : 2 * (y + 1) * C].astype(F32)
-
-        @pl.when(mine != y)
-        def _():
-            lg_ref[rows, :] = share_ref[here * NY + y, 0:4, :]
-            w_ref[rows, 0:C] = share_ref[here * NY + y, 4:8, :]
-            w_ref[rows, C : 2 * C] = share_ref[here * NY + y, 8:12, :]
-
-    weights = w_ref[...].astype(BF16)
-    hidden = sum(dot(t, weights, 0, 0) for t in split3(lg_ref[...]))
-    hidden_ref[...] = hidden.astype(BF16)
 
 
 def finish_kernel(parts_ref, wd_ref, wb_ref, rate_ref, bias_ref):
@@ -479,6 +526,10 @@
 def spread(a, count, axes):
     a = jnp.broadcast_to(a.astype(F16), (count, *a.shape))
     return exchange(a, axes).astype(F32)
+
+
+def swap(a, bit):
+    return lax.ppermute(a, "dp", [(i, i ^ bit) for i in range(NY)])
 
 
 def on_device(hidden, queries, keys, values, cotangent, w_decay, w_beta, rate, bias, doc_start):
@@ -524,14 +575,21 @@
         [pltpu.VMEM(square, F32), pltpu.VMEM(square, F32)],
     )
     ends = exchange(ends, "core")
-    dv, e, f, query_side, key_side, share, own = call(
+    dv, e, f, query_side, key_side, share, own, send, keep = call(
         grad_kernel,
-        (at_x, at_y),
+        (at_y,),
         (ends, hidden, keys, queries, cotangent, wd, wb, uhat, what, z0, y, gram, qk, rows),
-        [(wide, BF16)] + [(square, F32)] * 4 + [((NX * NY, 4 * PARTS, C), F32), ((8, C), F32)],
+        [(wide, BF16)]
+        + [(square, F32)] * 4
+        + [((NX, 4 * PARTS, C), F32), ((8, C), F32), ((40, C), F32), ((4, 8, C), F32)],
         [pltpu.VMEM((8, C), F32), pltpu.VMEM((16, C), F32)],
     )
-    share = exchange(share, ("x", "dp"))
+    got = swap(send, 4)
+    share = exchange(share, "x")
+    send, keep = call(second_kernel, (at_y,), (got, send, keep), [((40, C), F32), ((4, 8, C), F32)])
+    got = swap(send, 2)
+    (sums,) = call(sum_kernel, (), (share, own, send), [((4, (PARTS + 1) * C), F32)])
+    parts = spread(sums, NX * NZ * NC, CTX)
     dq, dk = call(
         vector_kernel,
         (),
@@ -539,14 +597,14 @@
         [(square, BF16), (square, BF16)],
         flops=1 << 28,
     )
-    (sums,) = call(sum_kernel, (at_y,), (share, own), [((4, (PARTS + 1) * C), F32)])
-    parts = spread(sums, NX * NZ * NC, CTX)
+    send, keep = call(third_kernel, (at_y,), (got, send, keep), [((48, C), F32), ((4, 8, C), F32)])
+    got = swap(send, 1)
     (hidden_grad,) = call(
         hidden_kernel,
-        (at_x, at_y),
-        (share, own, wd, wb),
+        (),
+        (got, send, keep),
         [(wide, BF16)],
-        [pltpu.VMEM((4 * NY, C), F32), pltpu.VMEM((4 * NY, 2 * C), F32)],
+        [pltpu.VMEM((4 * NY, 2 * C), F32)],
         flops=1 << 28,
     )
     wd_grad, wb_grad, rate_grad, bias_grad = call(

time: 105 us -> 99.5 us (0.948)
  blocking collectives: 70.8 us -> 53.6 us
  starting transfers between devices: 7.75 us -> 24.8 us
  waiting for transfers between devices: 11.4 us -> 5.06 us
    all_to_all x5 -> x4, blocking collectives: 70.8 us -> 53.6 us  [exchange(): return lax.all_to_all(a, axes, 0, 0, tiled=True)]
    ppermute x0 -> x3, starting transfers between devices: none -> 14.9 us  [swap(): return lax.ppermute(a, 'dp', [(i, i ^ bit) for i in range(NY)])]
    all_to_all x1 -> x2, waiting for transfers between devices: 11.4 us -> 1.77 us  [exchange(): return lax.all_to_all(a, axes, 0, 0, tiled=True)]
    ppermute x0 -> x3, waiting for transfers between devices: none -> 3.28 us  [swap(): return lax.ppermute(a, 'dp', [(i, i ^ bit) for i in range(NY)])]
    all_to_all x1 -> x2, starting transfers between devices: 7.75 us -> 9.89 us  [exchange(): return lax.all_to_all(a, axes, 0, 0, tiled=True)]
    pallas_call x9 -> x11, Pallas kernels: 12.4 us -> 12.8 us  [call(): pl.pallas_call(kernel, out_shape=tuple((jax.ShapeDtypeStruct(s, t) for s,...]
  transfers between devices with their start and end apart: 1 -> 5, of which waited for: 1 -> 4; matrix products, arithmetic and copies ran while one was open for 0% -> 0% of each run, Pallas kernels for 2% -> 2%
where the time goes in v5:
time: 99.5 us; the launch traced here: 99 us
  blocking collectives  53.6 us (54%)
  starting transfers between devices  24.8 us (25%)
  Pallas kernels  12.8 us (13%)
  waiting for transfers between devices  5.06 us (5%)
  between operations  1.51 us (2%)
    all_to_all x4, blocking collectives, exchange(): return lax.all_to_all(a, axes, 0, 0, tiled=True)  53.6 us
    ppermute x3, starting transfers between devices, swap(): return lax.ppermute(a, 'dp', [(i, i ^ bit) for i in range(NY)])  14.9 us
    pallas_call x11, Pallas kernels, call(): pl.pallas_call(kernel, out_shape=tuple((jax.ShapeDtypeStruct(s, t) for s,...  12.8 us
    all_to_all x2, starting transfers between devices, exchange(): return lax.all_to_all(a, axes, 0, 0, tiled=True)  9.89 us
    ppermute x3, waiting for transfers between devices, swap(): return lax.ppermute(a, 'dp', [(i, i ^ bit) for i in range(NY)])  3.28 us
  transfers between devices with their start and end apart: 5, of which 4 were waited for; matrix products, arithmetic and copies ran while one was open for 0% of the time, Pallas kernels for 2%

profile of v5, /device:TPU:1, one launch (start us, length us, event | category | flops | bytes accessed | tf_op | source)
XLA Modules:
  0.0 99.0 jit_solution(16236355007939068673)
XLA Ops:
  1.3 4.5 %shard_map.161 = (f32[2,384,128]{2,1,0:T(8,128)S(1)}, f32[2,128,128]{2,1,0:T(8,128)S(1)}, f32[2,128,128]{2,1,0:T(8,128)S(1)}, f32[2,128,128]{2,1,0:T(8,128)S(1)}...) custom-call(s32[1]{0:T(128)} %bitcast.3.at_ref, ...), custom_call_target="tpu_custom_call" | custom-call | tf_op jit(solution)/shard_map/pallas_call | solution.py:511
  5.8 10.6 %all_to_all.30.maps_ref = f32[2,384,128]{2,1,0:T(8,128)S(1)} all-to-all(f32[2,384,128]{2,1,0:T(8,128)S(1)} %get-tuple-element.37), channel_id=1, replica_groups=mesh['x'=4,'z'=8,'core'=2,'dp'=8] {'core'}, dimensions={0} | all-to-all | bytes 786432 | tf_op jit(solution)/shard_map/all_to_all | solution.py:523
  16.4 0.3 shard_map.162
  16.7 0.1 broadcast_in_dim.22
  16.9 26.8 %all_to_all.31 = f16[8,384,128]{2,1,0:T(8,128)(2,1)S(1)} all-to-all(f16[8,384,128]{2,1,0:T(8,128)(2,1)S(1)} %broadcast_in_dim.22), channel_id=1, replica_groups=mesh['x'=4,'z'=8,'core'=2,'dp'=8] {'z'}, dimensions={0} | all-to-all | bytes 1572864 | tf_op jit(solution)/shard_map/all_to_all | solution.py:523
  43.6 0.1 convert_element_type.19.maps_ref
  43.8 2.2 %shard_map.163 = (f32[4,256,128]{2,1,0:T(8,128)S(1)}, f32[512,128]{1,0:T(8,128)S(1)}) custom-call(s32[1]{0:T(128)} %bitcast.1._x_ref.at_x_ref.at_ref, s32[1]{0:T(128)} %bitcast.2._z_ref.at_ref, f32[8,384,128]{2,1,0:T(8,128)S(1)} %convert_element_type.19.maps_ref), custom_call_target="tpu_custom_call" | custom-call | tf_op jit(solution)/shard_map/pallas_call | solution.py:511
  46.0 0.0 copy-start
  46.0 0.0 copy-start.1
  46.0 0.0 copy-start.2
  46.1 0.0 copy-start.3
  46.1 0.0 copy-start.4
  46.1 0.0 copy-start.5
  46.1 9.5 %all_to_all.32 = f16[4,256,128]{2,1,0:T(8,128)(2,1)S(1)} all-to-all(f16[4,256,128]{2,1,0:T(8,128)(2,1)S(1)} %convert_element_type.20), channel_id=1, replica_groups=mesh['x'=4,'z'=8,'core'=2,'dp'=8] {'x'}, dimensions={0} | all-to-all | bytes 524288 | tf_op jit(solution)/shard_map/all_to_all | solution.py:523
  55.6 0.9 shard_map.164
  56.5 6.7 %all_to_all.33.ends_ref = f32[2,256,128]{2,1,0:T(8,128)S(1)} all-to-all(f32[2,256,128]{2,1,0:T(8,128)S(1)} %shard_map.164), channel_id=1, replica_groups=mesh['x'=4,'z'=8,'core'=2,'dp'=8] {'core'}, dimensions={0} | all-to-all | bytes 524288 | tf_op jit(solution)/shard_map/all_to_all | solution.py:523
  63.3 2.0 %shard_map.165 = (bf16[128,256]{1,0:T(8,128)(2,1)}, f32[128,128]{1,0:T(8,128)S(1)}, f32[128,128]{1,0:T(8,128)S(1)}, f32[128,128]{1,0:T(8,128)S(1)}, f32[128,128]...) custom-call(s32[1]{0:T(128)} %bitcast._y_ref.at_y_ref, ...), custom_call_target="tpu_custom_call" | custom-call | tf_op jit(solution)/shard_map/pallas_call | solution.py:511
  65.3 3.3 %all-to-all-start.4 = ((f32[4,16,128]{2,1,0:T(8,128)}), f32[4,16,128]{2,1,0:T(8,128)S(1)}, u32[]{:S(2)}, u32[]{:S(2)}) async-start(f32[4,16,128]{2,1,0:T(8,128)} %get-tuple-element.60), calls=%async_computation.4 | async-start | bytes 65536 | tf_op jit(solution)/shard_map/all_to_all | solution.py:523
  68.6 7.5 %collective-permute-start = (f32[40,128]{1,0:T(8,128)S(1)}, f32[40,128]{1,0:T(8,128)S(1)}, u32[]{:S(2)}, u32[]{:S(2)}) collective-permute-start(f32[40,128]{1,0:T(8,128)S(1)} %get-tuple-element.54.sent_ref), channel_id=1, source_target_pairs={{0,4},{1,5},{2,6},{3,7},{4,0},{5,1},{6,2},{7,3},{8,12},{9,13},{10,... | collective-permute-start | bytes 61448 | tf_op jit(solution)/shard_map/ppermute | solution.py:532
  76.0 1.2 %collective-permute-done.got_ref = f32[40,128]{1,0:T(8,128)S(1)} collective-permute-done((f32[40,128]{1,0:T(8,128)S(1)}, f32[40,128]{1,0:T(8,128)S(1)}, u32[]{:S(2)}, u32[]{:S(2)}) %collective-permute-start) | collective-permute-done | bytes 20512 | tf_op jit(solution)/shard_map/ppermute | solution.py:532
  77.2 0.1 shard_map.170
  77.3 0.8 broadcast_in_dim.23
  78.2 6.6 %all-to-all-start.5 = ((f16[64,4,640]{2,1,0:T(4,128)(2,1)}), f16[64,4,640]{2,1,0:T(4,128)(2,1)S(1)}, u32[]{:S(2)}, u32[]{:S(2)}) async-start(f16[64,4,640]{2,1,0:T(4,128)(2,1)} %broadcast_in_dim.23), calls=%async_computation.5 | async-start | bytes 655360 | tf_op jit(solution)/shard_map/all_to_all | solution.py:523
  84.8 4.2 %collective-permute-start.1 = (f32[40,128]{1,0:T(8,128)S(1)}, f32[40,128]{1,0:T(8,128)S(1)}, u32[]{:S(2)}, u32[]{:S(2)}) collective-permute-start(f32[40,128]{1,0:T(8,128)S(1)} %get-tuple-element.56.sent_ref._send_ref), channel_id=1, source_target_pairs={{0,2},{1,3},{2,0},{3,1},{4,6},{5,7},{6,4},{7,5},{8,10},{9,11},{10,... | collective-permute-start | bytes 61448 | tf_op jit(solution)/shard_map/ppermute | solution.py:532
  89.0 1.5 %collective-permute-done.1.got_ref = f32[40,128]{1,0:T(8,128)S(1)} collective-permute-done((f32[40,128]{1,0:T(8,128)S(1)}, f32[40,128]{1,0:T(8,128)S(1)}, u32[]{:S(2)}, u32[]{:S(2)}) %collective-permute-start.1) | collective-permute-done | bytes 20512 | tf_op jit(solution)/shard_map/ppermute | solution.py:532
  90.5 3.2 %collective-permute-start.2 = (f32[48,128]{1,0:T(8,128)S(1)}, f32[48,128]{1,0:T(8,128)S(1)}, u32[]{:S(2)}, u32[]{:S(2)}) collective-permute-start(f32[48,128]{1,0:T(8,128)S(1)} %get-tuple-element.58.sent_ref), channel_id=1, source_target_pairs={{0,1},{1,0},{2,3},{3,2},{4,5},{5,4},{6,7},{7,6},{8,9},{9,8},{10,11... | collective-permute-start | bytes 73736 | tf_op jit(solution)/shard_map/ppermute | solution.py:532
  93.8 1.0 %shard_map.166 = (bf16[128,128]{1,0:T(8,128)(2,1)}, bf16[128,128]{1,0:T(8,128)(2,1)}) custom-call(bf16[128,128]{1,0:T(8,128)(2,1)S(1)} %copy-done.2, bf16[128,128]{1,0:T(8,128)(2,1)S(1)} %copy-done.3, f32[128,128]{1,0:T(8,128)S(1)} %get-tuple-element.47.e_ref, f32[128,128]{1,0:T(8,128)S(1)} %get-tuple-element.48.f_ref, ...), custom_call_target="tpu_custom_call" | custom-call | flops 268435456 | bytes 1048576 | tf_op jit(solution)/shard_map/pallas_call | solution.py:511
  94.8 0.6 collective-permute-done.2.got_ref
  95.4 0.9 shard_map.169
  96.3 1.8 %all-to-all-done.5 = f16[64,4,640]{2,1,0:T(4,128)(2,1)S(1)} async-done(((f16[64,4,640]{2,1,0:T(4,128)(2,1)}), f16[64,4,640]{2,1,0:T(4,128)(2,1)S(1)}, u32[]{:S(2)}, u32[]{:S(2)}) %all-to-all-start.5) | async-done | bytes 327712 | tf_op jit(solution)/shard_map/all_to_all | solution.py:523
  98.0 0.1 convert_element_type.23.parts_ref
  98.2 0.8 shard_map.171
  (13 shorter events, 0.1 us)
Async XLA Ops:
  46.0 17.3 %copy-start = (bf16[128,2048]{1,0:T(8,128)(2,1)S(1)}, bf16[128,2048]{1,0:T(8,128)(2,1)}, u32[]{:S(2)}) copy-start(bf16[128,2048]{1,0:T(8,128)(2,1)} %hid_ref.1) | copy-start | bytes 1572868
  46.0 17.3 %copy-start.1 = (bf16[128,256]{1,0:T(8,128)(2,1)S(1)}, bf16[128,256]{1,0:T(8,128)(2,1)}, u32[]{:S(2)}) copy-start(bf16[128,256]{1,0:T(8,128)(2,1)} %do_ref.1) | copy-start | bytes 196612
  46.0 17.3 %copy-start.2 = (bf16[128,128]{1,0:T(8,128)(2,1)S(1)}, bf16[128,128]{1,0:T(8,128)(2,1)}, u32[]{:S(2)}) copy-start(bf16[128,128]{1,0:T(8,128)(2,1)} %k_ref.3) | copy-start | bytes 98308
  46.1 17.2 %copy-start.3 = (bf16[128,128]{1,0:T(8,128)(2,1)S(1)}, bf16[128,128]{1,0:T(8,128)(2,1)}, u32[]{:S(2)}) copy-start(bf16[128,128]{1,0:T(8,128)(2,1)} %q_ref.3) | copy-start | bytes 98308
  46.1 17.2 %copy-start.4 = (bf16[2048,2]{0,1:T(2,128)(2,1)S(1)}, bf16[2048,2]{0,1:T(2,128)(2,1)}, u32[]{:S(2)}) copy-start(bf16[2048,2]{0,1:T(2,128)(2,1)} %param.15) | copy-start | bytes 24580
  46.1 17.2 %copy-start.5 = (bf16[2048,2]{0,1:T(2,128)(2,1)S(1)}, bf16[2048,2]{0,1:T(2,128)(2,1)}, u32[]{:S(2)}) copy-start(bf16[2048,2]{0,1:T(2,128)(2,1)} %param.16) | copy-start | bytes 24580
  65.3 11.9 %all-to-all-start.4 = ((f32[4,16,128]{2,1,0:T(8,128)}), f32[4,16,128]{2,1,0:T(8,128)S(1)}, u32[]{:S(2)}, u32[]{:S(2)}) async-start(f32[4,16,128]{2,1,0:T(8,128)} %get-tuple-element.60), calls=%async_computation.4 | async-start | bytes 65536 | tf_op jit(solution)/shard_map/all_to_all | solution.py:523
  68.6 8.6 %collective-permute-start = (f32[40,128]{1,0:T(8,128)S(1)}, f32[40,128]{1,0:T(8,128)S(1)}, u32[]{:S(2)}, u32[]{:S(2)}) collective-permute-start(f32[40,128]{1,0:T(8,128)S(1)} %get-tuple-element.54.sent_ref), channel_id=1, source_target_pairs={{0,4},{1,5},{2,6},{3,7},{4,0},{5,1},{6,2},{7,3},{8,12},{9,13},{10,... | collective-permute-start | bytes 61448 | tf_op jit(solution)/shard_map/ppermute | solution.py:532
  78.2 19.9 %all-to-all-start.5 = ((f16[64,4,640]{2,1,0:T(4,128)(2,1)}), f16[64,4,640]{2,1,0:T(4,128)(2,1)S(1)}, u32[]{:S(2)}, u32[]{:S(2)}) async-start(f16[64,4,640]{2,1,0:T(4,128)(2,1)} %broadcast_in_dim.23), calls=%async_computation.5 | async-start | bytes 655360 | tf_op jit(solution)/shard_map/all_to_all | solution.py:523
  84.8 5.7 %collective-permute-start.1 = (f32[40,128]{1,0:T(8,128)S(1)}, f32[40,128]{1,0:T(8,128)S(1)}, u32[]{:S(2)}, u32[]{:S(2)}) collective-permute-start(f32[40,128]{1,0:T(8,128)S(1)} %get-tuple-element.56.sent_ref._send_ref), channel_id=1, source_target_pairs={{0,2},{1,3},{2,0},{3,1},{4,6},{5,7},{6,4},{7,5},{8,10},{9,11},{10,... | collective-permute-start | bytes 61448 | tf_op jit(solution)/shard_map/ppermute | solution.py:532
  90.5 4.9 %collective-permute-start.2 = (f32[48,128]{1,0:T(8,128)S(1)}, f32[48,128]{1,0:T(8,128)S(1)}, u32[]{:S(2)}, u32[]{:S(2)}) collective-permute-start(f32[48,128]{1,0:T(8,128)S(1)} %get-tuple-element.58.sent_ref), channel_id=1, source_target_pairs={{0,1},{1,0},{2,3},{3,2},{4,5},{5,4},{6,7},{7,6},{8,9},{9,8},{10,11... | collective-permute-start | bytes 73736 | tf_op jit(solution)/shard_map/ppermute | solution.py:532

commit v6 on v5

--- a/solution.py
+++ b/solution.py
@@ -80,7 +80,7 @@
 
 def local_kernel(
     at_ref, _x_ref, _y_ref, _z_ref, doc_ref, rate_hbm, bias_hbm, k_hbm, hid_hbm, wd_hbm, wb_hbm, q_hbm, v_hbm, do_hbm,
-    map_ref, uhat_ref, what_ref, z0_ref, y_ref, gram_ref, qk_ref, rows_ref,
+    map_ref, uhat_ref, what_ref, z0_ref, y_ref, gram_ref, qk_ref, rows_ref, weights_ref,
     rate_ref, bias_ref, k_ref, hid_ref, wd_ref, wb_ref, q_ref, v_ref, do_ref, sems,
 ):
     pairs = (
@@ -118,6 +118,11 @@
     rows_ref[6:8, :] = x
     rows_ref[8:10, :] = slope
     rows_ref[10:16, :] = jnp.broadcast_to(reset.astype(F32), (6, C))
+    for i, ref in enumerate((wd_ref, wb_ref)):
+        weights = ref[...].astype(F32)
+        for at in range(2 * NY):
+            first = 4 * (at % 2) + 2 * i
+            weights_ref[at // 2, first : first + 2, :] = weights[:, at * C : (at + 1) * C]
     cols = rows_ref[0:8, :].T
     copies[7].wait()
     copies[8].wait()
@@ -296,7 +301,7 @@
 
 def grad_kernel(
     at_y_ref,
-    ends_ref, hid_ref, k_ref, q_ref, do_ref, wd_ref, wb_ref,
+    ends_ref, hid_ref, k_ref, q_ref, do_ref, weights_ref,
     uhat_ref, what_ref, z0_ref, y_ref, gram_ref, qk_ref, rows_ref,
     dv_ref, e_ref, f_ref, query_side_ref, key_side_ref, share_ref, own_ref, send_ref, keep_ref,
     sums_ref, terms_ref,
@@ -370,31 +375,15 @@
             share_ref[x, 4 * i : 4 * i + 4, :] = grad[:, at]
     send_ref[0:4, :] = own_ref[0:4, :]
     send_ref[4:8, :] = own_ref[0:4, :]
-    for other in range(NY):
-
-        at = other % 4
-
-        @pl.when(mine // 4 == other // 4)
-        def _():
-            keep_ref[at] = weight_rows(wd_ref, wb_ref, other)
-
-        @pl.when(mine // 4 != other // 4)
-        def _():
-            send_ref[8 + 8 * at : 16 + 8 * at, :] = weight_rows(wd_ref, wb_ref, other)
-
-
-def weight_rows(wd_ref, wb_ref, place):
-    return jnp.concatenate(
-        [
-            jnp.concatenate([ref[:, (2 * place + half) * C : (2 * place + half + 1) * C] for ref in (wd_ref, wb_ref)], axis=0)
-            for half in range(2)
-        ],
-        axis=0,
-    ).astype(F32)
+    bit = mine & 1
+    for at in range(4):
+        pair = weights_ref[2 * at], weights_ref[2 * at + 1]
+        keep_ref[at] = jnp.where(bit == 0, pair[0], pair[1])
+        send_ref[8 + 8 * at : 16 + 8 * at, :] = jnp.where(bit == 0, pair[1], pair[0])
 
 
 def second_kernel(at_y_ref, got_ref, sent_ref, keep_ref, send_ref, kept_ref):
-    bit = (at_y_ref[0] >> 1) & 1
+    bit = (at_y_ref[0] >> 2) & 1
     send_ref[0:4, :] = sent_ref[0:4, :]
     send_ref[4:8, :] = got_ref[0:4, :]
     for high in range(2):
@@ -415,7 +404,7 @@
 
 
 def third_kernel(at_y_ref, got_ref, sent_ref, keep_ref, send_ref, kept_ref):
-    bit = at_y_ref[0] & 1
+    bit = (at_y_ref[0] >> 1) & 1
     send_ref[0:8, :] = sent_ref[0:8, :]
     send_ref[8:16, :] = got_ref[0:8, :]
     for source in range(4):
@@ -432,7 +421,7 @@
                 send_ref[16 + 8 * source : 24 + 8 * source, :] = rows
 
 
-def hidden_kernel(got_ref, sent_ref, keep_ref, hidden_ref, w_ref):
+def hidden_kernel(got_ref, sent_ref, keep_ref, _after_ref, hidden_ref, w_ref):
     for source in range(NY):
         for half in range(2):
             lanes, at = slice(half * C, (half + 1) * C), slice(4 * half, 4 * half + 4)
@@ -480,7 +469,8 @@
     out_ref[3:4, PARTS * C :] = (fractions - high) * 256.0
 
 
-def finish_kernel(parts_ref, wd_ref, wb_ref, rate_ref, bias_ref):
+def finish_kernel(parts_ref, wd_ref, wb_ref, after_ref, rate_ref, bias_ref):
+    after_ref[...] = jnp.zeros_like(after_ref)
     per = NZ * NC
     sums = jnp.zeros((1, C), F32)
     for x in range(NX):
@@ -541,11 +531,11 @@
     at_x, at_y, at_z, first = (a[None] for a in (at_x, at_y, at_z, first))
     wd, wb = w_decay.T, w_beta.T
     square, heads, wide = (C, C), (HEADS, C, C), (C, HEADS * C)
-    maps, uhat, what, z0, y, gram, qk, rows = call(
+    maps, uhat, what, z0, y, gram, qk, rows, weights = call(
         local_kernel,
         (first, at_x, at_y, at_z, doc_start),
         (rate, bias, keys, hidden, wd, wb, queries, values, cotangent),
-        [((HEADS, MAP_ROWS, C), F32)] + [(heads, F32)] * 4 + [(square, F32)] * 2 + [((16, C), F32)],
+        [((HEADS, MAP_ROWS, C), F32)] + [(heads, F32)] * 4 + [(square, F32)] * 2 + [((16, C), F32), ((NY, 8, C), F32)],
         [
             pltpu.SMEM((2,), F32),
             pltpu.SMEM((2,), F32),
@@ -578,16 +568,16 @@
     dv, e, f, query_side, key_side, share, own, send, keep = call(
         grad_kernel,
         (at_y,),
-        (ends, hidden, keys, queries, cotangent, wd, wb, uhat, what, z0, y, gram, qk, rows),
+        (ends, hidden, keys, queries, cotangent, weights, uhat, what, z0, y, gram, qk, rows),
         [(wide, BF16)]
         + [(square, F32)] * 4
         + [((NX, 4 * PARTS, C), F32), ((8, C), F32), ((40, C), F32), ((4, 8, C), F32)],
         [pltpu.VMEM((8, C), F32), pltpu.VMEM((16, C), F32)],
     )
-    got = swap(send, 4)
+    got = swap(send, 1)
     share = exchange(share, "x")
     send, keep = call(second_kernel, (at_y,), (got, send, keep), [((40, C), F32), ((4, 8, C), F32)])
-    got = swap(send, 2)
+    got = swap(send, 4)
     (sums,) = call(sum_kernel, (), (share, own, send), [((4, (PARTS + 1) * C), F32)])
     parts = spread(sums, NX * NZ * NC, CTX)
     dq, dk = call(
@@ -598,21 +588,21 @@
         flops=1 << 28,
     )
     send, keep = call(third_kernel, (at_y,), (got, send, keep), [((48, C), F32), ((4, 8, C), F32)])
-    got = swap(send, 1)
+    got = swap(send, 2)
+    wd_grad, wb_grad, after, rate_grad, bias_grad = call(
+        finish_kernel,
+        (),
+        (parts,),
+        [((2, D), F32), ((2, D), F32), ((8, C), F32), ((HEADS,), F32), ((HEADS,), F32)],
+        small=2,
+    )
     (hidden_grad,) = call(
         hidden_kernel,
         (),
-        (got, send, keep),
+        (got, send, keep, after),
         [(wide, BF16)],
         [pltpu.VMEM((4 * NY, 2 * C), F32)],
         flops=1 << 28,
-    )
-    wd_grad, wb_grad, rate_grad, bias_grad = call(
-        finish_kernel,
-        (),
-        (parts,),
-        [((2, D), F32), ((2, D), F32), ((HEADS,), F32), ((HEADS,), F32)],
-        small=2,
     )
     return (dq, dk, dv, hidden_grad, wd_grad.T, wb_grad.T, rate_grad, bias_grad)
 

time: 99.5 us -> 97.8 us (0.983)
  waiting for transfers between devices: 5.06 us -> 3.07 us
    all_to_all x2, waiting for transfers between devices: 1.77 us -> 0.01 us  [exchange(): return lax.all_to_all(a, axes, 0, 0, tiled=True)]
  transfers between devices with their start and end apart: 5 -> 5, of which waited for: 4 -> 2; matrix products, arithmetic and copies ran while one was open for 0% -> 0% of each run, Pallas kernels for 2% -> 2%
where the time goes in v6:
time: 97.8 us; the launch traced here: 96.8 us
  blocking collectives  53.6 us (55%)
  starting transfers between devices  24.7 us (25%)
  Pallas kernels  12.7 us (13%)
  waiting for transfers between devices  3.07 us (3%)
  between operations  1.49 us (2%)
    all_to_all x4, blocking collectives, exchange(): return lax.all_to_all(a, axes, 0, 0, tiled=True)  53.6 us
    ppermute x3, starting transfers between devices, swap(): return lax.ppermute(a, 'dp', [(i, i ^ bit) for i in range(NY)])  14.9 us
    pallas_call x11, Pallas kernels, call(): pl.pallas_call(kernel, out_shape=tuple((jax.ShapeDtypeStruct(s, t) for s,...  12.7 us
    all_to_all x2, starting transfers between devices, exchange(): return lax.all_to_all(a, axes, 0, 0, tiled=True)  9.8 us
    ppermute x3, waiting for transfers between devices, swap(): return lax.ppermute(a, 'dp', [(i, i ^ bit) for i in range(NY)])  3.06 us
  transfers between devices with their start and end apart: 5, of which 2 were waited for; matrix products, arithmetic and copies ran while one was open for 0% of the time, Pallas kernels for 2%

profile of v6, /device:TPU:1, one launch (start us, length us, event | category | flops | bytes accessed | tf_op | source)
XLA Modules:
  0.0 96.8 jit_solution(4654041513276394712)
XLA Ops:
  1.3 4.5 %shard_map.161 = (f32[2,384,128]{2,1,0:T(8,128)S(1)}, f32[2,128,128]{2,1,0:T(8,128)S(1)}, f32[2,128,128]{2,1,0:T(8,128)S(1)}, f32[2,128,128]{2,1,0:T(8,128)S(1)}...) custom-call(s32[1]{0:T(128)} %bitcast.3.at_ref, ...), custom_call_target="tpu_custom_call" | custom-call | tf_op jit(solution)/shard_map/pallas_call | solution.py:501
  5.8 10.6 %all_to_all.30.maps_ref = f32[2,384,128]{2,1,0:T(8,128)S(1)} all-to-all(f32[2,384,128]{2,1,0:T(8,128)S(1)} %get-tuple-element.39), channel_id=1, replica_groups=mesh['x'=4,'z'=8,'core'=2,'dp'=8] {'core'}, dimensions={0} | all-to-all | bytes 786432 | tf_op jit(solution)/shard_map/all_to_all | solution.py:513
  16.4 0.3 shard_map.162
  16.7 0.1 broadcast_in_dim.22
  16.9 26.8 %all_to_all.31 = f16[8,384,128]{2,1,0:T(8,128)(2,1)S(1)} all-to-all(f16[8,384,128]{2,1,0:T(8,128)(2,1)S(1)} %broadcast_in_dim.22), channel_id=1, replica_groups=mesh['x'=4,'z'=8,'core'=2,'dp'=8] {'z'}, dimensions={0} | all-to-all | bytes 1572864 | tf_op jit(solution)/shard_map/all_to_all | solution.py:513
  43.6 0.1 convert_element_type.19.maps_ref
  43.8 2.2 %shard_map.163 = (f32[4,256,128]{2,1,0:T(8,128)S(1)}, f32[512,128]{1,0:T(8,128)S(1)}) custom-call(s32[1]{0:T(128)} %bitcast.1._x_ref.at_x_ref.at_ref, s32[1]{0:T(128)} %bitcast.2._z_ref.at_ref, f32[8,384,128]{2,1,0:T(8,128)S(1)} %convert_element_type.19.maps_ref), custom_call_target="tpu_custom_call" | custom-call | tf_op jit(solution)/shard_map/pallas_call | solution.py:501
  46.0 0.0 copy-start
  46.0 0.0 copy-start.1
  46.0 0.0 copy-start.2
  46.1 0.0 copy-start.3
  46.1 9.5 %all_to_all.32 = f16[4,256,128]{2,1,0:T(8,128)(2,1)S(1)} all-to-all(f16[4,256,128]{2,1,0:T(8,128)(2,1)S(1)} %convert_element_type.20), channel_id=1, replica_groups=mesh['x'=4,'z'=8,'core'=2,'dp'=8] {'x'}, dimensions={0} | all-to-all | bytes 524288 | tf_op jit(solution)/shard_map/all_to_all | solution.py:513
  55.6 0.9 shard_map.164
  56.5 6.7 %all_to_all.33.ends_ref = f32[2,256,128]{2,1,0:T(8,128)S(1)} all-to-all(f32[2,256,128]{2,1,0:T(8,128)S(1)} %shard_map.164), channel_id=1, replica_groups=mesh['x'=4,'z'=8,'core'=2,'dp'=8] {'core'}, dimensions={0} | all-to-all | bytes 524288 | tf_op jit(solution)/shard_map/all_to_all | solution.py:513
  63.3 0.0 copy-done.2
  63.3 1.9 %shard_map.165 = (bf16[128,256]{1,0:T(8,128)(2,1)}, f32[128,128]{1,0:T(8,128)S(1)}, f32[128,128]{1,0:T(8,128)S(1)}, f32[128,128]{1,0:T(8,128)S(1)}, f32[128,128]...) custom-call(s32[1]{0:T(128)} %bitcast._y_ref.at_y_ref, ...), custom_call_target="tpu_custom_call" | custom-call | tf_op jit(solution)/shard_map/pallas_call | solution.py:501
  65.1 3.3 %all-to-all-start.4 = ((f32[4,16,128]{2,1,0:T(8,128)}), f32[4,16,128]{2,1,0:T(8,128)S(1)}, u32[]{:S(2)}, u32[]{:S(2)}) async-start(f32[4,16,128]{2,1,0:T(8,128)} %get-tuple-element.63), calls=%async_computation.4 | async-start | bytes 65536 | tf_op jit(solution)/shard_map/all_to_all | solution.py:513
  68.4 3.2 %collective-permute-start = (f32[40,128]{1,0:T(8,128)S(1)}, f32[40,128]{1,0:T(8,128)S(1)}, u32[]{:S(2)}, u32[]{:S(2)}) collective-permute-start(f32[40,128]{1,0:T(8,128)S(1)} %get-tuple-element.57.sent_ref), channel_id=1, source_target_pairs={{0,1},{1,0},{2,3},{3,2},{4,5},{5,4},{6,7},{7,6},{8,9},{9,8},{10,11... | collective-permute-start | bytes 61448 | tf_op jit(solution)/shard_map/ppermute | solution.py:522
  71.6 1.6 %collective-permute-done.got_ref = f32[40,128]{1,0:T(8,128)S(1)} collective-permute-done((f32[40,128]{1,0:T(8,128)S(1)}, f32[40,128]{1,0:T(8,128)S(1)}, u32[]{:S(2)}, u32[]{:S(2)}) %collective-permute-start) | collective-permute-done | bytes 20512 | tf_op jit(solution)/shard_map/ppermute | solution.py:522
  73.3 0.0 all-to-all-done.4.share_ref
  73.3 0.1 shard_map.169
  73.4 0.8 broadcast_in_dim.23
  74.2 6.5 %all-to-all-start.5 = ((f16[64,4,640]{2,1,0:T(4,128)(2,1)}), f16[64,4,640]{2,1,0:T(4,128)(2,1)S(1)}, u32[]{:S(2)}, u32[]{:S(2)}) async-start(f16[64,4,640]{2,1,0:T(4,128)(2,1)} %broadcast_in_dim.23), calls=%async_computation.5 | async-start | bytes 655360 | tf_op jit(solution)/shard_map/all_to_all | solution.py:513
  80.7 7.5 %collective-permute-start.1 = (f32[40,128]{1,0:T(8,128)S(1)}, f32[40,128]{1,0:T(8,128)S(1)}, u32[]{:S(2)}, u32[]{:S(2)}) collective-permute-start(f32[40,128]{1,0:T(8,128)S(1)} %get-tuple-element.59.sent_ref._send_ref), channel_id=1, source_target_pairs={{0,4},{1,5},{2,6},{3,7},{4,0},{5,1},{6,2},{7,3},{8,12},{9,13},{10,... | collective-permute-start | bytes 61448 | tf_op jit(solution)/shard_map/ppermute | solution.py:522
  88.2 1.5 %collective-permute-done.1.got_ref = f32[40,128]{1,0:T(8,128)S(1)} collective-permute-done((f32[40,128]{1,0:T(8,128)S(1)}, f32[40,128]{1,0:T(8,128)S(1)}, u32[]{:S(2)}, u32[]{:S(2)}) %collective-permute-start.1) | collective-permute-done | bytes 20512 | tf_op jit(solution)/shard_map/ppermute | solution.py:522
  89.7 4.2 %collective-permute-start.2 = (f32[48,128]{1,0:T(8,128)S(1)}, f32[48,128]{1,0:T(8,128)S(1)}, u32[]{:S(2)}, u32[]{:S(2)}) collective-permute-start(f32[48,128]{1,0:T(8,128)S(1)} %get-tuple-element.61.sent_ref), channel_id=1, source_target_pairs={{0,2},{1,3},{2,0},{3,1},{4,6},{5,7},{6,4},{7,5},{8,10},{9,11},{10,... | collective-permute-start | bytes 73736 | tf_op jit(solution)/shard_map/ppermute | solution.py:522
  93.9 1.0 %shard_map.166 = (bf16[128,128]{1,0:T(8,128)(2,1)}, bf16[128,128]{1,0:T(8,128)(2,1)}) custom-call(bf16[128,128]{1,0:T(8,128)(2,1)S(1)} %copy-done.2, bf16[128,128]{1,0:T(8,128)(2,1)S(1)} %copy-done.3, f32[128,128]{1,0:T(8,128)S(1)} %get-tuple-element.50.e_ref, f32[128,128]{1,0:T(8,128)S(1)} %get-tuple-element.51.f_ref, ...), custom_call_target="tpu_custom_call" | custom-call | flops 268435456 | bytes 1048576 | tf_op jit(solution)/shard_map/pallas_call | solution.py:501
  94.9 0.0 all-to-all-done.5
  94.9 0.1 convert_element_type.23.parts_ref
  95.0 0.8 shard_map.170
  95.9 0.0 collective-permute-done.2.got_ref
  95.9 0.9 shard_map.171
  (9 shorter events, 0.1 us)
Async XLA Ops:
  46.0 17.2 %copy-start = (bf16[128,2048]{1,0:T(8,128)(2,1)S(1)}, bf16[128,2048]{1,0:T(8,128)(2,1)}, u32[]{:S(2)}) copy-start(bf16[128,2048]{1,0:T(8,128)(2,1)} %hid_ref.1) | copy-start | bytes 1572868
  46.0 17.2 %copy-start.1 = (bf16[128,256]{1,0:T(8,128)(2,1)S(1)}, bf16[128,256]{1,0:T(8,128)(2,1)}, u32[]{:S(2)}) copy-start(bf16[128,256]{1,0:T(8,128)(2,1)} %do_ref.1) | copy-start | bytes 196612
  46.0 17.2 %copy-start.2 = (bf16[128,128]{1,0:T(8,128)(2,1)S(1)}, bf16[128,128]{1,0:T(8,128)(2,1)}, u32[]{:S(2)}) copy-start(bf16[128,128]{1,0:T(8,128)(2,1)} %k_ref.3) | copy-start | bytes 98308
  46.1 17.2 %copy-start.3 = (bf16[128,128]{1,0:T(8,128)(2,1)S(1)}, bf16[128,128]{1,0:T(8,128)(2,1)}, u32[]{:S(2)}) copy-start(bf16[128,128]{1,0:T(8,128)(2,1)} %q_ref.3) | copy-start | bytes 98308
  65.1 8.1 %all-to-all-start.4 = ((f32[4,16,128]{2,1,0:T(8,128)}), f32[4,16,128]{2,1,0:T(8,128)S(1)}, u32[]{:S(2)}, u32[]{:S(2)}) async-start(f32[4,16,128]{2,1,0:T(8,128)} %get-tuple-element.63), calls=%async_computation.4 | async-start | bytes 65536 | tf_op jit(solution)/shard_map/all_to_all | solution.py:513
  68.4 4.8 %collective-permute-start = (f32[40,128]{1,0:T(8,128)S(1)}, f32[40,128]{1,0:T(8,128)S(1)}, u32[]{:S(2)}, u32[]{:S(2)}) collective-permute-start(f32[40,128]{1,0:T(8,128)S(1)} %get-tuple-element.57.sent_ref), channel_id=1, source_target_pairs={{0,1},{1,0},{2,3},{3,2},{4,5},{5,4},{6,7},{7,6},{8,9},{9,8},{10,11... | collective-permute-start | bytes 61448 | tf_op jit(solution)/shard_map/ppermute | solution.py:522
  74.2 20.7 %all-to-all-start.5 = ((f16[64,4,640]{2,1,0:T(4,128)(2,1)}), f16[64,4,640]{2,1,0:T(4,128)(2,1)S(1)}, u32[]{:S(2)}, u32[]{:S(2)}) async-start(f16[64,4,640]{2,1,0:T(4,128)(2,1)} %broadcast_in_dim.23), calls=%async_computation.5 | async-start | bytes 655360 | tf_op jit(solution)/shard_map/all_to_all | solution.py:513
  80.7 8.9 %collective-permute-start.1 = (f32[40,128]{1,0:T(8,128)S(1)}, f32[40,128]{1,0:T(8,128)S(1)}, u32[]{:S(2)}, u32[]{:S(2)}) collective-permute-start(f32[40,128]{1,0:T(8,128)S(1)} %get-tuple-element.59.sent_ref._send_ref), channel_id=1, source_target_pairs={{0,4},{1,5},{2,6},{3,7},{4,0},{5,1},{6,2},{7,3},{8,12},{9,13},{10,... | collective-permute-start | bytes 61448 | tf_op jit(solution)/shard_map/ppermute | solution.py:522
  89.7 6.2 %collective-permute-start.2 = (f32[48,128]{1,0:T(8,128)S(1)}, f32[48,128]{1,0:T(8,128)S(1)}, u32[]{:S(2)}, u32[]{:S(2)}) collective-permute-start(f32[48,128]{1,0:T(8,128)S(1)} %get-tuple-element.61.sent_ref), channel_id=1, source_target_pairs={{0,2},{1,3},{2,0},{3,1},{4,6},{5,7},{6,4},{7,5},{8,10},{9,11},{10,... | collective-permute-start | bytes 73736 | tf_op jit(solution)/shard_map/ppermute | solution.py:522

commit v7 on v6

--- a/solution.py
+++ b/solution.py
@@ -15,8 +15,9 @@
 HEADS = 2
 D = 2048
 NX, NZ, NC, NY = 4, 8, 2, 8
+NQ, NP = 4, 2
 PARTS = D // NX // C
-CTX = ("x", "z", "core")
+CTX = ("x", "zq", "zp", "core")
 norm_epsilon = 1e-06
 SCALE = C**-0.5
 MAP_ROWS = 3 * C
@@ -79,7 +80,7 @@
 
 
 def local_kernel(
-    at_ref, _x_ref, _y_ref, _z_ref, doc_ref, rate_hbm, bias_hbm, k_hbm, hid_hbm, wd_hbm, wb_hbm, q_hbm, v_hbm, do_hbm,
+    at_ref, _x_ref, _y_ref, _q_ref, _p_ref, doc_ref, rate_hbm, bias_hbm, k_hbm, hid_hbm, wd_hbm, wb_hbm, q_hbm, v_hbm, do_hbm,
     map_ref, uhat_ref, what_ref, z0_ref, y_ref, gram_ref, qk_ref, rows_ref, weights_ref,
     rate_ref, bias_ref, k_ref, hid_ref, wd_ref, wb_ref, q_ref, v_ref, do_ref, sems,
 ):
@@ -213,6 +214,17 @@
     out_ref[0:C, :] = coded(n0 + n1 - forward[:, :C], (state_power, adjoint_power))
 
 
+def duo_kernel(maps_ref, out_ref):
+    n0, l0, a0 = unpack(maps_ref, 0, 2)
+    n1, l1, a1 = unpack(maps_ref, 1, 2)
+    n0s = split(n0)
+    forward = mm(split(n1), tuple(jnp.concatenate([a, b], axis=1) for a, b in zip(n0s, split(l0))))
+    backward = mm(n0s, split(a1), 0, 0)
+    out_ref[C : 2 * C, :], state_power = scaled(l0 + l1 - forward[:, C:])
+    out_ref[2 * C : 3 * C, :], adjoint_power = scaled(a0 + a1 - backward)
+    out_ref[0:C, :] = coded(n0 + n1 - forward[:, :C], (state_power, adjoint_power))
+
+
 def ring_kernel(at_x_ref, at_ref, maps_ref, out_ref, near_ref):
     here = at_ref[0]
     zero = jnp.zeros((C, C), F32)
@@ -222,17 +234,17 @@
         near_ref[0:C, :] = zero
         near_ref[C : 2 * C, :] = zero
 
-    @pl.when(here == NZ - 1)
+    @pl.when(here == NQ - 1)
     def _():
         near_ref[2 * C : 3 * C, :] = zero
         near_ref[3 * C : 4 * C, :] = zero
 
-    maps = [unpack(maps_ref, z, 2) for z in range(NZ)]
+    maps = [unpack(maps_ref, z, 2) for z in range(NQ)]
     n, state, _ = maps[0]
-    n_back, _, adjoint = maps[NZ - 1]
+    n_back, _, adjoint = maps[NQ - 1]
     n_back = n_back.T
-    for step in range(1, NZ):
-        back = NZ - 1 - step
+    for step in range(1, NQ):
+        back = NQ - 1 - step
 
         @pl.when(here == step)
         def _():
@@ -269,7 +281,7 @@
             out_ref[x, C : 2 * C, :] = adjoint
 
 
-def entry_kernel(at_ref, groups_ref, near_ref, maps_ref, out_ref, s_ref, a_ref):
+def entry_kernel(at_ref, at_pair_ref, groups_ref, near_ref, chips_ref, maps_ref, out_ref, s_ref, a_ref):
     here = at_ref[0]
     s_ref[...] = jnp.where(here > 0, unpack(groups_ref, 0, 1)[1], 0.0)
     a_ref[...] = jnp.where(here < NX - 1, unpack(groups_ref, NX - 1, 1)[1], 0.0)
@@ -291,6 +303,12 @@
     s, a = s_ref[...], a_ref[...]
     s = s - mm(split(near_ref[0:C, :]), split(s)) + near_ref[C : 2 * C, :]
     a = a - mm(split(near_ref[2 * C : 3 * C, :]), split(a)) + near_ref[3 * C : 4 * C, :]
+    n, state, _ = unpack(chips_ref, 0, 2)
+    second = s - mm(split(n), split(s)) + state
+    n, _, adjoint = unpack(chips_ref, 1, 2)
+    first = a - mm(split(n), split(a), 0, 0) + adjoint
+    s = jnp.where(at_pair_ref[0] == 0, s, second)
+    a = jnp.where(at_pair_ref[0] == 0, first, a)
     out_ref[0, 0:C, :] = s
     out_ref[1, C : 2 * C, :] = a
     n, state, _ = read_map(maps_ref, 0)
@@ -524,16 +542,17 @@
 
 def on_device(hidden, queries, keys, values, cotangent, w_decay, w_beta, rate, bias, doc_start):
     at_x = lax.axis_index("x").astype(jnp.int32)
-    at_z = lax.axis_index("z").astype(jnp.int32)
+    at_q = lax.axis_index("zq").astype(jnp.int32)
+    at_p = lax.axis_index("zp").astype(jnp.int32)
     at_core = lax.axis_index("core").astype(jnp.int32)
     at_y = lax.axis_index("dp").astype(jnp.int32)
-    first = ((at_x * NZ + at_z) * NC + at_core) * C
-    at_x, at_y, at_z, first = (a[None] for a in (at_x, at_y, at_z, first))
+    first = (((at_x * NQ + at_q) * NP + at_p) * NC + at_core) * C
+    at_x, at_y, at_q, at_p, first = (a[None] for a in (at_x, at_y, at_q, at_p, first))
     wd, wb = w_decay.T, w_beta.T
     square, heads, wide = (C, C), (HEADS, C, C), (C, HEADS * C)
     maps, uhat, what, z0, y, gram, qk, rows, weights = call(
         local_kernel,
-        (first, at_x, at_y, at_z, doc_start),
+        (first, at_x, at_y, at_q, at_p, doc_start),
         (rate, bias, keys, hidden, wd, wb, queries, values, cotangent),
         [((HEADS, MAP_ROWS, C), F32)] + [(heads, F32)] * 4 + [(square, F32)] * 2 + [((16, C), F32), ((NY, 8, C), F32)],
         [
@@ -552,15 +571,17 @@
     )
     maps = exchange(maps, "core")
     (packed,) = call(pair_kernel, (), (maps,), [((MAP_ROWS, C), F32)])
-    ring = spread(packed, NZ, "z")
+    chips = spread(packed, NP, "zp")
+    (packed,) = call(duo_kernel, (), (chips,), [((MAP_ROWS, C), F32)])
+    ring = spread(packed, NQ, "zq")
     groups, near = call(
-        ring_kernel, (at_x, at_z), (ring,), [((NX, 2 * C, C), F32), ((4 * C, C), F32)]
+        ring_kernel, (at_x, at_q), (ring,), [((NX, 2 * C, C), F32), ((4 * C, C), F32)]
     )
     groups = exchange(groups.astype(F16), "x").astype(F32)
     (ends,) = call(
         entry_kernel,
-        (at_x,),
-        (groups, near, maps),
+        (at_x, at_p),
+        (groups, near, chips, maps),
         [((NC, 2 * C, C), F32)],
         [pltpu.VMEM(square, F32), pltpu.VMEM(square, F32)],
     )
@@ -608,7 +629,7 @@
 
 
 def solution(mesh):
-    fine = Mesh(mesh.devices.reshape(NX, NZ, NC, NY), ("x", "z", "core", "dp"))
+    fine = Mesh(mesh.devices.reshape(NX, NQ, NP, NC, NY), (*CTX, "dp"))
     rows, both, cols = P(CTX, None), P(CTX, "dp"), P(None, "dp")
     return jax.shard_map(
         on_device,

time: 97.8 us -> 95.3 us (0.974)
  blocking collectives: 53.6 us -> 50.3 us
  starting transfers between devices: 24.7 us -> 25.9 us
    all_to_all x4 -> x5, blocking collectives: 53.6 us -> 50.3 us  [exchange(): return lax.all_to_all(a, axes, 0, 0, tiled=True)]
    all_to_all x2, starting transfers between devices: 9.8 us -> 11 us  [exchange(): return lax.all_to_all(a, axes, 0, 0, tiled=True)]
    pallas_call x11 -> x12, Pallas kernels: 12.7 us -> 12.2 us  [call(): pl.pallas_call(kernel, out_shape=tuple((jax.ShapeDtypeStruct(s, t) for s,...]
where the time goes in v7:
time: 95.3 us; the launch traced here: 94.3 us
  blocking collectives  50.3 us (53%)
  starting transfers between devices  25.9 us (27%)
  Pallas kernels  12.2 us (13%)
  waiting for transfers between devices  3.08 us (3%)
  between operations  1.52 us (2%)
    all_to_all x5, blocking collectives, exchange(): return lax.all_to_all(a, axes, 0, 0, tiled=True)  50.3 us
    ppermute x3, starting transfers between devices, swap(): return lax.ppermute(a, 'dp', [(i, i ^ bit) for i in range(NY)])  14.9 us
    pallas_call x12, Pallas kernels, call(): pl.pallas_call(kernel, out_shape=tuple((jax.ShapeDtypeStruct(s, t) for s,...  12.2 us
    all_to_all x2, starting transfers between devices, exchange(): return lax.all_to_all(a, axes, 0, 0, tiled=True)  11 us
    ppermute x3, waiting for transfers between devices, swap(): return lax.ppermute(a, 'dp', [(i, i ^ bit) for i in range(NY)])  3.07 us
  transfers between devices with their start and end apart: 5, of which 2 were waited for; matrix products, arithmetic and copies ran while one was open for 0% of the time, Pallas kernels for 2%

profile of v7, /device:TPU:1, one launch (start us, length us, event | category | flops | bytes accessed | tf_op | source)
XLA Modules:
  0.0 94.3 jit_solution(5384735530574951245)
XLA Ops:
  1.3 4.5 %shard_map.161 = (f32[2,384,128]{2,1,0:T(8,128)S(1)}, f32[2,128,128]{2,1,0:T(8,128)S(1)}, f32[2,128,128]{2,1,0:T(8,128)S(1)}, f32[2,128,128]{2,1,0:T(8,128)S(1)}...) custom-call(s32[1]{0:T(128)} %bitcast.4.at_ref, ...), custom_call_target="tpu_custom_call" | custom-call | tf_op jit(solution)/shard_map/pallas_call | solution.py:519
  5.8 10.6 %all_to_all.35.maps_ref = f32[2,384,128]{2,1,0:T(8,128)S(1)} all-to-all(f32[2,384,128]{2,1,0:T(8,128)S(1)} %get-tuple-element.39), channel_id=1, replica_groups=mesh['x'=4,'zq'=4,'zp'=2,'core'=2,'dp'=8] {'core'}, dimensions={0} | all-to-all | bytes 786432 | tf_op jit(solution)/shard_map/all_to_all | solution.py:531
  16.4 0.3 shard_map.162
  16.8 6.6 %all_to_all.36 = f16[2,384,128]{2,1,0:T(8,128)(2,1)S(1)} all-to-all(f16[2,384,128]{2,1,0:T(8,128)(2,1)S(1)} %broadcast_in_dim.29), channel_id=1, replica_groups=mesh['x'=4,'zq'=4,'zp'=2,'core'=2,'dp'=8] {'zp'}, dimensions={0} | all-to-all | bytes 393216 | tf_op jit(solution)/shard_map/all_to_all | solution.py:531
  23.4 0.4 shard_map.163
  23.9 0.1 broadcast_in_dim.30
  23.9 15.6 %all_to_all.37 = f16[4,384,128]{2,1,0:T(8,128)(2,1)S(1)} all-to-all(f16[4,384,128]{2,1,0:T(8,128)(2,1)S(1)} %broadcast_in_dim.30), channel_id=1, replica_groups=mesh['x'=4,'zq'=4,'zp'=2,'core'=2,'dp'=8] {'zq'}, dimensions={0} | all-to-all | bytes 786432 | tf_op jit(solution)/shard_map/all_to_all | solution.py:531
  39.6 0.1 convert_element_type.27.maps_ref
  39.6 1.1 %shard_map.164 = (f32[4,256,128]{2,1,0:T(8,128)S(1)}, f32[512,128]{1,0:T(8,128)S(1)}) custom-call(s32[1]{0:T(128)} %bitcast.1._x_ref.at_x_ref.at_ref, s32[1]{0:T(128)} %bitcast.3._q_ref.at_ref, f32[4,384,128]{2,1,0:T(8,128)S(1)} %convert_element_type.27.maps_ref), custom_call_target="tpu_custom_call" | custom-call | tf_op jit(solution)/shard_map/pallas_call | solution.py:519
  40.8 9.3 %all_to_all.38 = f16[4,256,128]{2,1,0:T(8,128)(2,1)S(1)} all-to-all(f16[4,256,128]{2,1,0:T(8,128)(2,1)S(1)} %convert_element_type.28), channel_id=1, replica_groups=mesh['x'=4,'zq'=4,'zp'=2,'core'=2,'dp'=8] {'x'}, dimensions={0} | all-to-all | bytes 524288 | tf_op jit(solution)/shard_map/all_to_all | solution.py:531
  50.2 0.0 copy-start.1
  50.2 0.0 copy-start.2
  50.2 0.0 copy-start.3
  50.2 1.1 %shard_map.165 = f32[2,256,128]{2,1,0:T(8,128)S(1)} custom-call(s32[1]{0:T(128)} %bitcast.1._x_ref.at_x_ref.at_ref, s32[1]{0:T(128)} %bitcast.2._p_ref.at_pair_ref, f32[4,256,128]{2,1,0:T(8,128)S(1)} %convert_element_type.29.groups_ref, f32[512,128]{1,0:T(8,128)S(1)} %get-tuple-element.41.near_ref, ...), custom_call_target="tpu_custom_call" | custom-call | tf_op jit(solution)/shard_map/pallas_call | solution.py:519
  51.4 0.0 copy-start
  51.4 8.2 %all_to_all.39.ends_ref = f32[2,256,128]{2,1,0:T(8,128)S(1)} all-to-all(f32[2,256,128]{2,1,0:T(8,128)S(1)} %shard_map.165), channel_id=1, replica_groups=mesh['x'=4,'zq'=4,'zp'=2,'core'=2,'dp'=8] {'core'}, dimensions={0} | all-to-all | bytes 524288 | tf_op jit(solution)/shard_map/all_to_all | solution.py:531
  59.6 1.9 %shard_map.166 = (bf16[128,256]{1,0:T(8,128)(2,1)}, f32[128,128]{1,0:T(8,128)S(1)}, f32[128,128]{1,0:T(8,128)S(1)}, f32[128,128]{1,0:T(8,128)S(1)}, f32[128,128]...) custom-call(s32[1]{0:T(128)} %bitcast._y_ref.at_y_ref, ...), custom_call_target="tpu_custom_call" | custom-call | tf_op jit(solution)/shard_map/pallas_call | solution.py:519
  61.4 3.3 %all-to-all-start.5 = ((f32[4,16,128]{2,1,0:T(8,128)}), f32[4,16,128]{2,1,0:T(8,128)S(1)}, u32[]{:S(2)}, u32[]{:S(2)}) async-start(f32[4,16,128]{2,1,0:T(8,128)} %get-tuple-element.63), calls=%async_computation.5 | async-start | bytes 65536 | tf_op jit(solution)/shard_map/all_to_all | solution.py:531
  64.7 3.2 %collective-permute-start = (f32[40,128]{1,0:T(8,128)S(1)}, f32[40,128]{1,0:T(8,128)S(1)}, u32[]{:S(2)}, u32[]{:S(2)}) collective-permute-start(f32[40,128]{1,0:T(8,128)S(1)} %get-tuple-element.57.sent_ref), channel_id=1, source_target_pairs={{0,1},{1,0},{2,3},{3,2},{4,5},{5,4},{6,7},{7,6},{8,9},{9,8},{10,11... | collective-permute-start | bytes 61448 | tf_op jit(solution)/shard_map/ppermute | solution.py:540
  67.9 1.6 %collective-permute-done.got_ref = f32[40,128]{1,0:T(8,128)S(1)} collective-permute-done((f32[40,128]{1,0:T(8,128)S(1)}, f32[40,128]{1,0:T(8,128)S(1)}, u32[]{:S(2)}, u32[]{:S(2)}) %collective-permute-start) | collective-permute-done | bytes 20512 | tf_op jit(solution)/shard_map/ppermute | solution.py:540
  69.5 0.0 all-to-all-done.5.share_ref
  69.5 0.1 shard_map.170
  69.7 0.8 broadcast_in_dim.31
  70.5 7.8 %all-to-all-start.6 = ((f16[64,4,640]{2,1,0:T(4,128)(2,1)}), f16[64,4,640]{2,1,0:T(4,128)(2,1)S(1)}, u32[]{:S(2)}, u32[]{:S(2)}) async-start(f16[64,4,640]{2,1,0:T(4,128)(2,1)} %broadcast_in_dim.31), calls=%async_computation.6 | async-start | bytes 655360 | tf_op jit(solution)/shard_map/all_to_all | solution.py:531
  78.2 7.5 %collective-permute-start.1 = (f32[40,128]{1,0:T(8,128)S(1)}, f32[40,128]{1,0:T(8,128)S(1)}, u32[]{:S(2)}, u32[]{:S(2)}) collective-permute-start(f32[40,128]{1,0:T(8,128)S(1)} %get-tuple-element.59.sent_ref._send_ref), channel_id=1, source_target_pairs={{0,4},{1,5},{2,6},{3,7},{4,0},{5,1},{6,2},{7,3},{8,12},{9,13},{10,... | collective-permute-start | bytes 61448 | tf_op jit(solution)/shard_map/ppermute | solution.py:540
  85.7 1.5 %collective-permute-done.1.got_ref = f32[40,128]{1,0:T(8,128)S(1)} collective-permute-done((f32[40,128]{1,0:T(8,128)S(1)}, f32[40,128]{1,0:T(8,128)S(1)}, u32[]{:S(2)}, u32[]{:S(2)}) %collective-permute-start.1) | collective-permute-done | bytes 20512 | tf_op jit(solution)/shard_map/ppermute | solution.py:540
  87.2 4.2 %collective-permute-start.2 = (f32[48,128]{1,0:T(8,128)S(1)}, f32[48,128]{1,0:T(8,128)S(1)}, u32[]{:S(2)}, u32[]{:S(2)}) collective-permute-start(f32[48,128]{1,0:T(8,128)S(1)} %get-tuple-element.61.sent_ref), channel_id=1, source_target_pairs={{0,2},{1,3},{2,0},{3,1},{4,6},{5,7},{6,4},{7,5},{8,10},{9,11},{10,... | collective-permute-start | bytes 73736 | tf_op jit(solution)/shard_map/ppermute | solution.py:540
  91.4 1.0 %shard_map.167 = (bf16[128,128]{1,0:T(8,128)(2,1)}, bf16[128,128]{1,0:T(8,128)(2,1)}) custom-call(bf16[128,128]{1,0:T(8,128)(2,1)S(1)} %copy-done.2, bf16[128,128]{1,0:T(8,128)(2,1)S(1)} %copy-done.3, f32[128,128]{1,0:T(8,128)S(1)} %get-tuple-element.50.e_ref, f32[128,128]{1,0:T(8,128)S(1)} %get-tuple-element.51.f_ref, ...), custom_call_target="tpu_custom_call" | custom-call | flops 268435456 | bytes 1048576 | tf_op jit(solution)/shard_map/pallas_call | solution.py:519
  92.4 0.0 all-to-all-done.6
  92.4 0.1 convert_element_type.31.parts_ref
  92.6 0.8 shard_map.171
  93.4 0.9 shard_map.172
  (14 shorter events, 0.2 us)
Async XLA Ops:
  50.2 9.3 %copy-start.1 = (bf16[128,256]{1,0:T(8,128)(2,1)S(1)}, bf16[128,256]{1,0:T(8,128)(2,1)}, u32[]{:S(2)}) copy-start(bf16[128,256]{1,0:T(8,128)(2,1)} %do_ref.1) | copy-start | bytes 196612
  50.2 9.3 %copy-start.2 = (bf16[128,128]{1,0:T(8,128)(2,1)S(1)}, bf16[128,128]{1,0:T(8,128)(2,1)}, u32[]{:S(2)}) copy-start(bf16[128,128]{1,0:T(8,128)(2,1)} %k_ref.3) | copy-start | bytes 98308
  50.2 9.3 %copy-start.3 = (bf16[128,128]{1,0:T(8,128)(2,1)S(1)}, bf16[128,128]{1,0:T(8,128)(2,1)}, u32[]{:S(2)}) copy-start(bf16[128,128]{1,0:T(8,128)(2,1)} %q_ref.3) | copy-start | bytes 98308
  51.4 8.2 %copy-start = (bf16[128,2048]{1,0:T(8,128)(2,1)S(1)}, bf16[128,2048]{1,0:T(8,128)(2,1)}, u32[]{:S(2)}) copy-start(bf16[128,2048]{1,0:T(8,128)(2,1)} %hid_ref.1) | copy-start | bytes 1572868
  61.4 8.1 %all-to-all-start.5 = ((f32[4,16,128]{2,1,0:T(8,128)}), f32[4,16,128]{2,1,0:T(8,128)S(1)}, u32[]{:S(2)}, u32[]{:S(2)}) async-start(f32[4,16,128]{2,1,0:T(8,128)} %get-tuple-element.63), calls=%async_computation.5 | async-start | bytes 65536 | tf_op jit(solution)/shard_map/all_to_all | solution.py:531
  64.7 4.8 %collective-permute-start = (f32[40,128]{1,0:T(8,128)S(1)}, f32[40,128]{1,0:T(8,128)S(1)}, u32[]{:S(2)}, u32[]{:S(2)}) collective-permute-start(f32[40,128]{1,0:T(8,128)S(1)} %get-tuple-element.57.sent_ref), channel_id=1, source_target_pairs={{0,1},{1,0},{2,3},{3,2},{4,5},{5,4},{6,7},{7,6},{8,9},{9,8},{10,11... | collective-permute-start | bytes 61448 | tf_op jit(solution)/shard_map/ppermute | solution.py:540
  70.5 22.0 %all-to-all-start.6 = ((f16[64,4,640]{2,1,0:T(4,128)(2,1)}), f16[64,4,640]{2,1,0:T(4,128)(2,1)S(1)}, u32[]{:S(2)}, u32[]{:S(2)}) async-start(f16[64,4,640]{2,1,0:T(4,128)(2,1)} %broadcast_in_dim.31), calls=%async_computation.6 | async-start | bytes 655360 | tf_op jit(solution)/shard_map/all_to_all | solution.py:531
  78.2 8.9 %collective-permute-start.1 = (f32[40,128]{1,0:T(8,128)S(1)}, f32[40,128]{1,0:T(8,128)S(1)}, u32[]{:S(2)}, u32[]{:S(2)}) collective-permute-start(f32[40,128]{1,0:T(8,128)S(1)} %get-tuple-element.59.sent_ref._send_ref), channel_id=1, source_target_pairs={{0,4},{1,5},{2,6},{3,7},{4,0},{5,1},{6,2},{7,3},{8,12},{9,13},{10,... | collective-permute-start | bytes 61448 | tf_op jit(solution)/shard_map/ppermute | solution.py:540
  87.2 6.2 %collective-permute-start.2 = (f32[48,128]{1,0:T(8,128)S(1)}, f32[48,128]{1,0:T(8,128)S(1)}, u32[]{:S(2)}, u32[]{:S(2)}) collective-permute-start(f32[48,128]{1,0:T(8,128)S(1)} %get-tuple-element.61.sent_ref), channel_id=1, source_target_pairs={{0,2},{1,3},{2,0},{3,1},{4,6},{5,7},{6,4},{7,5},{8,10},{9,11},{10,... | collective-permute-start | bytes 73736 | tf_op jit(solution)/shard_map/ppermute | solution.py:540

commit v8 on v7

--- a/solution.py
+++ b/solution.py
@@ -16,7 +16,7 @@
 D = 2048
 NX, NZ, NC, NY = 4, 8, 2, 8
 NQ, NP = 4, 2
-PARTS = D // NX // C
+PARTS = D // (NX * NC) // C
 CTX = ("x", "zq", "zp", "core")
 norm_epsilon = 1e-06
 SCALE = C**-0.5
@@ -387,7 +387,7 @@
     terms_ref[12:16, :] = jnp.zeros((4, C), F32)
     grad = dot(terms_ref[...].astype(BF16), hid_ref[...], 1, 0)
     grad = grad[0:4, :] + grad[4:8, :] + grad[8:12, :]
-    for x in range(NX):
+    for x in range(NX * NC):
         for i in range(PARTS):
             at = slice((PARTS * x + i) * C, (PARTS * x + i + 1) * C)
             share_ref[x, 4 * i : 4 * i + 4, :] = grad[:, at]
@@ -401,7 +401,7 @@
 
 
 def second_kernel(at_y_ref, got_ref, sent_ref, keep_ref, send_ref, kept_ref):
-    bit = (at_y_ref[0] >> 2) & 1
+    bit = (at_y_ref[0] >> 1) & 1
     send_ref[0:4, :] = sent_ref[0:4, :]
     send_ref[4:8, :] = got_ref[0:4, :]
     for high in range(2):
@@ -410,31 +410,31 @@
             pair = (keep_ref[place], got_ref[8 + 8 * place : 16 + 8 * place, :])
             for source, rows in enumerate(pair):
 
-                at = 2 * source + low
-
-                @pl.when(bit == high)
+                at = 2 * source + high
+
+                @pl.when(bit == low)
                 def _():
                     kept_ref[at] = rows
 
-                @pl.when(bit != high)
+                @pl.when(bit != low)
                 def _():
                     send_ref[8 + 8 * at : 16 + 8 * at, :] = rows
 
 
 def third_kernel(at_y_ref, got_ref, sent_ref, keep_ref, send_ref, kept_ref):
-    bit = (at_y_ref[0] >> 1) & 1
+    bit = (at_y_ref[0] >> 2) & 1
     send_ref[0:8, :] = sent_ref[0:8, :]
     send_ref[8:16, :] = got_ref[0:8, :]
     for source in range(4):
-        for low in range(2):
-            at = 2 * (source % 2) + low
+        for high in range(2):
+            at = 2 * (source % 2) + high
             rows = keep_ref[at] if source < 2 else got_ref[8 + 8 * at : 16 + 8 * at, :]
 
-            @pl.when(bit == low)
+            @pl.when(bit == high)
             def _():
                 kept_ref[source] = rows
 
-            @pl.when(bit != low)
+            @pl.when(bit != high)
             def _():
                 send_ref[16 + 8 * source : 24 + 8 * source, :] = rows
 
@@ -469,7 +469,7 @@
 
 def sum_kernel(share_ref, own_ref, _send_ref, out_ref):
     total = share_ref[0]
-    for x in range(1, NX):
+    for x in range(1, NX * NC):
         total = total + share_ref[x]
     total, power = scaled(total)
     lane = lax.broadcasted_iota(jnp.int32, (1, C), 1) >> 5
@@ -489,11 +489,11 @@
 
 def finish_kernel(parts_ref, wd_ref, wb_ref, after_ref, rate_ref, bias_ref):
     after_ref[...] = jnp.zeros_like(after_ref)
-    per = NZ * NC
     sums = jnp.zeros((1, C), F32)
-    for x in range(NX):
+    for x in range(NX * NC):
         totals = [jnp.zeros((4, C), F32)] * PARTS
-        for at in range(x * per, (x + 1) * per):
+        for z in range(NZ):
+            at = (x // NC * NZ + z) * NC + x % NC
             meta = parts_ref[at, :, PARTS * C :]
             scale = jnp.exp2(meta[0:1, :] - 13.0)
             totals = [t + parts_ref[at, :, i * C : (i + 1) * C] * scale for i, t in enumerate(totals)]
@@ -592,13 +592,13 @@
         (ends, hidden, keys, queries, cotangent, weights, uhat, what, z0, y, gram, qk, rows),
         [(wide, BF16)]
         + [(square, F32)] * 4
-        + [((NX, 4 * PARTS, C), F32), ((8, C), F32), ((40, C), F32), ((4, 8, C), F32)],
+        + [((NX * NC, 4 * PARTS, C), F32), ((8, C), F32), ((40, C), F32), ((4, 8, C), F32)],
         [pltpu.VMEM((8, C), F32), pltpu.VMEM((16, C), F32)],
     )
     got = swap(send, 1)
-    share = exchange(share, "x")
+    share = exchange(share, ("x", "core"))
     send, keep = call(second_kernel, (at_y,), (got, send, keep), [((40, C), F32), ((4, 8, C), F32)])
-    got = swap(send, 4)
+    got = swap(send, 2)
     (sums,) = call(sum_kernel, (), (share, own, send), [((4, (PARTS + 1) * C), F32)])
     parts = spread(sums, NX * NZ * NC, CTX)
     dq, dk = call(
@@ -609,7 +609,7 @@
         flops=1 << 28,
     )
     send, keep = call(third_kernel, (at_y,), (got, send, keep), [((48, C), F32), ((4, 8, C), F32)])
-    got = swap(send, 2)
+    got = swap(send, 4)
     wd_grad, wb_grad, after, rate_grad, bias_grad = call(
         finish_kernel,
         (),

time: 95.3 us -> 95.5 us (level)
  no operation moved by 1% of the time
where the time goes in v8:
time: 95.5 us; the launch traced here: 94.4 us
  blocking collectives  50.3 us (53%)
  starting transfers between devices  26.2 us (27%)
  Pallas kernels  12.2 us (13%)
  waiting for transfers between devices  3.12 us (3%)
  between operations  1.5 us (2%)
    all_to_all x5, blocking collectives, exchange(): return lax.all_to_all(a, axes, 0, 0, tiled=True)  50.3 us
    ppermute x3, starting transfers between devices, swap(): return lax.ppermute(a, 'dp', [(i, i ^ bit) for i in range(NY)])  15.1 us
    pallas_call x12, Pallas kernels, call(): pl.pallas_call(kernel, out_shape=tuple((jax.ShapeDtypeStruct(s, t) for s,...  12.2 us
    all_to_all x2, starting transfers between devices, exchange(): return lax.all_to_all(a, axes, 0, 0, tiled=True)  11.1 us
    ppermute x3, waiting for transfers between devices, swap(): return lax.ppermute(a, 'dp', [(i, i ^ bit) for i in range(NY)])  3.11 us
  transfers between devices with their start and end apart: 5, of which 2 were waited for; matrix products, arithmetic and copies ran while one was open for 0% of the time, Pallas kernels for 2%

profile of v8, /device:TPU:1, one launch (start us, length us, event | category | flops | bytes accessed | tf_op | source)
XLA Modules:
  0.0 94.4 jit_solution(5024137414448263151)
XLA Ops:
  1.3 4.5 %shard_map.161 = (f32[2,384,128]{2,1,0:T(8,128)S(1)}, f32[2,128,128]{2,1,0:T(8,128)S(1)}, f32[2,128,128]{2,1,0:T(8,128)S(1)}, f32[2,128,128]{2,1,0:T(8,128)S(1)}...) custom-call(s32[1]{0:T(128)} %bitcast.4.at_ref, ...), custom_call_target="tpu_custom_call" | custom-call | tf_op jit(solution)/shard_map/pallas_call | solution.py:519
  5.8 10.6 %all_to_all.35.maps_ref = f32[2,384,128]{2,1,0:T(8,128)S(1)} all-to-all(f32[2,384,128]{2,1,0:T(8,128)S(1)} %get-tuple-element.39), channel_id=1, replica_groups=mesh['x'=4,'zq'=4,'zp'=2,'core'=2,'dp'=8] {'core'}, dimensions={0} | all-to-all | bytes 786432 | tf_op jit(solution)/shard_map/all_to_all | solution.py:531
  16.4 0.3 shard_map.162
  16.8 6.6 %all_to_all.36 = f16[2,384,128]{2,1,0:T(8,128)(2,1)S(1)} all-to-all(f16[2,384,128]{2,1,0:T(8,128)(2,1)S(1)} %broadcast_in_dim.29), channel_id=1, replica_groups=mesh['x'=4,'zq'=4,'zp'=2,'core'=2,'dp'=8] {'zp'}, dimensions={0} | all-to-all | bytes 393216 | tf_op jit(solution)/shard_map/all_to_all | solution.py:531
  23.4 0.4 shard_map.163
  23.9 0.1 broadcast_in_dim.30
  23.9 15.6 %all_to_all.37 = f16[4,384,128]{2,1,0:T(8,128)(2,1)S(1)} all-to-all(f16[4,384,128]{2,1,0:T(8,128)(2,1)S(1)} %broadcast_in_dim.30), channel_id=1, replica_groups=mesh['x'=4,'zq'=4,'zp'=2,'core'=2,'dp'=8] {'zq'}, dimensions={0} | all-to-all | bytes 786432 | tf_op jit(solution)/shard_map/all_to_all | solution.py:531
  39.6 0.1 convert_element_type.27.maps_ref
  39.6 1.1 %shard_map.164 = (f32[4,256,128]{2,1,0:T(8,128)S(1)}, f32[512,128]{1,0:T(8,128)S(1)}) custom-call(s32[1]{0:T(128)} %bitcast.1._x_ref.at_x_ref.at_ref, s32[1]{0:T(128)} %bitcast.3._q_ref.at_ref, f32[4,384,128]{2,1,0:T(8,128)S(1)} %convert_element_type.27.maps_ref), custom_call_target="tpu_custom_call" | custom-call | tf_op jit(solution)/shard_map/pallas_call | solution.py:519
  40.8 9.3 %all_to_all.38 = f16[4,256,128]{2,1,0:T(8,128)(2,1)S(1)} all-to-all(f16[4,256,128]{2,1,0:T(8,128)(2,1)S(1)} %convert_element_type.28), channel_id=1, replica_groups=mesh['x'=4,'zq'=4,'zp'=2,'core'=2,'dp'=8] {'x'}, dimensions={0} | all-to-all | bytes 524288 | tf_op jit(solution)/shard_map/all_to_all | solution.py:531
  50.2 0.0 copy-start.1
  50.2 0.0 copy-start.2
  50.2 0.0 copy-start.3
  50.2 1.1 %shard_map.165 = f32[2,256,128]{2,1,0:T(8,128)S(1)} custom-call(s32[1]{0:T(128)} %bitcast.1._x_ref.at_x_ref.at_ref, s32[1]{0:T(128)} %bitcast.2._p_ref.at_pair_ref, f32[4,256,128]{2,1,0:T(8,128)S(1)} %convert_element_type.29.groups_ref, f32[512,128]{1,0:T(8,128)S(1)} %get-tuple-element.41.near_ref, ...), custom_call_target="tpu_custom_call" | custom-call | tf_op jit(solution)/shard_map/pallas_call | solution.py:519
  51.4 0.0 copy-start
  51.4 8.2 %all_to_all.39.ends_ref = f32[2,256,128]{2,1,0:T(8,128)S(1)} all-to-all(f32[2,256,128]{2,1,0:T(8,128)S(1)} %shard_map.165), channel_id=1, replica_groups=mesh['x'=4,'zq'=4,'zp'=2,'core'=2,'dp'=8] {'core'}, dimensions={0} | all-to-all | bytes 524288 | tf_op jit(solution)/shard_map/all_to_all | solution.py:531
  59.6 1.9 %shard_map.166 = (bf16[128,256]{1,0:T(8,128)(2,1)}, f32[128,128]{1,0:T(8,128)S(1)}, f32[128,128]{1,0:T(8,128)S(1)}, f32[128,128]{1,0:T(8,128)S(1)}, f32[128,128]...) custom-call(s32[1]{0:T(128)} %bitcast._y_ref.at_y_ref, ...), custom_call_target="tpu_custom_call" | custom-call | tf_op jit(solution)/shard_map/pallas_call | solution.py:519
  61.4 3.6 %all-to-all-start.5 = ((f32[8,8,128]{2,1,0:T(8,128)}), f32[8,8,128]{2,1,0:T(8,128)S(1)}, u32[]{:S(2)}, u32[]{:S(2)}) async-start(f32[8,8,128]{2,1,0:T(8,128)} %get-tuple-element.63), calls=%async_computation.5 | async-start | bytes 65536 | tf_op jit(solution)/shard_map/all_to_all | solution.py:531
  65.0 3.2 %collective-permute-start = (f32[40,128]{1,0:T(8,128)S(1)}, f32[40,128]{1,0:T(8,128)S(1)}, u32[]{:S(2)}, u32[]{:S(2)}) collective-permute-start(f32[40,128]{1,0:T(8,128)S(1)} %get-tuple-element.57.sent_ref), channel_id=1, source_target_pairs={{0,1},{1,0},{2,3},{3,2},{4,5},{5,4},{6,7},{7,6},{8,9},{9,8},{10,11... | collective-permute-start | bytes 61448 | tf_op jit(solution)/shard_map/ppermute | solution.py:540
  68.2 1.6 %collective-permute-done.got_ref = f32[40,128]{1,0:T(8,128)S(1)} collective-permute-done((f32[40,128]{1,0:T(8,128)S(1)}, f32[40,128]{1,0:T(8,128)S(1)}, u32[]{:S(2)}, u32[]{:S(2)}) %collective-permute-start) | collective-permute-done | bytes 20512 | tf_op jit(solution)/shard_map/ppermute | solution.py:540
  69.9 0.1 shard_map.170
  70.0 0.7 broadcast_in_dim.31
  70.7 7.5 %all-to-all-start.6 = ((f16[64,4,384]{2,1,0:T(4,128)(2,1)}), f16[64,4,384]{2,1,0:T(4,128)(2,1)S(1)}, u32[]{:S(2)}, u32[]{:S(2)}) async-start(f16[64,4,384]{2,1,0:T(4,128)(2,1)} %broadcast_in_dim.31), calls=%async_computation.6 | async-start | bytes 393216 | tf_op jit(solution)/shard_map/all_to_all | solution.py:531
  78.2 4.2 %collective-permute-start.1 = (f32[40,128]{1,0:T(8,128)S(1)}, f32[40,128]{1,0:T(8,128)S(1)}, u32[]{:S(2)}, u32[]{:S(2)}) collective-permute-start(f32[40,128]{1,0:T(8,128)S(1)} %get-tuple-element.59.sent_ref._send_ref), channel_id=1, source_target_pairs={{0,2},{1,3},{2,0},{3,1},{4,6},{5,7},{6,4},{7,5},{8,10},{9,11},{10,... | collective-permute-start | bytes 61448 | tf_op jit(solution)/shard_map/ppermute | solution.py:540
  82.4 1.5 %collective-permute-done.1.got_ref = f32[40,128]{1,0:T(8,128)S(1)} collective-permute-done((f32[40,128]{1,0:T(8,128)S(1)}, f32[40,128]{1,0:T(8,128)S(1)}, u32[]{:S(2)}, u32[]{:S(2)}) %collective-permute-start.1) | collective-permute-done | bytes 20512 | tf_op jit(solution)/shard_map/ppermute | solution.py:540
  83.9 7.7 %collective-permute-start.2 = (f32[48,128]{1,0:T(8,128)S(1)}, f32[48,128]{1,0:T(8,128)S(1)}, u32[]{:S(2)}, u32[]{:S(2)}) collective-permute-start(f32[48,128]{1,0:T(8,128)S(1)} %get-tuple-element.61.sent_ref), channel_id=1, source_target_pairs={{0,4},{1,5},{2,6},{3,7},{4,0},{5,1},{6,2},{7,3},{8,12},{9,13},{10,... | collective-permute-start | bytes 73736 | tf_op jit(solution)/shard_map/ppermute | solution.py:540
  91.6 1.0 %shard_map.167 = (bf16[128,128]{1,0:T(8,128)(2,1)}, bf16[128,128]{1,0:T(8,128)(2,1)}) custom-call(bf16[128,128]{1,0:T(8,128)(2,1)S(1)} %copy-done.2, bf16[128,128]{1,0:T(8,128)(2,1)S(1)} %copy-done.3, f32[128,128]{1,0:T(8,128)S(1)} %get-tuple-element.50.e_ref, f32[128,128]{1,0:T(8,128)S(1)} %get-tuple-element.51.f_ref, ...), custom_call_target="tpu_custom_call" | custom-call | flops 268435456 | bytes 1048576 | tf_op jit(solution)/shard_map/pallas_call | solution.py:519
  92.7 0.0 all-to-all-done.6
  92.7 0.1 convert_element_type.31.parts_ref
  92.7 0.8 shard_map.171
  93.5 0.0 collective-permute-done.2.got_ref
  93.5 0.9 shard_map.172
  (14 shorter events, 0.2 us)
Async XLA Ops:
  50.2 9.3 %copy-start.1 = (bf16[128,256]{1,0:T(8,128)(2,1)S(1)}, bf16[128,256]{1,0:T(8,128)(2,1)}, u32[]{:S(2)}) copy-start(bf16[128,256]{1,0:T(8,128)(2,1)} %do_ref.1) | copy-start | bytes 196612
  50.2 9.3 %copy-start.2 = (bf16[128,128]{1,0:T(8,128)(2,1)S(1)}, bf16[128,128]{1,0:T(8,128)(2,1)}, u32[]{:S(2)}) copy-start(bf16[128,128]{1,0:T(8,128)(2,1)} %k_ref.3) | copy-start | bytes 98308
  50.2 9.3 %copy-start.3 = (bf16[128,128]{1,0:T(8,128)(2,1)S(1)}, bf16[128,128]{1,0:T(8,128)(2,1)}, u32[]{:S(2)}) copy-start(bf16[128,128]{1,0:T(8,128)(2,1)} %q_ref.3) | copy-start | bytes 98308
  51.4 8.2 %copy-start = (bf16[128,2048]{1,0:T(8,128)(2,1)S(1)}, bf16[128,2048]{1,0:T(8,128)(2,1)}, u32[]{:S(2)}) copy-start(bf16[128,2048]{1,0:T(8,128)(2,1)} %hid_ref.1) | copy-start | bytes 1572868
  61.4 8.4 %all-to-all-start.5 = ((f32[8,8,128]{2,1,0:T(8,128)}), f32[8,8,128]{2,1,0:T(8,128)S(1)}, u32[]{:S(2)}, u32[]{:S(2)}) async-start(f32[8,8,128]{2,1,0:T(8,128)} %get-tuple-element.63), calls=%async_computation.5 | async-start | bytes 65536 | tf_op jit(solution)/shard_map/all_to_all | solution.py:531
  65.0 4.8 %collective-permute-start = (f32[40,128]{1,0:T(8,128)S(1)}, f32[40,128]{1,0:T(8,128)S(1)}, u32[]{:S(2)}, u32[]{:S(2)}) collective-permute-start(f32[40,128]{1,0:T(8,128)S(1)} %get-tuple-element.57.sent_ref), channel_id=1, source_target_pairs={{0,1},{1,0},{2,3},{3,2},{4,5},{5,4},{6,7},{7,6},{8,9},{9,8},{10,11... | collective-permute-start | bytes 61448 | tf_op jit(solution)/shard_map/ppermute | solution.py:540
  70.7 21.9 %all-to-all-start.6 = ((f16[64,4,384]{2,1,0:T(4,128)(2,1)}), f16[64,4,384]{2,1,0:T(4,128)(2,1)S(1)}, u32[]{:S(2)}, u32[]{:S(2)}) async-start(f16[64,4,384]{2,1,0:T(4,128)(2,1)} %broadcast_in_dim.31), calls=%async_computation.6 | async-start | bytes 393216 | tf_op jit(solution)/shard_map/all_to_all | solution.py:531
  78.2 5.7 %collective-permute-start.1 = (f32[40,128]{1,0:T(8,128)S(1)}, f32[40,128]{1,0:T(8,128)S(1)}, u32[]{:S(2)}, u32[]{:S(2)}) collective-permute-start(f32[40,128]{1,0:T(8,128)S(1)} %get-tuple-element.59.sent_ref._send_ref), channel_id=1, source_target_pairs={{0,2},{1,3},{2,0},{3,1},{4,6},{5,7},{6,4},{7,5},{8,10},{9,11},{10,... | collective-permute-start | bytes 61448 | tf_op jit(solution)/shard_map/ppermute | solution.py:540
  83.9 9.6 %collective-permute-start.2 = (f32[48,128]{1,0:T(8,128)S(1)}, f32[48,128]{1,0:T(8,128)S(1)}, u32[]{:S(2)}, u32[]{:S(2)}) collective-permute-start(f32[48,128]{1,0:T(8,128)S(1)} %get-tuple-element.61.sent_ref), channel_id=1, source_target_pairs={{0,4},{1,5},{2,6},{3,7},{4,0},{5,1},{6,2},{7,3},{8,12},{9,13},{10,... | collective-permute-start | bytes 73736 | tf_op jit(solution)/shard_map/ppermute | solution.py:540
